TPU v7x, 512 devices: a whole 4x4x16 slice. The times are simulated.
512 devices in a mesh: dp: 128 (over z, y_lo, x), pair: 4 (over y_hi, core).
Axes of the slice: x: 4, y: 4 (y_hi: 2, y_lo: 2; y = y_hi * 2 + y_lo), z: 16, core: 2. Of those that a mesh axis runs over, the one named last changes fastest.
Arguments:
- images: bfloat16 [229376, 1152], P(('dp', 'pair')), may hold values from -0.59765625 to 0.59765625
- texts: bfloat16 [229376, 1152], P(('dp', 'pair')), may hold values from -0.59765625 to 0.59765625
- labels: int32 [229376], P(('dp', 'pair')), may hold values from 0 to 229375, as said below
- log_scale: float32 [1], replicated, may hold values from 1.8 to 2.6
- bias: float32 [1], replicated, may hold values from -8 to -4
Outputs:
- image_grad: bfloat16 [229376, 1152], P(('dp', 'pair'))
- text_grad: bfloat16 [229376, 1152], P(('dp', 'pair'))
Inputs may be any that keep to these rules, and one draw needn't show every extreme that they name: `labels`: each image's matching text lies in its own block (row // 448) or in block (row // 448) xor m for one of m = 1, 4, 8, 256; each image has exactly one match.
All inputs are finite; a program needn't handle non-finite values.
Results may differ from a plain program's by a relative error of at most 0.0039.
Values may be sent and summed in bfloat16 or wider, within the bound.
No kernel may reach another device: no remote copies, remote signals or barrier semaphores. Data moves between devices by JAX's collectives and lax.ppermute only.
A program may use at most 64 MiB of HBM per device.

v0:
```python
import jax
import jax.numpy as jnp
from jax import lax
from jax.sharding import PartitionSpec as P


def from_partner(block, axis, bit):
    count = lax.axis_size(axis)
    route = []
    for low in range(count):
        high = low | 1 << bit
        if high != low and high < count:
            route += [(low, high), (high, low)]
    return lax.ppermute(block, axis, route)


def coeff_tile(rows, cols, row_labels, col_start, scale, shift):
    logits = (
        scale
        * lax.dot_general(rows, cols, (((1,), (1,)), ((), ())), preferred_element_type=jnp.float32)
        + shift
    )
    count = cols.shape[0]
    target = (
        row_labels[:, None] == col_start + jnp.arange(count, dtype=jnp.int32)[None, :]
    ).astype(jnp.float32)
    return (jax.nn.sigmoid(logits) - target).astype(jnp.bfloat16)


def left_product(coeff, data):
    return jnp.dot(coeff, data, preferred_element_type=jnp.float32)


def right_product(coeff, data):
    return lax.dot_general(
        coeff, data, (((0,), (0,)), ((), ())), preferred_element_type=jnp.float32
    )


def local(images, texts, labels, log_scale, bias):
    count = images.shape[0]
    scale = jnp.exp(log_scale[0])
    shift = bias[0]
    pair_size = lax.axis_size("pair")
    dp_bits = lax.axis_size("dp").bit_length() - 1
    myself = lax.axis_index("dp") * pair_size + lax.axis_index("pair")
    own = coeff_tile(images, texts, labels, myself * count, scale, shift)
    img_acc = left_product(own, texts)
    txt_acc = right_product(own, images)
    far_list = [0, 1, dp_bits - 1]
    their_txt = from_partner(texts, "pair", 0)
    partner = jnp.bitwise_xor(myself, 1)
    coeff = coeff_tile(images, their_txt, labels, partner * count, scale, shift)
    img_acc = img_acc + left_product(coeff, their_txt)
    txt_acc = txt_acc + from_partner(right_product(coeff, images), "pair", 0)
    for bit in far_list:
        their_txt = from_partner(texts, "dp", bit)
        partner = jnp.bitwise_xor(myself, pair_size << bit)
        coeff = coeff_tile(images, their_txt, labels, partner * count, scale, shift)
        img_acc = img_acc + left_product(coeff, their_txt)
        txt_acc = txt_acc + from_partner(right_product(coeff, images), "dp", bit)
    return ((scale * img_acc).astype(jnp.bfloat16), (scale * txt_acc).astype(jnp.bfloat16))


def solution(mesh):
    placed = (P(("dp", "pair"), None), P(("dp", "pair"), None), P(("dp", "pair")), P(), P())
    return jax.shard_map(
        local,
        mesh=mesh,
        in_specs=placed,
        out_specs=(P(("dp", "pair"), None), P(("dp", "pair"), None)),
        check_vma=False,
    )
```

profile of v0, /device:TPU:49, one launch (start us, length us, event | category | flops | bytes accessed | tf_op | source)
XLA Modules:
  0.0 293.9 jit_solution(13631051033859302585)
XLA Ops:
  0.6 0.0 copy-start
  0.6 14.7 %collective-permute-start.3 = (bf16[448,1152]{1,0:T(8,128)(2,1)}, bf16[448,1152]{1,0:T(8,128)(2,1)S(1)}, u32[]{:S(2)}, u32[]{:S(2)}) collective-permute-start(bf16[448,1152]{1,0:T(8,128)(2,1)} %param.6), channel_id=1, source_target_pairs={{0,256},{256,0},{4,260},{260,4},{8,264},{264,8},{12,268},{268,12},... | collective-permute-start | bytes 3096584 | tf_op jit(solution)/shard_map/ppermute | solution.py:14
  15.3 4.7 %collective-permute-start.2 = (bf16[448,1152]{1,0:T(8,128)(2,1)}, bf16[448,1152]{1,0:T(8,128)(2,1)S(1)}, u32[]{:S(2)}, u32[]{:S(2)}) collective-permute-start(bf16[448,1152]{1,0:T(8,128)(2,1)} %param.6), channel_id=1, source_target_pairs={{0,8},{8,0},{4,12},{12,4},{16,24},{24,16},{20,28},{28,20},{32,40},... | collective-permute-start | bytes 3096584 | tf_op jit(solution)/shard_map/ppermute | solution.py:14
  20.0 3.1 %collective-permute-start = (bf16[448,1152]{1,0:T(8,128)(2,1)}, bf16[448,1152]{1,0:T(8,128)(2,1)}, u32[]{:S(2)}, u32[]{:S(2)}) collective-permute-start(bf16[448,1152]{1,0:T(8,128)(2,1)} %param.6), channel_id=1, source_target_pairs={{0,1},{1,0},{2,3},{3,2},{4,5},{5,4},{6,7},{7,6},{8,9},{9,8},{10,11... | collective-permute-start | bytes 3096584 | tf_op jit(solution)/shard_map/ppermute | solution.py:14
  23.1 2.2 collective-permute-start.1
  26.8 78.0 %collective-permute-done.3 = bf16[448,1152]{1,0:T(8,128)(2,1)S(1)} collective-permute-done((bf16[448,1152]{1,0:T(8,128)(2,1)}, bf16[448,1152]{1,0:T(8,128)(2,1)S(1)}, u32[]{:S(2)}, u32[]{:S(2)}) %collective-permute-start.3) | collective-permute-done | bytes 1032224 | tf_op jit(solution)/shard_map/ppermute | solution.py:14
  104.8 0.0 copy-done
  104.8 1.6 fusion.39
  106.5 0.0 copy-start.2
  106.5 0.8 fusion.50
  107.3 11.5 %collective-permute-start.7 = (f32[448,1152]{1,0:T(8,128)S(1)}, f32[448,1152]{1,0:T(8,128)S(1)}, u32[]{:S(2)}, u32[]{:S(2)}) collective-permute-start(f32[448,1152]{1,0:T(8,128)S(1)} %fusion.50), channel_id=1, source_target_pairs={{0,256},{256,0},{4,260},{260,4},{8,264},{264,8},{12,268},{268,12},... | collective-permute-start | bytes 6193160 | tf_op jit(solution)/shard_map/ppermute | solution.py:14
  118.8 0.0 collective-permute-done.2
  118.8 0.0 copy-done.2
  118.8 0.9 fusion.40
  119.8 0.8 fusion.49
  120.5 4.7 %collective-permute-start.6 = (f32[448,1152]{1,0:T(8,128)S(1)}, f32[448,1152]{1,0:T(8,128)S(1)}, u32[]{:S(2)}, u32[]{:S(2)}) collective-permute-start(f32[448,1152]{1,0:T(8,128)S(1)} %fusion.49), channel_id=1, source_target_pairs={{0,8},{8,0},{4,12},{12,4},{16,24},{24,16},{20,28},{28,20},{32,40},... | collective-permute-start | bytes 6193160 | tf_op jit(solution)/shard_map/ppermute | solution.py:14
  125.2 0.0 collective-permute-done.1
  125.2 2.1 fusion.41
  127.4 0.8 fusion.48
  128.2 2.2 collective-permute-start.5
  130.4 0.0 collective-permute-done
  130.4 2.2 fusion.42
  132.6 0.0 copy-start.1
  132.6 0.8 fusion.47
  133.4 4.4 %collective-permute-start.4 = (f32[448,1152]{1,0:T(8,128)S(1)}, f32[448,1152]{1,0:T(8,128)S(1)}, u32[]{:S(2)}, u32[]{:S(2)}) collective-permute-start(f32[448,1152]{1,0:T(8,128)S(1)} %fusion.47), channel_id=1, source_target_pairs={{0,1},{1,0},{2,3},{3,2},{4,5},{5,4},{6,7},{7,6},{8,9},{9,8},{10,11... | collective-permute-start | bytes 6193160 | tf_op jit(solution)/shard_map/ppermute | solution.py:14
  137.8 0.0 copy-done.1
  137.8 0.9 fusion.43
  138.7 0.8 fusion.44
  139.5 0.8 fusion.46
  140.3 0.8 fusion.45
  141.0 2.0 convolution_add_fusion.2
  143.0 3.0 %fusion.8 = bf16[448,1152]{1,0:T(8,128)(2,1)} fusion(f32[448,1152]{1,0:T(8,128)S(1)} %fusion.46, f32[448,1152]{1,0:T(8,128)S(1)} %fusion.45, f32[448,1152]{1,0:T(8,128)S(1)} %convolution_add_fusion.2, bf16[448,448]{1,0:T(8,128)(2,1)S(1)} %fusion.41, bf16[448,1152]{1,0:T(8,128)(2,1)} %collective-permute-done.1, f32[]{:T(128)} %bitcast), kind=kOutput, calls=%fused_computation.11 | convolution fusion | flops 465002496 | bytes 8658948 | tf_op jit(solution)/shard_map/dot_general | solution.py:31
  146.0 145.9 %collective-permute-done.7 = f32[448,1152]{1,0:T(8,128)S(1)} collective-permute-done((f32[448,1152]{1,0:T(8,128)S(1)}, f32[448,1152]{1,0:T(8,128)S(1)}, u32[]{:S(2)}, u32[]{:S(2)}) %collective-permute-start.7) | collective-permute-done | bytes 2064416 | tf_op jit(solution)/shard_map/ppermute | solution.py:14
  291.9 0.0 collective-permute-done.6
  291.9 0.0 collective-permute-done.5
  291.9 0.0 collective-permute-done.4
  291.9 2.0 fusion.7
  (5 shorter events, 0.0 us)
Async XLA Ops:
  0.6 104.2 %copy-start = (bf16[448,1152]{1,0:T(8,128)(2,1)S(1)}, bf16[448,1152]{1,0:T(8,128)(2,1)}, u32[]{:S(2)}) copy-start(bf16[448,1152]{1,0:T(8,128)(2,1)} %param.5) | copy-start | bytes 3096580
  0.6 104.2 %collective-permute-start.3 = (bf16[448,1152]{1,0:T(8,128)(2,1)}, bf16[448,1152]{1,0:T(8,128)(2,1)S(1)}, u32[]{:S(2)}, u32[]{:S(2)}) collective-permute-start(bf16[448,1152]{1,0:T(8,128)(2,1)} %param.6), channel_id=1, source_target_pairs={{0,256},{256,0},{4,260},{260,4},{8,264},{264,8},{12,268},{268,12},... | collective-permute-start | bytes 3096584 | tf_op jit(solution)/shard_map/ppermute | solution.py:14
  15.3 103.5 %collective-permute-start.2 = (bf16[448,1152]{1,0:T(8,128)(2,1)}, bf16[448,1152]{1,0:T(8,128)(2,1)S(1)}, u32[]{:S(2)}, u32[]{:S(2)}) collective-permute-start(bf16[448,1152]{1,0:T(8,128)(2,1)} %param.6), channel_id=1, source_target_pairs={{0,8},{8,0},{4,12},{12,4},{16,24},{24,16},{20,28},{28,20},{32,40},... | collective-permute-start | bytes 3096584 | tf_op jit(solution)/shard_map/ppermute | solution.py:14
  20.0 110.4 %collective-permute-start = (bf16[448,1152]{1,0:T(8,128)(2,1)}, bf16[448,1152]{1,0:T(8,128)(2,1)}, u32[]{:S(2)}, u32[]{:S(2)}) collective-permute-start(bf16[448,1152]{1,0:T(8,128)(2,1)} %param.6), channel_id=1, source_target_pairs={{0,1},{1,0},{2,3},{3,2},{4,5},{5,4},{6,7},{7,6},{8,9},{9,8},{10,11... | collective-permute-start | bytes 3096584 | tf_op jit(solution)/shard_map/ppermute | solution.py:14
  23.1 102.1 %collective-permute-start.1 = (bf16[448,1152]{1,0:T(8,128)(2,1)}, bf16[448,1152]{1,0:T(8,128)(2,1)}, u32[]{:S(2)}, u32[]{:S(2)}) collective-permute-start(bf16[448,1152]{1,0:T(8,128)(2,1)} %param.6), channel_id=1, source_target_pairs={{0,4},{4,0},{8,12},{12,8},{16,20},{20,16},{24,28},{28,24},{32,36},... | collective-permute-start | bytes 3096584 | tf_op jit(solution)/shard_map/ppermute | solution.py:14
  106.5 12.4 %copy-start.2 = (s32[448]{0:T(512)S(1)}, s32[448]{0:T(512)}, u32[]{:S(2)}) copy-start(s32[448]{0:T(512)} %param.7) | copy-start | bytes 5380
  107.3 184.6 %collective-permute-start.7 = (f32[448,1152]{1,0:T(8,128)S(1)}, f32[448,1152]{1,0:T(8,128)S(1)}, u32[]{:S(2)}, u32[]{:S(2)}) collective-permute-start(f32[448,1152]{1,0:T(8,128)S(1)} %fusion.50), channel_id=1, source_target_pairs={{0,256},{256,0},{4,260},{260,4},{8,264},{264,8},{12,268},{268,12},... | collective-permute-start | bytes 6193160 | tf_op jit(solution)/shard_map/ppermute | solution.py:14
  120.5 171.4 %collective-permute-start.6 = (f32[448,1152]{1,0:T(8,128)S(1)}, f32[448,1152]{1,0:T(8,128)S(1)}, u32[]{:S(2)}, u32[]{:S(2)}) collective-permute-start(f32[448,1152]{1,0:T(8,128)S(1)} %fusion.49), channel_id=1, source_target_pairs={{0,8},{8,0},{4,12},{12,4},{16,24},{24,16},{20,28},{28,20},{32,40},... | collective-permute-start | bytes 6193160 | tf_op jit(solution)/shard_map/ppermute | solution.py:14
  128.2 163.7 %collective-permute-start.5 = (f32[448,1152]{1,0:T(8,128)S(1)}, f32[448,1152]{1,0:T(8,128)S(1)}, u32[]{:S(2)}, u32[]{:S(2)}) collective-permute-start(f32[448,1152]{1,0:T(8,128)S(1)} %fusion.48), channel_id=1, source_target_pairs={{0,4},{4,0},{8,12},{12,8},{16,20},{20,16},{24,28},{28,24},{32,36},... | collective-permute-start | bytes 6193160 | tf_op jit(solution)/shard_map/ppermute | solution.py:14
  132.6 5.2 %copy-start.1 = (bf16[448,1152]{1,0:T(8,128)(2,1)S(1)}, bf16[448,1152]{1,0:T(8,128)(2,1)}, u32[]{:S(2)}) copy-start(bf16[448,1152]{1,0:T(8,128)(2,1)} %param.6) | copy-start | bytes 3096580
  133.4 158.5 %collective-permute-start.4 = (f32[448,1152]{1,0:T(8,128)S(1)}, f32[448,1152]{1,0:T(8,128)S(1)}, u32[]{:S(2)}, u32[]{:S(2)}) collective-permute-start(f32[448,1152]{1,0:T(8,128)S(1)} %fusion.47), channel_id=1, source_target_pairs={{0,1},{1,0},{2,3},{3,2},{4,5},{5,4},{6,7},{7,6},{8,9},{9,8},{10,11... | collective-permute-start | bytes 6193160 | tf_op jit(solution)/shard_map/ppermute | solution.py:14
where the time goes:
time: 294 us
  waiting for transfers between devices  224 us (76%)
  starting transfers between devices  47.5 us (16%)
  matrix products  20.1 us (7%)
    ppermute x8, waiting for transfers between devices, from_partner(): return lax.ppermute(block, axis, route)  224 us
    ppermute x8, starting transfers between devices, from_partner(): return lax.ppermute(block, axis, route)  47.5 us
    dot_general x5, matrix products, coeff_tile(): lax.dot_general(rows, cols, (((1,), (1,)), ((), ())), preferred_element_t...  7.78 us
    dot_general x5, matrix products, left_product(): return jnp.dot(coeff, data, preferred_element_type=jnp.float32)  7.22 us
  transfers between devices with their start and end apart: 8, of which 2 were waited for; matrix products, arithmetic and copies ran while one was open for 6% of the time, Pallas kernels for 0%

commit v1 on v0

v1 whole, which is shorter than its diff:
```python
import functools

import jax
import jax.numpy as jnp
from jax import lax
from jax.experimental import pallas as pl
from jax.experimental.pallas import tpu as pltpu
from jax.sharding import PartitionSpec as P

VMEM = pl.BlockSpec(memory_space=pltpu.VMEM)
SMEM = pl.BlockSpec(memory_space=pltpu.SMEM)
DIGIT_ROWS = 16


def from_partner(block, axis, bit):
    count = lax.axis_size(axis)
    return lax.ppermute(block, axis, [(i, i ^ (1 << bit)) for i in range(count)])


def gradient(rows, cols, hit, scale, shift):
    logits = scale * lax.dot_general(
        rows, cols, (((1,), (1,)), ((), ())), preferred_element_type=jnp.float32
    ) + shift
    coeff = (jax.nn.sigmoid(logits) - hit.astype(jnp.float32)).astype(jnp.bfloat16)
    return jnp.dot(coeff, cols, preferred_element_type=jnp.float32)


def hit_columns(label_column, base, count):
    return label_column - base == lax.broadcasted_iota(jnp.int32, (count, count), 1)


def hit_rows(label_row, base, count):
    return label_row - base == lax.broadcasted_iota(jnp.int32, (count, count), 0)


def label_row_of(digit_rows, count):
    d = digit_rows[:, :count].astype(jnp.float32)
    return (d[0:1] + 256.0 * d[1:2] + 65536.0 * d[2:3]).astype(jnp.int32)


def first_kernel(scalars, bases, img, txt, lab_col, lab_row, far_txt, img_acc, txt_acc):
    count = img.shape[0]
    scale, shift = scalars[0], scalars[1]
    img_acc[...] = gradient(img[...], far_txt[...], hit_columns(lab_col[...], bases[4], count), scale, shift)
    img_acc[...] += gradient(img[...], txt[...], hit_columns(lab_col[...], bases[0], count), scale, shift)
    txt_acc[...] = gradient(txt[...], img[...], hit_rows(lab_row[...], bases[0], count), scale, shift)


def near_kernel(which, last, scalars, bases, img, txt, lab_col, packed, img_in, txt_in, img_out, txt_out):
    count = img.shape[0]
    scale, shift = scalars[0], scalars[1]
    their_txt = packed[:count, :]
    their_img = packed[count : 2 * count, :]
    their_lab = label_row_of(packed[2 * count :, :], count)
    total = img_in[...] + gradient(
        img[...], their_txt, hit_columns(lab_col[...], bases[which], count), scale, shift
    )
    img_out[...] = (scale * total).astype(jnp.bfloat16) if last else total
    txt_out[...] = txt_in[...] + gradient(
        txt[...], their_img, hit_rows(their_lab, bases[0], count), scale, shift
    )


def last_kernel(scalars, bases, txt, packed, txt_in, image_grad, text_grad, image_grad_out):
    count = txt.shape[0]
    scale, shift = scalars[0], scalars[1]
    their_lab = label_row_of(packed[count:, :], count)
    total = txt_in[...] + gradient(
        txt[...], packed[:count, :], hit_rows(their_lab, bases[0], count), scale, shift
    )
    text_grad[...] = (scale * total).astype(jnp.bfloat16)


def cost(products, count, width):
    return pl.CostEstimate(
        flops=4 * products * count * count * width,
        bytes_accessed=6 * products * count * width,
        transcendentals=products * count * count,
    )


def local(images, texts, labels, log_scale, bias):
    count, width = images.shape
    pair_size = lax.axis_size("pair")
    far = lax.axis_size("dp").bit_length() - 2
    myself = lax.axis_index("dp") * pair_size + lax.axis_index("pair")

    far_txt = from_partner(texts, "dp", far)

    digits = jnp.stack([labels & 255, (labels >> 8) & 255, labels >> 16]).astype(jnp.bfloat16)
    digits = jnp.pad(digits, ((0, DIGIT_ROWS - 3), (0, width - count)))
    packed = jnp.concatenate([texts, images, digits], axis=0)
    near = [("pair", 0, 1), ("dp", 0, pair_size), ("dp", 1, 2 * pair_size)]
    arrived = [from_partner(packed, axis, bit) for axis, bit, _ in near]
    far_img = from_partner(jnp.concatenate([images, digits], axis=0), "dp", far)

    offsets = jnp.array([0, 1, pair_size, 2 * pair_size, pair_size << far], jnp.int32)
    bases = jnp.bitwise_xor(myself, offsets) * count
    scalars = jnp.concatenate([jnp.exp(log_scale), bias])
    lab_col = labels.reshape(count, 1)
    lab_row = labels.reshape(1, count)
    params = pltpu.CompilerParams(vmem_limit_bytes=48 << 20)
    acc = jax.ShapeDtypeStruct((count, width), jnp.float32)
    out = jax.ShapeDtypeStruct((count, width), jnp.bfloat16)

    img_acc, txt_acc = pl.pallas_call(
        first_kernel,
        out_shape=(acc, acc),
        in_specs=[SMEM, SMEM] + [VMEM] * 5,
        out_specs=(VMEM, VMEM),
        compiler_params=params,
        cost_estimate=cost(3, count, width),
        name="own_and_far_texts",
    )(scalars, bases, images, texts, lab_col, lab_row, far_txt)
    for at, got in enumerate(arrived):
        last = at == len(arrived) - 1
        img_acc, txt_acc = pl.pallas_call(
            functools.partial(near_kernel, at + 1, last),
            out_shape=(out if last else acc, acc),
            in_specs=[SMEM, SMEM] + [VMEM] * 6,
            out_specs=(VMEM, VMEM),
            compiler_params=params,
            cost_estimate=cost(2, count, width),
            name="near_partner",
        )(scalars, bases, images, texts, lab_col, got, img_acc, txt_acc)
    text_grad, image_grad = pl.pallas_call(
        last_kernel,
        out_shape=(out, out),
        in_specs=[SMEM, SMEM] + [VMEM] * 3 + [pl.BlockSpec(memory_space=pl.ANY)],
        out_specs=(VMEM, pl.BlockSpec(memory_space=pl.ANY)),
        input_output_aliases={5: 1},
        compiler_params=params,
        cost_estimate=cost(1, count, width),
        name="far_images",
    )(scalars, bases, texts, far_img, txt_acc, img_acc)
    return image_grad, text_grad


def solution(mesh):
    placed = (P(("dp", "pair"), None), P(("dp", "pair"), None), P(("dp", "pair")), P(), P())
    return jax.shard_map(
        local,
        mesh=mesh,
        in_specs=placed,
        out_specs=(P(("dp", "pair"), None), P(("dp", "pair"), None)),
        check_vma=False,
    )
```

time: 294 us -> 214 us (0.73)
  the two profiles are of different devices: /device:TPU:49 before, /device:TPU:48 now
where the time goes in v1:
time: 214 us
  waiting for transfers between devices  146 us (68%)
  Pallas kernels  29.4 us (14%)
  starting transfers between devices  26.8 us (13%)
  other arithmetic  5.05 us (2%)
  local copies, waits for them, and re-layouts  4.16 us (2%)
    ppermute x5, waiting for transfers between devices, from_partner(): return lax.ppermute(block, axis, [(i, i ^ 1 << bit) for i in range(count)])  146 us
    ppermute x5, starting transfers between devices, from_partner(): return lax.ppermute(block, axis, [(i, i ^ 1 << bit) for i in range(count)])  26.8 us
    pallas_call x3, Pallas kernels, local(): pl.pallas_call(functools.partial(near_kernel, at + 1, last), out_shape=(o...  19.6 us
    pallas_call x1, Pallas kernels, local(): pl.pallas_call(first_kernel, out_shape=(acc, acc), in_specs=[SMEM, SMEM]...  6.78 us
  transfers between devices with their start and end apart: 5, of which 2 were waited for; matrix products, arithmetic and copies ran while one was open for 1% of the time, Pallas kernels for 12%

profile of v1, /device:TPU:48, one launch (start us, length us, event | category | flops | bytes accessed | tf_op | source)
XLA Modules:
  0.0 214.0 jit_solution(5045087932835326214)
XLA Ops:
  0.6 0.7 and_convert_fusion.1
  1.4 0.0 copy-start
  1.4 0.0 copy-start.1
  1.4 3.2 %pad_maximum_fusion = bf16[912,1152]{1,0:T(8,128)(2,1)} fusion(bf16[16,1152]{1,0:T(8,128)(2,1)S(1)} %fusion.8, bf16[448,1152]{1,0:T(8,128)(2,1)} %img.7, bf16[448,1152]{1,0:T(8,128)(2,1)} %txt.9), kind=kLoop, calls=%fused_computation | loop fusion | flops 6303744 | bytes 4202496 | tf_op jit(solution)/shard_map/concatenate | solution.py:92
  4.6 0.0 copy-start.5
  4.6 0.0 copy-start.6
  4.6 2.0 collective-permute-start.3
  6.6 3.4 %collective-permute-start.2 = (bf16[912,1152]{1,0:T(8,128)(2,1)}, bf16[912,1152]{1,0:T(8,128)(2,1)}, u32[]{:S(2)}, u32[]{:S(2)}) collective-permute-start(bf16[912,1152]{1,0:T(8,128)(2,1)} %pad_maximum_fusion), channel_id=1, source_target_pairs={{0,4},{4,0},{8,12},{12,8},{16,20},{20,16},{24,28},{28,24},{32,36},... | collective-permute-start | bytes 6303752 | tf_op jit(solution)/shard_map/ppermute | solution.py:17
  10.0 4.6 %collective-permute-start.1 = (bf16[912,1152]{1,0:T(8,128)(2,1)}, bf16[912,1152]{1,0:T(8,128)(2,1)}, u32[]{:S(2)}, u32[]{:S(2)}) collective-permute-start(bf16[912,1152]{1,0:T(8,128)(2,1)} %pad_maximum_fusion), channel_id=1, source_target_pairs={{0,8},{4,12},{8,0},{12,4},{16,24},{20,28},{24,16},{28,20},{32,40},... | collective-permute-start | bytes 6303752 | tf_op jit(solution)/shard_map/ppermute | solution.py:17
  14.7 0.0 copy-done
  14.7 14.8 %collective-permute-start.4 = (bf16[448,1152]{1,0:T(8,128)(2,1)S(1)}, bf16[448,1152]{1,0:T(8,128)(2,1)}, u32[]{:S(2)}, u32[]{:S(2)}) collective-permute-start(bf16[448,1152]{1,0:T(8,128)(2,1)S(1)} %copy-done), channel_id=1, source_target_pairs={{0,256},{4,260},{8,264},{12,268},{16,272},{20,276},{24,280},{28,28... | collective-permute-start | bytes 3096584 | tf_op jit(solution)/shard_map/ppermute | solution.py:17
  29.5 0.0 copy-done.1
  29.5 1.1 pad_maximum_fusion.1
  30.6 1.9 collective-permute-start
  33.9 0.0 copy-done.5
  33.9 0.1 copy.12.lab_col
  34.0 0.1 pad_maximum_fusion.2.scalars
  34.1 0.0 copy-done.6
  34.1 132.9 %collective-permute-done.4.far_txt = bf16[448,1152]{1,0:T(8,128)(2,1)} collective-permute-done((bf16[448,1152]{1,0:T(8,128)(2,1)S(1)}, bf16[448,1152]{1,0:T(8,128)(2,1)}, u32[]{:S(2)}, u32[]{:S(2)}) %collective-permute-start.4) | collective-permute-done | bytes 1032224 | tf_op jit(solution)/shard_map/ppermute | solution.py:17
  167.0 6.8 %own_and_far_texts.1 = (f32[448,1152]{1,0:T(8,128)S(1)}, f32[448,1152]{1,0:T(8,128)}) custom-call(f32[2]{0:T(128)S(1)} %pad_maximum_fusion.2.scalars, s32[5]{0:T(128)S(1)} %xor_multiply_fusion.bases, bf16[448,1152]{1,0:T(8,128)(2,1)S(1)} %copy-done.1, bf16[448,1152]{1,0:T(8,128)(2,1)S(1)} %copy-done, s32[448,1]{1,0:T(8,128)S(1)} %copy.12.lab_col, ...), custom_call_target="tpu_custom_call" | custom-call | flops 2774532096 | bytes 9289728 | tf_op jit(solution)/shard_map/own_and_far_texts/pallas_call | solution.py:106
  173.8 0.0 copy-start.4
  173.8 1.3 copy-done.4
  175.1 0.0 collective-permute-done.3.packed
  175.1 7.0 %near_partner.3 = (f32[448,1152]{1,0:T(8,128)S(1)}, f32[448,1152]{1,0:T(8,128)}) custom-call(f32[2]{0:T(128)S(1)} %pad_maximum_fusion.2.scalars, s32[5]{0:T(128)S(1)} %xor_multiply_fusion.bases, bf16[448,1152]{1,0:T(8,128)(2,1)S(1)} %copy-done.1, bf16[448,1152]{1,0:T(8,128)(2,1)S(1)} %copy-done, s32[448,1]{1,0:T(8,128)S(1)} %copy.12.lab_col, ...), custom_call_target="tpu_custom_call" | custom-call | flops 1849688064 | bytes 6193152 | tf_op jit(solution)/shard_map/near_partner/pallas_call | solution.py:117
  182.1 0.0 copy-start.3
  182.1 1.3 copy-done.3
  183.5 0.0 collective-permute-done.2.packed
  183.5 7.0 %near_partner.4 = (f32[448,1152]{1,0:T(8,128)S(1)}, f32[448,1152]{1,0:T(8,128)}) custom-call(f32[2]{0:T(128)S(1)} %pad_maximum_fusion.2.scalars, s32[5]{0:T(128)S(1)} %xor_multiply_fusion.bases, bf16[448,1152]{1,0:T(8,128)(2,1)S(1)} %copy-done.1, bf16[448,1152]{1,0:T(8,128)(2,1)S(1)} %copy-done, s32[448,1]{1,0:T(8,128)S(1)} %copy.12.lab_col, ...), custom_call_target="tpu_custom_call" | custom-call | flops 1849688064 | bytes 6193152 | tf_op jit(solution)/shard_map/near_partner/pallas_call | solution.py:117
  190.4 0.0 copy-start.2
  190.4 1.3 copy-done.2
  191.8 0.0 collective-permute-done.1.packed
  191.8 5.6 %near_partner.5 = (bf16[448,1152]{1,0:T(8,128)(2,1)}, f32[448,1152]{1,0:T(8,128)S(1)}) custom-call(f32[2]{0:T(128)S(1)} %pad_maximum_fusion.2.scalars, s32[5]{0:T(128)S(1)} %xor_multiply_fusion.bases, bf16[448,1152]{1,0:T(8,128)(2,1)S(1)} %copy-done.1, bf16[448,1152]{1,0:T(8,128)(2,1)S(1)} %copy-done, s32[448,1]{1,0:T(8,128)S(1)} %copy.12.lab_col, ...), custom_call_target="tpu_custom_call" | custom-call | flops 1849688064 | bytes 6193152 | tf_op jit(solution)/shard_map/near_partner/pallas_call | solution.py:117
  197.4 13.6 %collective-permute-done.packed = bf16[464,1152]{1,0:T(8,128)(2,1)S(1)} collective-permute-done((bf16[464,1152]{1,0:T(8,128)(2,1)}, bf16[464,1152]{1,0:T(8,128)(2,1)S(1)}, u32[]{:S(2)}, u32[]{:S(2)}) %collective-permute-start) | collective-permute-done | bytes 1069088 | tf_op jit(solution)/shard_map/ppermute | solution.py:17
  211.0 3.0 %far_images.1 = (bf16[448,1152]{1,0:T(8,128)(2,1)}, bf16[448,1152]{1,0:T(8,128)(2,1)}) custom-call(f32[2]{0:T(128)S(1)} %pad_maximum_fusion.2.scalars, s32[5]{0:T(128)S(1)} %xor_multiply_fusion.bases, bf16[448,1152]{1,0:T(8,128)(2,1)S(1)} %copy-done, bf16[464,1152]{1,0:T(8,128)(2,1)S(1)} %collective-permute-done.packed, ...), custom_call_target="tpu_custom_call", output_to_operand_aliasing={{1}: (5, {})} | custom-call | flops 924844032 | bytes 3096576 | tf_op jit(solution)/shard_map/far_images/pallas_call | solution.py:126
  (5 shorter events, 0.0 us)
Async XLA Ops:
  1.4 13.3 %copy-start = (bf16[448,1152]{1,0:T(8,128)(2,1)S(1)}, bf16[448,1152]{1,0:T(8,128)(2,1)}, u32[]{:S(2)}) copy-start(bf16[448,1152]{1,0:T(8,128)(2,1)} %txt.9) | copy-start | bytes 3096580
  1.4 28.1 %copy-start.1 = (bf16[448,1152]{1,0:T(8,128)(2,1)S(1)}, bf16[448,1152]{1,0:T(8,128)(2,1)}, u32[]{:S(2)}) copy-start(bf16[448,1152]{1,0:T(8,128)(2,1)} %img.7) | copy-start | bytes 3096580
  4.6 29.3 %copy-start.5 = (s32[448]{0:T(512)S(1)}, s32[448]{0:T(512)}, u32[]{:S(2)}) copy-start(s32[448]{0:T(512)} %param.8) | copy-start | bytes 5380
  4.6 29.5 %copy-start.6 = (s32[5]{0:T(128)S(1)}, s32[5]{0:T(128)}, u32[]{:S(2)}) copy-start(s32[5]{0:T(128)} %constant.24.clone) | copy-start | bytes 64
  4.6 170.6 %collective-permute-start.3 = (bf16[912,1152]{1,0:T(8,128)(2,1)}, bf16[912,1152]{1,0:T(8,128)(2,1)}, u32[]{:S(2)}, u32[]{:S(2)}) collective-permute-start(bf16[912,1152]{1,0:T(8,128)(2,1)} %pad_maximum_fusion), channel_id=1, source_target_pairs={{0,1},{1,0},{2,3},{3,2},{4,5},{5,4},{6,7},{7,6},{8,9},{9,8},{10,11... | collective-permute-start | bytes 6303752 | tf_op jit(solution)/shard_map/ppermute | solution.py:17
  6.6 176.8 %collective-permute-start.2 = (bf16[912,1152]{1,0:T(8,128)(2,1)}, bf16[912,1152]{1,0:T(8,128)(2,1)}, u32[]{:S(2)}, u32[]{:S(2)}) collective-permute-start(bf16[912,1152]{1,0:T(8,128)(2,1)} %pad_maximum_fusion), channel_id=1, source_target_pairs={{0,4},{4,0},{8,12},{12,8},{16,20},{20,16},{24,28},{28,24},{32,36},... | collective-permute-start | bytes 6303752 | tf_op jit(solution)/shard_map/ppermute | solution.py:17
  10.0 181.7 %collective-permute-start.1 = (bf16[912,1152]{1,0:T(8,128)(2,1)}, bf16[912,1152]{1,0:T(8,128)(2,1)}, u32[]{:S(2)}, u32[]{:S(2)}) collective-permute-start(bf16[912,1152]{1,0:T(8,128)(2,1)} %pad_maximum_fusion), channel_id=1, source_target_pairs={{0,8},{4,12},{8,0},{12,4},{16,24},{20,28},{24,16},{28,20},{32,40},... | collective-permute-start | bytes 6303752 | tf_op jit(solution)/shard_map/ppermute | solution.py:17
  14.7 152.3 %collective-permute-start.4 = (bf16[448,1152]{1,0:T(8,128)(2,1)S(1)}, bf16[448,1152]{1,0:T(8,128)(2,1)}, u32[]{:S(2)}, u32[]{:S(2)}) collective-permute-start(bf16[448,1152]{1,0:T(8,128)(2,1)S(1)} %copy-done), channel_id=1, source_target_pairs={{0,256},{4,260},{8,264},{12,268},{16,272},{20,276},{24,280},{28,28... | collective-permute-start | bytes 3096584 | tf_op jit(solution)/shard_map/ppermute | solution.py:17
  30.6 180.3 %collective-permute-start = (bf16[464,1152]{1,0:T(8,128)(2,1)}, bf16[464,1152]{1,0:T(8,128)(2,1)S(1)}, u32[]{:S(2)}, u32[]{:S(2)}) collective-permute-start(bf16[464,1152]{1,0:T(8,128)(2,1)} %pad_maximum_fusion.1), channel_id=1, source_target_pairs={{0,256},{4,260},{8,264},{12,268},{16,272},{20,276},{24,280},{28,28... | collective-permute-start | bytes 3207176 | tf_op jit(solution)/shard_map/ppermute | solution.py:17
  173.8 1.3 copy-start.4
  182.1 1.3 copy-start.3
  190.4 1.3 copy-start.2

commit v2 on v1

v2 whole, which is shorter than its diff:
```python
import jax
import jax.numpy as jnp
from jax import lax
from jax.experimental import pallas as pl
from jax.experimental.pallas import tpu as pltpu
from jax.sharding import PartitionSpec as P

VMEM = pl.BlockSpec(memory_space=pltpu.VMEM)
SMEM = pl.BlockSpec(memory_space=pltpu.SMEM)
DIGIT_ROWS = 16
CHUNKS = 2


def from_partner(block, axis, bit):
    count = lax.axis_size(axis)
    return lax.ppermute(block, axis, [(i, i ^ (1 << bit)) for i in range(count)])


def gradient(rows, cols, hit, scale, shift):
    logits = scale * lax.dot_general(
        rows, cols, (((1,), (1,)), ((), ())), preferred_element_type=jnp.float32
    ) + shift
    coeff = (jax.nn.sigmoid(logits) - hit.astype(jnp.float32)).astype(jnp.bfloat16)
    return jnp.dot(coeff, cols, preferred_element_type=jnp.float32)


def hit_columns(label_column, base, count, chunk):
    return label_column - base == lax.broadcasted_iota(jnp.int32, (count, chunk), 1)


def hit_rows(label_row, base, count, chunk):
    return label_row - base == lax.broadcasted_iota(jnp.int32, (count, chunk), 0)


def label_row_of(digit_rows, count):
    d = digit_rows[:, :count].astype(jnp.float32)
    return (d[0:1] + 256.0 * d[1:2] + 65536.0 * d[2:3]).astype(jnp.int32)


def own_kernel(scalars, bases, img, txt, lab_col, lab_row, img_acc, txt_acc):
    count = img.shape[0]
    scale, shift = scalars[0], scalars[1]
    img_acc[...] = gradient(img[...], txt[...], hit_columns(lab_col[...], bases[0], count, count), scale, shift)
    txt_acc[...] = gradient(txt[...], img[...], hit_rows(lab_row[...], bases[0], count, count), scale, shift)


def near_kernel(bases, scalars, img, txt, lab_col, near1, near2, near3, img_in, txt_in, img_out, txt_out):
    count = img.shape[0]
    chunk = (near1.shape[0] - DIGIT_ROWS) // 2
    scale, shift = scalars[0], scalars[1]
    img_total, txt_total = img_in[...], txt_in[...]
    for which, near in ((1, near1), (2, near2), (3, near3)):
        hit = hit_columns(lab_col[...], bases[which] + bases[5], count, chunk)
        img_total += gradient(img[...], near[:chunk, :], hit, scale, shift)
        hit = hit_rows(label_row_of(near[2 * chunk :, :], chunk), bases[0], count, chunk)
        txt_total += gradient(txt[...], near[chunk : 2 * chunk, :], hit, scale, shift)
    img_out[...] = img_total
    txt_out[...] = txt_total


def far_texts_kernel(scalars, bases, img, lab_col, far_txt, img_in, image_grad):
    count = img.shape[0]
    scale, shift = scalars[0], scalars[1]
    hit = hit_columns(lab_col[...], bases[4], count, count)
    total = img_in[...] + gradient(img[...], far_txt[...], hit, scale, shift)
    image_grad[...] = (scale * total).astype(jnp.bfloat16)


def far_images_kernel(scalars, bases, txt, packed, txt_in, image_grad, text_grad, image_grad_out):
    count = txt.shape[0]
    scale, shift = scalars[0], scalars[1]
    hit = hit_rows(label_row_of(packed[count:, :], count), bases[0], count, count)
    total = txt_in[...] + gradient(txt[...], packed[:count, :], hit, scale, shift)
    text_grad[...] = (scale * total).astype(jnp.bfloat16)


def cost(products, count, width):
    return pl.CostEstimate(
        flops=4 * products * count * count * width,
        bytes_accessed=6 * products * count * width,
        transcendentals=products * count * count,
    )


def local(images, texts, labels, log_scale, bias):
    count, width = images.shape
    pair_size = lax.axis_size("pair")
    far = lax.axis_size("dp").bit_length() - 2
    myself = lax.axis_index("dp") * pair_size + lax.axis_index("pair")

    anywhere = pl.BlockSpec(memory_space=pl.ANY)
    params = pltpu.CompilerParams(vmem_limit_bytes=48 << 20)
    acc = jax.ShapeDtypeStruct((count, width), jnp.float32)
    out = jax.ShapeDtypeStruct((count, width), jnp.bfloat16)

    def kernel(body, out_shape, *args, passed=None, products=1):
        many = isinstance(out_shape, tuple)
        specs = [SMEM, SMEM] + [VMEM] * (len(args) - 2)
        out_specs = (VMEM,) * len(out_shape) if many else VMEM
        aliases = {}
        if passed is not None:
            specs[-1] = anywhere
            out_specs = out_specs[:-1] + (anywhere,)
            aliases = {len(args) - 1: len(out_shape) - 1}
        return pl.pallas_call(
            body,
            out_shape=out_shape,
            in_specs=specs,
            out_specs=out_specs,
            input_output_aliases=aliases,
            compiler_params=params,
            cost_estimate=cost(products, count, width),
            name=body.__name__,
        )(*args)

    digits = jnp.stack([labels & 255, (labels >> 8) & 255, labels >> 16]).astype(jnp.bfloat16)
    digits = jnp.pad(digits, ((0, DIGIT_ROWS - 3), (0, width - count)))
    far_txt = from_partner(texts, "dp", far)
    far_img = from_partner(jnp.concatenate([images, digits], axis=0), "dp", far)

    offsets = jnp.array([0, 1, pair_size, 2 * pair_size, pair_size << far], jnp.int32)
    bases = jnp.bitwise_xor(myself, offsets) * count
    scalars = jnp.concatenate([jnp.exp(log_scale), bias])
    lab_col = labels.reshape(count, 1)
    lab_row = labels.reshape(1, count)

    sums = kernel(own_kernel, (acc, acc), scalars, bases, images, texts, lab_col, lab_row, products=2)
    chunk = count // CHUNKS

    def near(step, sums):
        at = step * chunk
        part = jnp.concatenate(
            [
                lax.dynamic_slice_in_dim(texts, at, chunk, 0),
                lax.dynamic_slice_in_dim(images, at, chunk, 0),
                jnp.pad(
                    lax.dynamic_slice_in_dim(digits, at, chunk, 1), ((0, 0), (0, width - chunk))
                ),
            ],
            axis=0,
        )
        arrived = [from_partner(part, axis, bit) for axis, bit in (("dp", 1), ("dp", 0), ("pair", 0))]
        here = jnp.concatenate([bases, jnp.reshape(at, (1,))])
        return kernel(
            near_kernel, (acc, acc), here, scalars, images, texts, lab_col, *arrived[::-1], *sums, products=3
        )

    img_acc, txt_acc = lax.fori_loop(0, CHUNKS, near, sums)
    image_grad = kernel(far_texts_kernel, out, scalars, bases, images, lab_col, far_txt, img_acc)
    text_grad, image_grad = kernel(
        far_images_kernel, (out, out), scalars, bases, texts, far_img, txt_acc, image_grad, passed=image_grad
    )
    return image_grad, text_grad


def solution(mesh):
    placed = (P(("dp", "pair"), None), P(("dp", "pair"), None), P(("dp", "pair")), P(), P())
    return jax.shard_map(
        local,
        mesh=mesh,
        in_specs=placed,
        out_specs=(P(("dp", "pair"), None), P(("dp", "pair"), None)),
        check_vma=False,
    )
```

time: 214 us -> 201 us (0.939)
  the two profiles are of different devices: /device:TPU:48 before, /device:TPU:37 now
where the time goes in v2:
time: 201 us; the launch traced here: 200 us
  waiting for transfers between devices  117 us (58%)
  starting transfers between devices  33.7 us (17%)
  Pallas kernels  33.5 us (17%)
  local copies, waits for them, and re-layouts  8.97 us (4%)
  other arithmetic  5.39 us (3%)
  between operations  2.06 us (1%)
    ppermute x8, waiting for transfers between devices, from_partner(): return lax.ppermute(block, axis, [(i, i ^ 1 << bit) for i in range(count)])  117 us
    ppermute x8, starting transfers between devices, from_partner(): return lax.ppermute(block, axis, [(i, i ^ 1 << bit) for i in range(count)])  33.7 us
    pallas_call x5, Pallas kernels, kernel(): pl.pallas_call(body, out_shape=out_shape, in_specs=specs, out_specs=out_s...  33.5 us
    while x12, local copies, waits for them, and re-layouts  5.8 us
  transfers between devices with their start and end apart: 8, of which 5 were waited for; matrix products, arithmetic and copies ran while one was open for 6% of the time, Pallas kernels for 15%

profile of v2, /device:TPU:37, one launch (start us, length us, event | category | flops | bytes accessed | tf_op | source)
XLA Modules:
  0.0 200.2 jit_solution(11617400776101272820)
XLA Ops:
  0.6 0.0 copy-start.5
  0.6 0.0 copy-start
  0.7 14.7 %collective-permute-start.4 = (bf16[448,1152]{1,0:T(8,128)(2,1)}, bf16[448,1152]{1,0:T(8,128)(2,1)}, u32[]{:S(2)}, u32[]{:S(2)}) collective-permute-start(bf16[448,1152]{1,0:T(8,128)(2,1)} %txt.3), channel_id=1, source_target_pairs={{0,256},{4,260},{8,264},{12,268},{16,272},{20,276},{24,280},{28,28... | collective-permute-start | bytes 3096584 | tf_op jit(solution)/shard_map/ppermute | solution.py:16
  15.3 0.7 and_convert_fusion.1
  16.1 2.3 %pad_maximum_fusion = bf16[464,1152]{1,0:T(8,128)(2,1)} fusion(bf16[16,1152]{1,0:T(8,128)(2,1)S(1)} %fusion.12, bf16[448,1152]{1,0:T(8,128)(2,1)} %img.3), kind=kLoop, calls=%fused_computation.9 | loop fusion | flops 2138112 | bytes 2138112 | tf_op jit(solution)/shard_map/concatenate | solution.py:119
  18.4 1.9 collective-permute-start.3
  21.6 0.0 copy-done
  21.6 0.1 copy.9.lab_col
  21.8 0.0 copy-done.5
  21.8 0.1 pad_maximum_fusion.1.scalars
  21.9 0.0 copy-start.4
  21.9 5.7 %own_kernel.1 = (f32[448,1152]{1,0:T(8,128)}, f32[448,1152]{1,0:T(8,128)}) custom-call(f32[2]{0:T(128)S(1)} %pad_maximum_fusion.1.scalars, s32[5]{0:T(128)S(1)} %xor_multiply_fusion.1.bases, bf16[448,1152]{1,0:T(8,128)(2,1)} %img.3, bf16[448,1152]{1,0:T(8,128)(2,1)} %txt.3, s32[448,1]{1,0:T(8,128)S(1)} %copy.9.lab_col, s32[1,448]{1,0:T(1,128)S(1)} %bitcast.6), custom_call_target="tpu_custom_call" | custom-call | flops 1849688064 | bytes 6193152 | tf_op jit(solution)/shard_map/own_kernel/pallas_call | solution.py:105
  27.6 0.0 copy-done.4
  27.6 131.7 %while.18 = (s32[]{:T(128)}, f32[448,1152]{1,0:T(8,128)}, f32[448,1152]{1,0:T(8,128)}, bf16[448,1152]{1,0:T(8,128)(2,1)}, bf16[448,1152]{1,0:T(8,128)(2,1)}, /*i...) while((s32[]{:T(128)}, f32[448,1152]{1,0:T(8,128)}, ...), condition=%wide.region_1.2_spmd.clone, body=%wide.region_0.1_spmd.clone.sunk | while | flops 2778808320 | bytes 51078632 | solution.py:148
  27.6 0.1 constant_dynamic-slice_fusion.5
  27.7 0.0 copy-start.1
  27.7 1.4 constant_dynamic-slice_fusion.6
  29.1 1.1 fusion.14
  30.1 2.8 %collective-permute-start = (bf16[464,1152]{1,0:T(8,128)(2,1)}, bf16[464,1152]{1,0:T(8,128)(2,1)}, u32[]{:S(2)}, u32[]{:S(2)}) collective-permute-start(bf16[464,1152]{1,0:T(8,128)(2,1)} %fusion.14), channel_id=1, source_target_pairs={{0,1},{1,0},{2,3},{3,2},{4,5},{5,4},{6,7},{7,6},{8,9},{9,8},{10,11... | collective-permute-start | bytes 3207176 | tf_op jit(solution)/shard_map/while/body/eval_jaxpr/ppermute | solution.py:16
  33.0 2.8 %collective-permute-start.1 = (bf16[464,1152]{1,0:T(8,128)(2,1)}, bf16[464,1152]{1,0:T(8,128)(2,1)}, u32[]{:S(2)}, u32[]{:S(2)}) collective-permute-start(bf16[464,1152]{1,0:T(8,128)(2,1)} %fusion.14), channel_id=1, source_target_pairs={{0,4},{4,0},{8,12},{12,8},{16,20},{20,16},{24,28},{28,24},{32,36},... | collective-permute-start | bytes 3207176 | tf_op jit(solution)/shard_map/while/body/eval_jaxpr/ppermute | solution.py:16
  35.8 2.4 %collective-permute-start.2 = (bf16[464,1152]{1,0:T(8,128)(2,1)}, bf16[464,1152]{1,0:T(8,128)(2,1)}, u32[]{:S(2)}, u32[]{:S(2)}) collective-permute-start(bf16[464,1152]{1,0:T(8,128)(2,1)} %fusion.14), channel_id=1, source_target_pairs={{0,8},{4,12},{8,0},{12,4},{16,24},{20,28},{24,16},{28,20},{32,40},... | collective-permute-start | bytes 3207176 | tf_op jit(solution)/shard_map/while/body/eval_jaxpr/ppermute | solution.py:16
  38.3 0.0 copy-done.1
  38.3 0.0 copy-start.2
  38.3 0.1 copy.26.img_in
  38.4 1.4 copy-done.2
  39.9 1.3 copy.27.txt_in
  41.2 0.1 pad_add_fusion.2.bases
  41.3 0.0 collective-permute-done.near1
  41.3 19.2 %collective-permute-done.1.near2 = bf16[464,1152]{1,0:T(8,128)(2,1)} collective-permute-done((bf16[464,1152]{1,0:T(8,128)(2,1)}, bf16[464,1152]{1,0:T(8,128)(2,1)}, u32[]{:S(2)}, u32[]{:S(2)}) %collective-permute-start.1) | collective-permute-done | bytes 1069088 | tf_op jit(solution)/shard_map/while/body/eval_jaxpr/ppermute | solution.py:16
  60.4 22.9 %collective-permute-done.2.near3 = bf16[464,1152]{1,0:T(8,128)(2,1)} collective-permute-done((bf16[464,1152]{1,0:T(8,128)(2,1)}, bf16[464,1152]{1,0:T(8,128)(2,1)}, u32[]{:S(2)}, u32[]{:S(2)}) %collective-permute-start.2) | collective-permute-done | bytes 1069088 | tf_op jit(solution)/shard_map/while/body/eval_jaxpr/ppermute | solution.py:16
  83.3 9.7 %near_kernel.8 = (f32[448,1152]{1,0:T(8,128)}, f32[448,1152]{1,0:T(8,128)}) custom-call(s32[6]{0:T(128)S(1)} %pad_add_fusion.2.bases, f32[2]{0:T(128)S(1)} %get-tuple-element.385.scalars, bf16[448,1152]{1,0:T(8,128)(2,1)} %get-tuple-element.383.img, bf16[448,1152]{1,0:T(8,128)(2,1)} %get-tuple-element.382.txt, s32[448,1]{1,0:T(8,128)S(1)} %get-tuple-element.386.lab_col, ...), custom_call_target="tpu_custom_call" | custom-call | flops 2774532096 | bytes 9289728 | tf_op jit(solution)/shard_map/while/body/eval_jaxpr/near_kernel/pallas_call | solution.py:105
  93.0 0.1 constant_dynamic-slice_fusion.5
  93.0 0.0 copy-start.1
  93.0 1.4 constant_dynamic-slice_fusion.6
  94.5 1.1 fusion.14
  95.5 2.7 %collective-permute-start = (bf16[464,1152]{1,0:T(8,128)(2,1)}, bf16[464,1152]{1,0:T(8,128)(2,1)}, u32[]{:S(2)}, u32[]{:S(2)}) collective-permute-start(bf16[464,1152]{1,0:T(8,128)(2,1)} %fusion.14), channel_id=1, source_target_pairs={{0,1},{1,0},{2,3},{3,2},{4,5},{5,4},{6,7},{7,6},{8,9},{9,8},{10,11... | collective-permute-start | bytes 3207176 | tf_op jit(solution)/shard_map/while/body/eval_jaxpr/ppermute | solution.py:16
  98.2 2.8 %collective-permute-start.1 = (bf16[464,1152]{1,0:T(8,128)(2,1)}, bf16[464,1152]{1,0:T(8,128)(2,1)}, u32[]{:S(2)}, u32[]{:S(2)}) collective-permute-start(bf16[464,1152]{1,0:T(8,128)(2,1)} %fusion.14), channel_id=1, source_target_pairs={{0,4},{4,0},{8,12},{12,8},{16,20},{20,16},{24,28},{28,24},{32,36},... | collective-permute-start | bytes 3207176 | tf_op jit(solution)/shard_map/while/body/eval_jaxpr/ppermute | solution.py:16
  101.0 3.5 %collective-permute-start.2 = (bf16[464,1152]{1,0:T(8,128)(2,1)}, bf16[464,1152]{1,0:T(8,128)(2,1)}, u32[]{:S(2)}, u32[]{:S(2)}) collective-permute-start(bf16[464,1152]{1,0:T(8,128)(2,1)} %fusion.14), channel_id=1, source_target_pairs={{0,8},{4,12},{8,0},{12,4},{16,24},{20,28},{24,16},{28,20},{32,40},... | collective-permute-start | bytes 3207176 | tf_op jit(solution)/shard_map/while/body/eval_jaxpr/ppermute | solution.py:16
  104.5 0.0 copy-done.1
  104.5 0.0 copy-start.2
  104.6 0.1 copy.26.img_in
  104.7 1.4 copy-done.2
  106.1 1.3 copy.27.txt_in
  107.5 0.1 pad_add_fusion.2.bases
  107.5 0.0 collective-permute-done.near1
  107.5 18.1 %collective-permute-done.1.near2 = bf16[464,1152]{1,0:T(8,128)(2,1)} collective-permute-done((bf16[464,1152]{1,0:T(8,128)(2,1)}, bf16[464,1152]{1,0:T(8,128)(2,1)}, u32[]{:S(2)}, u32[]{:S(2)}) %collective-permute-start.1) | collective-permute-done | bytes 1069088 | tf_op jit(solution)/shard_map/while/body/eval_jaxpr/ppermute | solution.py:16
  125.7 24.0 %collective-permute-done.2.near3 = bf16[464,1152]{1,0:T(8,128)(2,1)} collective-permute-done((bf16[464,1152]{1,0:T(8,128)(2,1)}, bf16[464,1152]{1,0:T(8,128)(2,1)}, u32[]{:S(2)}, u32[]{:S(2)}) %collective-permute-start.2) | collective-permute-done | bytes 1069088 | tf_op jit(solution)/shard_map/while/body/eval_jaxpr/ppermute | solution.py:16
  149.6 9.7 %near_kernel.8 = (f32[448,1152]{1,0:T(8,128)}, f32[448,1152]{1,0:T(8,128)}) custom-call(s32[6]{0:T(128)S(1)} %pad_add_fusion.2.bases, f32[2]{0:T(128)S(1)} %get-tuple-element.385.scalars, bf16[448,1152]{1,0:T(8,128)(2,1)} %get-tuple-element.383.img, bf16[448,1152]{1,0:T(8,128)(2,1)} %get-tuple-element.382.txt, s32[448,1]{1,0:T(8,128)S(1)} %get-tuple-element.386.lab_col, ...), custom_call_target="tpu_custom_call" | custom-call | flops 2774532096 | bytes 9289728 | tf_op jit(solution)/shard_map/while/body/eval_jaxpr/near_kernel/pallas_call | solution.py:105
  159.3 0.0 collective-permute-done.4.far_txt
  159.3 0.0 copy-start.3
  159.3 4.8 %far_texts_kernel.1.image_grad = bf16[448,1152]{1,0:T(8,128)(2,1)} custom-call(f32[2]{0:T(128)S(1)} %get-tuple-element.396, s32[5]{0:T(128)S(1)} %xor_multiply_fusion.1.bases, bf16[448,1152]{1,0:T(8,128)(2,1)} %img.3, s32[448,1]{1,0:T(8,128)S(1)} %get-tuple-element.395, bf16[448,1152]{1,0:T(8,128)(2,1)} %collective-permute-done.4.far_txt, ...), custom_call_target="tpu_custom_call" | custom-call | flops 924844032 | bytes 3096576 | tf_op jit(solution)/shard_map/far_texts_kernel/pallas_call | solution.py:105
  164.1 32.4 %collective-permute-done.3.packed = bf16[464,1152]{1,0:T(8,128)(2,1)S(1)} collective-permute-done((bf16[464,1152]{1,0:T(8,128)(2,1)}, bf16[464,1152]{1,0:T(8,128)(2,1)S(1)}, u32[]{:S(2)}, u32[]{:S(2)}) %collective-permute-start.3) | collective-permute-done | bytes 1069088 | tf_op jit(solution)/shard_map/ppermute | solution.py:16
  196.5 0.0 copy-done.3
  196.5 3.7 %far_images_kernel.1 = (bf16[448,1152]{1,0:T(8,128)(2,1)}, bf16[448,1152]{1,0:T(8,128)(2,1)}) custom-call(f32[2]{0:T(128)S(1)} %get-tuple-element.396, s32[5]{0:T(128)S(1)} %xor_multiply_fusion.1.bases, bf16[448,1152]{1,0:T(8,128)(2,1)} %txt.3, bf16[464,1152]{1,0:T(8,128)(2,1)S(1)} %collective-permute-done.3.packed, ...), custom_call_target="tpu_custom_call", output_to_operand_aliasing={{1}: (5, {})} | custom-call | flops 924844032 | bytes 3096576 | tf_op jit(solution)/shard_map/far_images_kernel/pallas_call | solution.py:105
  (7 shorter events, 0.0 us)
Async XLA Ops:
  0.6 21.2 %copy-start.5 = (s32[5]{0:T(128)S(1)}, s32[5]{0:T(128)}, u32[]{:S(2)}) copy-start(s32[5]{0:T(128)} %constant.78.clone) | copy-start | bytes 64
  0.6 21.0 %copy-start = (s32[448]{0:T(512)S(1)}, s32[448]{0:T(512)}, u32[]{:S(2)}) copy-start(s32[448]{0:T(512)} %param.10) | copy-start | bytes 5380
  0.7 158.7 %collective-permute-start.4 = (bf16[448,1152]{1,0:T(8,128)(2,1)}, bf16[448,1152]{1,0:T(8,128)(2,1)}, u32[]{:S(2)}, u32[]{:S(2)}) collective-permute-start(bf16[448,1152]{1,0:T(8,128)(2,1)} %txt.3), channel_id=1, source_target_pairs={{0,256},{4,260},{8,264},{12,268},{16,272},{20,276},{24,280},{28,28... | collective-permute-start | bytes 3096584 | tf_op jit(solution)/shard_map/ppermute | solution.py:16
  18.4 178.1 %collective-permute-start.3 = (bf16[464,1152]{1,0:T(8,128)(2,1)}, bf16[464,1152]{1,0:T(8,128)(2,1)S(1)}, u32[]{:S(2)}, u32[]{:S(2)}) collective-permute-start(bf16[464,1152]{1,0:T(8,128)(2,1)} %pad_maximum_fusion), channel_id=1, source_target_pairs={{0,256},{4,260},{8,264},{12,268},{16,272},{20,276},{24,280},{28,28... | collective-permute-start | bytes 3207176 | tf_op jit(solution)/shard_map/ppermute | solution.py:16
  21.9 5.7 %copy-start.4 = (s32[5]{0:T(128)S(1)}, s32[5]{0:T(128)}, u32[]{:S(2)}) copy-start(s32[5]{0:T(128)} %constant.78.clone.5) | copy-start | bytes 64
  27.7 10.6 %copy-start.1 = (f32[448,1152]{1,0:T(8,128)S(1)}, f32[448,1152]{1,0:T(8,128)}, u32[]{:S(2)}) copy-start(f32[448,1152]{1,0:T(8,128)} %get-tuple-element.365) | copy-start | bytes 6193156 | tf_op jit(solution)/shard_map/while
  30.1 11.1 %collective-permute-start = (bf16[464,1152]{1,0:T(8,128)(2,1)}, bf16[464,1152]{1,0:T(8,128)(2,1)}, u32[]{:S(2)}, u32[]{:S(2)}) collective-permute-start(bf16[464,1152]{1,0:T(8,128)(2,1)} %fusion.14), channel_id=1, source_target_pairs={{0,1},{1,0},{2,3},{3,2},{4,5},{5,4},{6,7},{7,6},{8,9},{9,8},{10,11... | collective-permute-start | bytes 3207176 | tf_op jit(solution)/shard_map/while/body/eval_jaxpr/ppermute | solution.py:16
  33.0 27.4 %collective-permute-start.1 = (bf16[464,1152]{1,0:T(8,128)(2,1)}, bf16[464,1152]{1,0:T(8,128)(2,1)}, u32[]{:S(2)}, u32[]{:S(2)}) collective-permute-start(bf16[464,1152]{1,0:T(8,128)(2,1)} %fusion.14), channel_id=1, source_target_pairs={{0,4},{4,0},{8,12},{12,8},{16,20},{20,16},{24,28},{28,24},{32,36},... | collective-permute-start | bytes 3207176 | tf_op jit(solution)/shard_map/while/body/eval_jaxpr/ppermute | solution.py:16
  35.8 47.5 %collective-permute-start.2 = (bf16[464,1152]{1,0:T(8,128)(2,1)}, bf16[464,1152]{1,0:T(8,128)(2,1)}, u32[]{:S(2)}, u32[]{:S(2)}) collective-permute-start(bf16[464,1152]{1,0:T(8,128)(2,1)} %fusion.14), channel_id=1, source_target_pairs={{0,8},{4,12},{8,0},{12,4},{16,24},{20,28},{24,16},{28,20},{32,40},... | collective-permute-start | bytes 3207176 | tf_op jit(solution)/shard_map/while/body/eval_jaxpr/ppermute | solution.py:16
  38.3 1.6 copy-start.2
  93.0 11.5 %copy-start.1 = (f32[448,1152]{1,0:T(8,128)S(1)}, f32[448,1152]{1,0:T(8,128)}, u32[]{:S(2)}) copy-start(f32[448,1152]{1,0:T(8,128)} %get-tuple-element.365) | copy-start | bytes 6193156 | tf_op jit(solution)/shard_map/while
  95.5 12.0 %collective-permute-start = (bf16[464,1152]{1,0:T(8,128)(2,1)}, bf16[464,1152]{1,0:T(8,128)(2,1)}, u32[]{:S(2)}, u32[]{:S(2)}) collective-permute-start(bf16[464,1152]{1,0:T(8,128)(2,1)} %fusion.14), channel_id=1, source_target_pairs={{0,1},{1,0},{2,3},{3,2},{4,5},{5,4},{6,7},{7,6},{8,9},{9,8},{10,11... | collective-permute-start | bytes 3207176 | tf_op jit(solution)/shard_map/while/body/eval_jaxpr/ppermute | solution.py:16
  98.2 27.4 %collective-permute-start.1 = (bf16[464,1152]{1,0:T(8,128)(2,1)}, bf16[464,1152]{1,0:T(8,128)(2,1)}, u32[]{:S(2)}, u32[]{:S(2)}) collective-permute-start(bf16[464,1152]{1,0:T(8,128)(2,1)} %fusion.14), channel_id=1, source_target_pairs={{0,4},{4,0},{8,12},{12,8},{16,20},{20,16},{24,28},{28,24},{32,36},... | collective-permute-start | bytes 3207176 | tf_op jit(solution)/shard_map/while/body/eval_jaxpr/ppermute | solution.py:16
  101.0 48.6 %collective-permute-start.2 = (bf16[464,1152]{1,0:T(8,128)(2,1)}, bf16[464,1152]{1,0:T(8,128)(2,1)}, u32[]{:S(2)}, u32[]{:S(2)}) collective-permute-start(bf16[464,1152]{1,0:T(8,128)(2,1)} %fusion.14), channel_id=1, source_target_pairs={{0,8},{4,12},{8,0},{12,4},{16,24},{20,28},{24,16},{28,20},{32,40},... | collective-permute-start | bytes 3207176 | tf_op jit(solution)/shard_map/while/body/eval_jaxpr/ppermute | solution.py:16
  104.5 1.6 copy-start.2
  159.3 37.2 %copy-start.3 = (f32[448,1152]{1,0:T(8,128)S(1)}, f32[448,1152]{1,0:T(8,128)}, u32[]{:S(2)}) copy-start(f32[448,1152]{1,0:T(8,128)} %get-tuple-element.227.txt_in) | copy-start | bytes 6193156

commit v3 on v2

--- a/solution.py
+++ b/solution.py
@@ -9,6 +9,7 @@
 SMEM = pl.BlockSpec(memory_space=pltpu.SMEM)
 DIGIT_ROWS = 16
 CHUNKS = 2
+VMEM_LIMIT = 28 << 20
 
 
 def from_partner(block, axis, bit):
@@ -37,14 +38,15 @@
     return (d[0:1] + 256.0 * d[1:2] + 65536.0 * d[2:3]).astype(jnp.int32)
 
 
-def own_kernel(scalars, bases, img, txt, lab_col, lab_row, img_acc, txt_acc):
+def own_kernel(scalars, bases, img, txt, lab_col, lab_row, img_acc, txt_acc, lab_out):
     count = img.shape[0]
     scale, shift = scalars[0], scalars[1]
     img_acc[...] = gradient(img[...], txt[...], hit_columns(lab_col[...], bases[0], count, count), scale, shift)
     txt_acc[...] = gradient(txt[...], img[...], hit_rows(lab_row[...], bases[0], count, count), scale, shift)
+    lab_out[...] = lab_row[...]
 
 
-def near_kernel(bases, scalars, img, txt, lab_col, near1, near2, near3, img_in, txt_in, img_out, txt_out):
+def near_kernel(bases, scalars, img, txt, lab_col, near1, near2, near3, img_in, txt_in, far_lab, img_out, txt_out):
     count = img.shape[0]
     chunk = (near1.shape[0] - DIGIT_ROWS) // 2
     scale, shift = scalars[0], scalars[1]
@@ -66,11 +68,11 @@
     image_grad[...] = (scale * total).astype(jnp.bfloat16)
 
 
-def far_images_kernel(scalars, bases, txt, packed, txt_in, image_grad, text_grad, image_grad_out):
+def far_images_kernel(scalars, bases, txt, far_img, far_lab, txt_in, image_grad, text_grad, image_grad_out):
     count = txt.shape[0]
     scale, shift = scalars[0], scalars[1]
-    hit = hit_rows(label_row_of(packed[count:, :], count), bases[0], count, count)
-    total = txt_in[...] + gradient(txt[...], packed[:count, :], hit, scale, shift)
+    hit = hit_rows(far_lab[...], bases[0], count, count)
+    total = txt_in[...] + gradient(txt[...], far_img[...], hit, scale, shift)
     text_grad[...] = (scale * total).astype(jnp.bfloat16)
 
 
@@ -89,7 +91,7 @@
     myself = lax.axis_index("dp") * pair_size + lax.axis_index("pair")
 
     anywhere = pl.BlockSpec(memory_space=pl.ANY)
-    params = pltpu.CompilerParams(vmem_limit_bytes=48 << 20)
+    params = pltpu.CompilerParams(vmem_limit_bytes=VMEM_LIMIT)
     acc = jax.ShapeDtypeStruct((count, width), jnp.float32)
     out = jax.ShapeDtypeStruct((count, width), jnp.bfloat16)
 
@@ -116,7 +118,7 @@
     digits = jnp.stack([labels & 255, (labels >> 8) & 255, labels >> 16]).astype(jnp.bfloat16)
     digits = jnp.pad(digits, ((0, DIGIT_ROWS - 3), (0, width - count)))
     far_txt = from_partner(texts, "dp", far)
-    far_img = from_partner(jnp.concatenate([images, digits], axis=0), "dp", far)
+    far_img = from_partner(images, "dp", far)
 
     offsets = jnp.array([0, 1, pair_size, 2 * pair_size, pair_size << far], jnp.int32)
     bases = jnp.bitwise_xor(myself, offsets) * count
@@ -124,7 +126,11 @@
     lab_col = labels.reshape(count, 1)
     lab_row = labels.reshape(1, count)
 
-    sums = kernel(own_kernel, (acc, acc), scalars, bases, images, texts, lab_col, lab_row, products=2)
+    lab = jax.ShapeDtypeStruct((1, count), jnp.int32)
+    *sums, lab_sent = kernel(
+        own_kernel, (acc, acc, lab), scalars, bases, images, texts, lab_col, lab_row, products=2
+    )
+    far_lab = from_partner(lab_sent, "dp", far)
     chunk = count // CHUNKS
 
     def near(step, sums):
@@ -142,13 +148,13 @@
         arrived = [from_partner(part, axis, bit) for axis, bit in (("dp", 1), ("dp", 0), ("pair", 0))]
         here = jnp.concatenate([bases, jnp.reshape(at, (1,))])
         return kernel(
-            near_kernel, (acc, acc), here, scalars, images, texts, lab_col, *arrived[::-1], *sums, products=3
+            near_kernel, (acc, acc), here, scalars, images, texts, lab_col, *arrived[::-1], *sums, far_lab, products=3
         )
 
-    img_acc, txt_acc = lax.fori_loop(0, CHUNKS, near, sums)
+    img_acc, txt_acc = lax.fori_loop(0, CHUNKS, near, tuple(sums))
     image_grad = kernel(far_texts_kernel, out, scalars, bases, images, lab_col, far_txt, img_acc)
     text_grad, image_grad = kernel(
-        far_images_kernel, (out, out), scalars, bases, texts, far_img, txt_acc, image_grad, passed=image_grad
+        far_images_kernel, (out, out), scalars, bases, texts, far_img, far_lab, txt_acc, image_grad, passed=image_grad
     )
     return image_grad, text_grad
 

time: 201 us -> 338 us (1.68)
  the two profiles are of different devices: /device:TPU:37 before, /device:TPU:56 now
where the time goes in v3:
time: 338 us; the launch traced here: 337 us
  waiting for transfers between devices  239 us (71%)
  starting transfers between devices  47 us (14%)
  Pallas kernels  32.3 us (10%)
  local copies, waits for them, and re-layouts  13.5 us (4%)
    ppermute x9, waiting for transfers between devices, from_partner(): return lax.ppermute(block, axis, [(i, i ^ 1 << bit) for i in range(count)])  239 us
    ppermute x9, starting transfers between devices, from_partner(): return lax.ppermute(block, axis, [(i, i ^ 1 << bit) for i in range(count)])  47 us
    pallas_call x5, Pallas kernels, kernel(): pl.pallas_call(body, out_shape=out_shape, in_specs=specs, out_specs=out_s...  32.3 us
    while x16, local copies, waits for them, and re-layouts  8.94 us
  transfers between devices with their start and end apart: 9, of which 5 were waited for; matrix products, arithmetic and copies ran while one was open for 3% of the time, Pallas kernels for 8%

profile of v3, /device:TPU:56, one launch (start us, length us, event | category | flops | bytes accessed | tf_op | source)
XLA Modules:
  0.0 337.5 jit_solution(9556098946799175489)
XLA Ops:
  0.6 14.8 %collective-permute-start.5 = (bf16[448,1152]{1,0:T(8,128)(2,1)}, bf16[448,1152]{1,0:T(8,128)(2,1)}, u32[]{:S(2)}, u32[]{:S(2)}) collective-permute-start(bf16[448,1152]{1,0:T(8,128)(2,1)} %txt.3), channel_id=1, source_target_pairs={{0,256},{4,260},{8,264},{12,268},{16,272},{20,276},{24,280},{28,28... | collective-permute-start | bytes 3096584 | tf_op jit(solution)/shard_map/ppermute | solution.py:17
  15.5 1.9 collective-permute-start.3
  18.7 0.8 copy.9.lab_col
  19.6 0.7 xor_multiply_fusion.1.bases
  20.2 0.1 pad_maximum_fusion.scalars
  20.3 0.0 copy-start.1
  20.3 0.7 copy-done.1
  21.0 0.0 copy-start.5
  21.0 5.6 %own_kernel.1 = (f32[448,1152]{1,0:T(8,128)}, f32[448,1152]{1,0:T(8,128)}, s32[1,448]{1,0:T(1,128)S(1)}) custom-call(f32[2]{0:T(128)S(1)} %pad_maximum_fusion.scalars, s32[5]{0:T(128)S(1)} %xor_multiply_fusion.1.bases, bf16[448,1152]{1,0:T(8,128)(2,1)} %img.3, bf16[448,1152]{1,0:T(8,128)(2,1)} %txt.3, s32[448,1]{1,0:T(8,128)S(1)} %copy.9.lab_col, ...), custom_call_target="tpu_custom_call" | custom-call | flops 1849688064 | bytes 6193152 | tf_op jit(solution)/shard_map/own_kernel/pallas_call | solution.py:107
  26.6 12.6 %collective-permute-start.4 = (s32[1,448]{1,0:T(1,128)S(1)}, s32[1,448]{1,0:T(1,128)S(1)}, u32[]{:S(2)}, u32[]{:S(2)}) collective-permute-start(s32[1,448]{1,0:T(1,128)S(1)} %get-tuple-element.246), channel_id=1, source_target_pairs={{0,256},{4,260},{8,264},{12,268},{16,272},{20,276},{24,280},{28,28... | collective-permute-start | bytes 5384 | tf_op jit(solution)/shard_map/ppermute | solution.py:17
  39.3 154.8 %collective-permute-done.4.far_lab = s32[1,448]{1,0:T(1,128)S(1)} collective-permute-done((s32[1,448]{1,0:T(1,128)S(1)}, s32[1,448]{1,0:T(1,128)S(1)}, u32[]{:S(2)}, u32[]{:S(2)}) %collective-permute-start.4) | collective-permute-done | bytes 1824 | tf_op jit(solution)/shard_map/ppermute | solution.py:17
  194.1 0.0 copy-done.5
  194.1 134.9 %while.18 = (s32[]{:T(128)}, f32[448,1152]{1,0:T(8,128)}, f32[448,1152]{1,0:T(8,128)}, bf16[448,1152]{1,0:T(8,128)(2,1)}, bf16[448,1152]{1,0:T(8,128)(2,1)}, /*i...) while((s32[]{:T(128)}, f32[448,1152]{1,0:T(8,128)}, ...), condition=%wide.region_1.2_spmd.clone, body=%wide.region_0.1_spmd.clone.sunk | while | flops 2778808320 | bytes 59336204 | solution.py:154
  194.1 0.1 constant_dynamic-slice_fusion.5
  194.2 0.0 copy-start.2
  194.2 1.4 constant_dynamic-slice_fusion.6
  195.6 1.1 fusion.14
  196.8 1.9 collective-permute-start
  198.7 3.4 %collective-permute-start.1 = (bf16[464,1152]{1,0:T(8,128)(2,1)}, bf16[464,1152]{1,0:T(8,128)(2,1)}, u32[]{:S(2)}, u32[]{:S(2)}) collective-permute-start(bf16[464,1152]{1,0:T(8,128)(2,1)} %fusion.14), channel_id=1, source_target_pairs={{0,4},{4,0},{8,12},{12,8},{16,20},{20,16},{24,28},{28,24},{32,36},... | collective-permute-start | bytes 3207176 | tf_op jit(solution)/shard_map/while/body/eval_jaxpr/ppermute | solution.py:17
  202.1 4.6 %collective-permute-start.2 = (bf16[464,1152]{1,0:T(8,128)(2,1)}, bf16[464,1152]{1,0:T(8,128)(2,1)}, u32[]{:S(2)}, u32[]{:S(2)}) collective-permute-start(bf16[464,1152]{1,0:T(8,128)(2,1)} %fusion.14), channel_id=1, source_target_pairs={{0,8},{4,12},{8,0},{12,4},{16,24},{20,28},{24,16},{28,20},{32,40},... | collective-permute-start | bytes 3207176 | tf_op jit(solution)/shard_map/while/body/eval_jaxpr/ppermute | solution.py:17
  206.8 0.0 copy-done.2
  206.8 0.0 copy-start.3
  206.8 0.1 copy.26.img_in
  206.9 1.4 copy-done.3
  208.3 1.3 copy.27.txt_in
  209.7 0.1 pad_add_fusion.2.bases
  209.8 0.0 collective-permute-done.near1
  209.8 17.5 %collective-permute-done.1.near2 = bf16[464,1152]{1,0:T(8,128)(2,1)} collective-permute-done((bf16[464,1152]{1,0:T(8,128)(2,1)}, bf16[464,1152]{1,0:T(8,128)(2,1)}, u32[]{:S(2)}, u32[]{:S(2)}) %collective-permute-start.1) | collective-permute-done | bytes 1069088 | tf_op jit(solution)/shard_map/while/body/eval_jaxpr/ppermute | solution.py:17
  227.3 24.7 %collective-permute-done.2.near3 = bf16[464,1152]{1,0:T(8,128)(2,1)} collective-permute-done((bf16[464,1152]{1,0:T(8,128)(2,1)}, bf16[464,1152]{1,0:T(8,128)(2,1)}, u32[]{:S(2)}, u32[]{:S(2)}) %collective-permute-start.2) | collective-permute-done | bytes 1069088 | tf_op jit(solution)/shard_map/while/body/eval_jaxpr/ppermute | solution.py:17
  252.0 0.0 copy-start
  252.0 1.6 copy-done
  253.6 9.1 %near_kernel.8 = (f32[448,1152]{1,0:T(8,128)}, f32[448,1152]{1,0:T(8,128)}) custom-call(s32[6]{0:T(128)S(1)} %pad_add_fusion.2.bases, f32[2]{0:T(128)S(1)} %get-tuple-element.420.scalars, bf16[448,1152]{1,0:T(8,128)(2,1)} %get-tuple-element.418.img, bf16[448,1152]{1,0:T(8,128)(2,1)} %get-tuple-element.417.txt, s32[448,1]{1,0:T(8,128)S(1)} %get-tuple-element.421.lab_col, ...), custom_call_target="tpu_custom_call" | custom-call | flops 2774532096 | bytes 9289728 | tf_op jit(solution)/shard_map/while/body/eval_jaxpr/near_kernel/pallas_call | solution.py:107
  262.7 0.1 constant_dynamic-slice_fusion.5
  262.8 0.0 copy-start.2
  262.8 1.4 constant_dynamic-slice_fusion.6
  264.2 1.1 fusion.14
  265.3 1.9 collective-permute-start
  267.3 2.1 collective-permute-start.1
  269.4 3.6 %collective-permute-start.2 = (bf16[464,1152]{1,0:T(8,128)(2,1)}, bf16[464,1152]{1,0:T(8,128)(2,1)}, u32[]{:S(2)}, u32[]{:S(2)}) collective-permute-start(bf16[464,1152]{1,0:T(8,128)(2,1)} %fusion.14), channel_id=1, source_target_pairs={{0,8},{4,12},{8,0},{12,4},{16,24},{20,28},{24,16},{28,20},{32,40},... | collective-permute-start | bytes 3207176 | tf_op jit(solution)/shard_map/while/body/eval_jaxpr/ppermute | solution.py:17
  273.0 0.0 copy-done.2
  273.0 0.0 copy-start.3
  273.1 0.1 copy.26.img_in
  273.2 1.4 copy-done.3
  274.6 1.3 copy.27.txt_in
  276.0 0.1 pad_add_fusion.2.bases
  276.0 0.0 collective-permute-done.near1
  276.0 19.8 %collective-permute-done.1.near2 = bf16[464,1152]{1,0:T(8,128)(2,1)} collective-permute-done((bf16[464,1152]{1,0:T(8,128)(2,1)}, bf16[464,1152]{1,0:T(8,128)(2,1)}, u32[]{:S(2)}, u32[]{:S(2)}) %collective-permute-start.1) | collective-permute-done | bytes 1069088 | tf_op jit(solution)/shard_map/while/body/eval_jaxpr/ppermute | solution.py:17
  295.9 22.4 %collective-permute-done.2.near3 = bf16[464,1152]{1,0:T(8,128)(2,1)} collective-permute-done((bf16[464,1152]{1,0:T(8,128)(2,1)}, bf16[464,1152]{1,0:T(8,128)(2,1)}, u32[]{:S(2)}, u32[]{:S(2)}) %collective-permute-start.2) | collective-permute-done | bytes 1069088 | tf_op jit(solution)/shard_map/while/body/eval_jaxpr/ppermute | solution.py:17
  318.3 0.0 copy-start
  318.3 1.6 copy-done
  319.9 9.1 %near_kernel.8 = (f32[448,1152]{1,0:T(8,128)}, f32[448,1152]{1,0:T(8,128)}) custom-call(s32[6]{0:T(128)S(1)} %pad_add_fusion.2.bases, f32[2]{0:T(128)S(1)} %get-tuple-element.420.scalars, bf16[448,1152]{1,0:T(8,128)(2,1)} %get-tuple-element.418.img, bf16[448,1152]{1,0:T(8,128)(2,1)} %get-tuple-element.417.txt, s32[448,1]{1,0:T(8,128)S(1)} %get-tuple-element.421.lab_col, ...), custom_call_target="tpu_custom_call" | custom-call | flops 2774532096 | bytes 9289728 | tf_op jit(solution)/shard_map/while/body/eval_jaxpr/near_kernel/pallas_call | solution.py:107
  329.0 0.0 collective-permute-done.5.far_txt
  329.0 0.0 copy-start.4
  329.0 4.8 %far_texts_kernel.1.image_grad = bf16[448,1152]{1,0:T(8,128)(2,1)} custom-call(f32[2]{0:T(128)S(1)} %get-tuple-element.435, s32[5]{0:T(128)S(1)} %xor_multiply_fusion.1.bases, bf16[448,1152]{1,0:T(8,128)(2,1)} %img.3, s32[448,1]{1,0:T(8,128)S(1)} %get-tuple-element.432, bf16[448,1152]{1,0:T(8,128)(2,1)} %collective-permute-done.5.far_txt, ...), custom_call_target="tpu_custom_call" | custom-call | flops 924844032 | bytes 3096576 | tf_op jit(solution)/shard_map/far_texts_kernel/pallas_call | solution.py:107
  333.8 0.0 collective-permute-done.3.far_img
  333.8 0.0 copy-done.4
  333.8 3.7 %far_images_kernel.1 = (bf16[448,1152]{1,0:T(8,128)(2,1)}, bf16[448,1152]{1,0:T(8,128)(2,1)}) custom-call(f32[2]{0:T(128)S(1)} %get-tuple-element.435, s32[5]{0:T(128)S(1)} %xor_multiply_fusion.1.bases, bf16[448,1152]{1,0:T(8,128)(2,1)} %txt.3, bf16[448,1152]{1,0:T(8,128)(2,1)S(1)} %collective-permute-done.3.far_img, ...), custom_call_target="tpu_custom_call", output_to_operand_aliasing={{1}: (6, {})} | custom-call | flops 924844032 | bytes 3096576 | tf_op jit(solution)/shard_map/far_images_kernel/pallas_call | solution.py:107
  (7 shorter events, 0.0 us)
Async XLA Ops:
  0.6 328.3 %collective-permute-start.5 = (bf16[448,1152]{1,0:T(8,128)(2,1)}, bf16[448,1152]{1,0:T(8,128)(2,1)}, u32[]{:S(2)}, u32[]{:S(2)}) collective-permute-start(bf16[448,1152]{1,0:T(8,128)(2,1)} %txt.3), channel_id=1, source_target_pairs={{0,256},{4,260},{8,264},{12,268},{16,272},{20,276},{24,280},{28,28... | collective-permute-start | bytes 3096584 | tf_op jit(solution)/shard_map/ppermute | solution.py:17
  15.5 318.3 %collective-permute-start.3 = (bf16[448,1152]{1,0:T(8,128)(2,1)}, bf16[448,1152]{1,0:T(8,128)(2,1)S(1)}, u32[]{:S(2)}, u32[]{:S(2)}) collective-permute-start(bf16[448,1152]{1,0:T(8,128)(2,1)} %img.3), channel_id=1, source_target_pairs={{0,256},{4,260},{8,264},{12,268},{16,272},{20,276},{24,280},{28,28... | collective-permute-start | bytes 3096584 | tf_op jit(solution)/shard_map/ppermute | solution.py:17
  20.3 0.7 copy-start.1
  21.0 173.1 %copy-start.5 = (s32[5]{0:T(128)S(1)}, s32[5]{0:T(128)}, u32[]{:S(2)}) copy-start(s32[5]{0:T(128)} %constant.78.clone.5) | copy-start | bytes 64
  26.6 167.5 %collective-permute-start.4 = (s32[1,448]{1,0:T(1,128)S(1)}, s32[1,448]{1,0:T(1,128)S(1)}, u32[]{:S(2)}, u32[]{:S(2)}) collective-permute-start(s32[1,448]{1,0:T(1,128)S(1)} %get-tuple-element.246), channel_id=1, source_target_pairs={{0,256},{4,260},{8,264},{12,268},{16,272},{20,276},{24,280},{28,28... | collective-permute-start | bytes 5384 | tf_op jit(solution)/shard_map/ppermute | solution.py:17
  194.2 12.5 %copy-start.2 = (f32[448,1152]{1,0:T(8,128)S(1)}, f32[448,1152]{1,0:T(8,128)}, u32[]{:S(2)}) copy-start(f32[448,1152]{1,0:T(8,128)} %get-tuple-element.399) | copy-start | bytes 6193156 | tf_op jit(solution)/shard_map/while
  196.8 13.0 %collective-permute-start = (bf16[464,1152]{1,0:T(8,128)(2,1)}, bf16[464,1152]{1,0:T(8,128)(2,1)}, u32[]{:S(2)}, u32[]{:S(2)}) collective-permute-start(bf16[464,1152]{1,0:T(8,128)(2,1)} %fusion.14), channel_id=1, source_target_pairs={{0,1},{1,0},{2,3},{3,2},{4,5},{5,4},{6,7},{7,6},{8,9},{9,8},{10,11... | collective-permute-start | bytes 3207176 | tf_op jit(solution)/shard_map/while/body/eval_jaxpr/ppermute | solution.py:17
  198.7 28.6 %collective-permute-start.1 = (bf16[464,1152]{1,0:T(8,128)(2,1)}, bf16[464,1152]{1,0:T(8,128)(2,1)}, u32[]{:S(2)}, u32[]{:S(2)}) collective-permute-start(bf16[464,1152]{1,0:T(8,128)(2,1)} %fusion.14), channel_id=1, source_target_pairs={{0,4},{4,0},{8,12},{12,8},{16,20},{20,16},{24,28},{28,24},{32,36},... | collective-permute-start | bytes 3207176 | tf_op jit(solution)/shard_map/while/body/eval_jaxpr/ppermute | solution.py:17
  202.1 49.9 %collective-permute-start.2 = (bf16[464,1152]{1,0:T(8,128)(2,1)}, bf16[464,1152]{1,0:T(8,128)(2,1)}, u32[]{:S(2)}, u32[]{:S(2)}) collective-permute-start(bf16[464,1152]{1,0:T(8,128)(2,1)} %fusion.14), channel_id=1, source_target_pairs={{0,8},{4,12},{8,0},{12,4},{16,24},{20,28},{24,16},{28,20},{32,40},... | collective-permute-start | bytes 3207176 | tf_op jit(solution)/shard_map/while/body/eval_jaxpr/ppermute | solution.py:17
  206.8 1.6 copy-start.3
  252.0 1.6 copy-start
  262.8 10.3 %copy-start.2 = (f32[448,1152]{1,0:T(8,128)S(1)}, f32[448,1152]{1,0:T(8,128)}, u32[]{:S(2)}) copy-start(f32[448,1152]{1,0:T(8,128)} %get-tuple-element.399) | copy-start | bytes 6193156 | tf_op jit(solution)/shard_map/while
  265.3 10.7 %collective-permute-start = (bf16[464,1152]{1,0:T(8,128)(2,1)}, bf16[464,1152]{1,0:T(8,128)(2,1)}, u32[]{:S(2)}, u32[]{:S(2)}) collective-permute-start(bf16[464,1152]{1,0:T(8,128)(2,1)} %fusion.14), channel_id=1, source_target_pairs={{0,1},{1,0},{2,3},{3,2},{4,5},{5,4},{6,7},{7,6},{8,9},{9,8},{10,11... | collective-permute-start | bytes 3207176 | tf_op jit(solution)/shard_map/while/body/eval_jaxpr/ppermute | solution.py:17
  267.3 28.6 %collective-permute-start.1 = (bf16[464,1152]{1,0:T(8,128)(2,1)}, bf16[464,1152]{1,0:T(8,128)(2,1)}, u32[]{:S(2)}, u32[]{:S(2)}) collective-permute-start(bf16[464,1152]{1,0:T(8,128)(2,1)} %fusion.14), channel_id=1, source_target_pairs={{0,4},{4,0},{8,12},{12,8},{16,20},{20,16},{24,28},{28,24},{32,36},... | collective-permute-start | bytes 3207176 | tf_op jit(solution)/shard_map/while/body/eval_jaxpr/ppermute | solution.py:17
  269.4 48.9 %collective-permute-start.2 = (bf16[464,1152]{1,0:T(8,128)(2,1)}, bf16[464,1152]{1,0:T(8,128)(2,1)}, u32[]{:S(2)}, u32[]{:S(2)}) collective-permute-start(bf16[464,1152]{1,0:T(8,128)(2,1)} %fusion.14), channel_id=1, source_target_pairs={{0,8},{4,12},{8,0},{12,4},{16,24},{20,28},{24,16},{28,20},{32,40},... | collective-permute-start | bytes 3207176 | tf_op jit(solution)/shard_map/while/body/eval_jaxpr/ppermute | solution.py:17
  273.0 1.6 copy-start.3
  318.3 1.6 copy-start
  329.0 4.8 %copy-start.4 = (f32[448,1152]{1,0:T(8,128)S(1)}, f32[448,1152]{1,0:T(8,128)}, u32[]{:S(2)}) copy-start(f32[448,1152]{1,0:T(8,128)} %get-tuple-element.249.txt_in) | copy-start | bytes 6193156

commit v4 on v3

--- a/solution.py
+++ b/solution.py
@@ -46,7 +46,7 @@
     lab_out[...] = lab_row[...]
 
 
-def near_kernel(bases, scalars, img, txt, lab_col, near1, near2, near3, img_in, txt_in, far_lab, img_out, txt_out):
+def near_kernel(bases, scalars, img, txt, lab_col, near1, near2, near3, img_in, txt_in, img_out, txt_out):
     count = img.shape[0]
     chunk = (near1.shape[0] - DIGIT_ROWS) // 2
     scale, shift = scalars[0], scalars[1]
@@ -148,7 +148,7 @@
         arrived = [from_partner(part, axis, bit) for axis, bit in (("dp", 1), ("dp", 0), ("pair", 0))]
         here = jnp.concatenate([bases, jnp.reshape(at, (1,))])
         return kernel(
-            near_kernel, (acc, acc), here, scalars, images, texts, lab_col, *arrived[::-1], *sums, far_lab, products=3
+            near_kernel, (acc, acc), here, scalars, images, texts, lab_col, *arrived[::-1], *sums, products=3
         )
 
     img_acc, txt_acc = lax.fori_loop(0, CHUNKS, near, tuple(sums))

time: 338 us -> 199 us (0.59)
  the two profiles are of different devices: /device:TPU:56 before, /device:TPU:40 now
where the time goes in v4:
time: 199 us; the launch traced here: 198 us
  waiting for transfers between devices  99 us (50%)
  starting transfers between devices  47 us (24%)
  Pallas kernels  32.4 us (16%)
  local copies, waits for them, and re-layouts  13.5 us (7%)
  other arithmetic  3.9 us (2%)
  between operations  2.06 us (1%)
    ppermute x9, waiting for transfers between devices, from_partner(): return lax.ppermute(block, axis, [(i, i ^ 1 << bit) for i in range(count)])  99 us
    ppermute x9, starting transfers between devices, from_partner(): return lax.ppermute(block, axis, [(i, i ^ 1 << bit) for i in range(count)])  47 us
    pallas_call x5, Pallas kernels, kernel(): pl.pallas_call(body, out_shape=out_shape, in_specs=specs, out_specs=out_s...  32.4 us
    while x16, local copies, waits for them, and re-layouts  8.94 us
  transfers between devices with their start and end apart: 9, of which 5 were waited for; matrix products, arithmetic and copies ran while one was open for 5% of the time, Pallas kernels for 14%

profile of v4, /device:TPU:40, one launch (start us, length us, event | category | flops | bytes accessed | tf_op | source)
XLA Modules:
  0.0 197.8 jit_solution(9821452696107231517)
XLA Ops:
  0.6 14.8 %collective-permute-start.5 = (bf16[448,1152]{1,0:T(8,128)(2,1)}, bf16[448,1152]{1,0:T(8,128)(2,1)}, u32[]{:S(2)}, u32[]{:S(2)}) collective-permute-start(bf16[448,1152]{1,0:T(8,128)(2,1)} %txt.3), channel_id=1, source_target_pairs={{0,256},{4,260},{8,264},{12,268},{16,272},{20,276},{24,280},{28,28... | collective-permute-start | bytes 3096584 | tf_op jit(solution)/shard_map/ppermute | solution.py:17
  15.5 1.9 collective-permute-start.3
  18.7 0.7 and_convert_fusion.1
  19.4 0.8 copy.9.lab_col
  20.3 0.7 xor_multiply_fusion.1.bases
  20.9 0.1 pad_maximum_fusion.scalars
  21.0 0.0 copy-start.1
  21.1 0.7 copy-done.1
  21.7 0.0 copy-start.5
  21.7 5.7 %own_kernel.1 = (f32[448,1152]{1,0:T(8,128)}, f32[448,1152]{1,0:T(8,128)}, s32[1,448]{1,0:T(1,128)S(1)}) custom-call(f32[2]{0:T(128)S(1)} %pad_maximum_fusion.scalars, s32[5]{0:T(128)S(1)} %xor_multiply_fusion.1.bases, bf16[448,1152]{1,0:T(8,128)(2,1)} %img.3, bf16[448,1152]{1,0:T(8,128)(2,1)} %txt.3, s32[448,1]{1,0:T(8,128)S(1)} %copy.9.lab_col, ...), custom_call_target="tpu_custom_call" | custom-call | flops 1849688064 | bytes 6193152 | tf_op jit(solution)/shard_map/own_kernel/pallas_call | solution.py:107
  27.4 0.0 copy-done.5
  27.4 134.9 %while.18 = (s32[]{:T(128)}, f32[448,1152]{1,0:T(8,128)}, f32[448,1152]{1,0:T(8,128)}, bf16[448,1152]{1,0:T(8,128)(2,1)}, bf16[448,1152]{1,0:T(8,128)(2,1)}, /*i...) while((s32[]{:T(128)}, f32[448,1152]{1,0:T(8,128)}, ...), condition=%wide.region_1.2_spmd.clone, body=%wide.region_0.1_spmd.clone.sunk | while | flops 2778808320 | bytes 59336196 | solution.py:154
  27.4 0.1 constant_dynamic-slice_fusion.5
  27.5 0.0 copy-start.2
  27.5 1.4 constant_dynamic-slice_fusion.6
  28.9 1.1 fusion.14
  30.0 1.9 collective-permute-start
  32.0 3.4 %collective-permute-start.1 = (bf16[464,1152]{1,0:T(8,128)(2,1)}, bf16[464,1152]{1,0:T(8,128)(2,1)}, u32[]{:S(2)}, u32[]{:S(2)}) collective-permute-start(bf16[464,1152]{1,0:T(8,128)(2,1)} %fusion.14), channel_id=1, source_target_pairs={{0,4},{4,0},{8,12},{12,8},{16,20},{20,16},{24,28},{28,24},{32,36},... | collective-permute-start | bytes 3207176 | tf_op jit(solution)/shard_map/while/body/eval_jaxpr/ppermute | solution.py:17
  35.4 4.6 %collective-permute-start.2 = (bf16[464,1152]{1,0:T(8,128)(2,1)}, bf16[464,1152]{1,0:T(8,128)(2,1)}, u32[]{:S(2)}, u32[]{:S(2)}) collective-permute-start(bf16[464,1152]{1,0:T(8,128)(2,1)} %fusion.14), channel_id=1, source_target_pairs={{0,8},{4,12},{8,0},{12,4},{16,24},{20,28},{24,16},{28,20},{32,40},... | collective-permute-start | bytes 3207176 | tf_op jit(solution)/shard_map/while/body/eval_jaxpr/ppermute | solution.py:17
  40.0 0.0 copy-done.2
  40.0 0.0 copy-start.3
  40.0 0.1 copy.26.img_in
  40.2 1.4 copy-done.3
  41.6 1.3 copy.27.txt_in
  42.9 0.1 pad_add_fusion.2.bases
  43.0 0.0 collective-permute-done.near1
  43.0 17.6 %collective-permute-done.1.near2 = bf16[464,1152]{1,0:T(8,128)(2,1)} collective-permute-done((bf16[464,1152]{1,0:T(8,128)(2,1)}, bf16[464,1152]{1,0:T(8,128)(2,1)}, u32[]{:S(2)}, u32[]{:S(2)}) %collective-permute-start.1) | collective-permute-done | bytes 1069088 | tf_op jit(solution)/shard_map/while/body/eval_jaxpr/ppermute | solution.py:17
  60.6 24.7 %collective-permute-done.2.near3 = bf16[464,1152]{1,0:T(8,128)(2,1)} collective-permute-done((bf16[464,1152]{1,0:T(8,128)(2,1)}, bf16[464,1152]{1,0:T(8,128)(2,1)}, u32[]{:S(2)}, u32[]{:S(2)}) %collective-permute-start.2) | collective-permute-done | bytes 1069088 | tf_op jit(solution)/shard_map/while/body/eval_jaxpr/ppermute | solution.py:17
  85.3 0.0 copy-start
  85.3 1.6 copy-done
  86.8 9.1 %near_kernel.8 = (f32[448,1152]{1,0:T(8,128)}, f32[448,1152]{1,0:T(8,128)}) custom-call(s32[6]{0:T(128)S(1)} %pad_add_fusion.2.bases, f32[2]{0:T(128)S(1)} %get-tuple-element.387.scalars, bf16[448,1152]{1,0:T(8,128)(2,1)} %get-tuple-element.385.img, bf16[448,1152]{1,0:T(8,128)(2,1)} %get-tuple-element.384.txt, s32[448,1]{1,0:T(8,128)S(1)} %get-tuple-element.388.lab_col, ...), custom_call_target="tpu_custom_call" | custom-call | flops 2774532096 | bytes 9289728 | tf_op jit(solution)/shard_map/while/body/eval_jaxpr/near_kernel/pallas_call | solution.py:107
  96.0 0.1 constant_dynamic-slice_fusion.5
  96.0 0.0 copy-start.2
  96.0 1.4 constant_dynamic-slice_fusion.6
  97.5 1.1 fusion.14
  98.6 1.9 collective-permute-start
  100.5 2.1 %collective-permute-start.1 = (bf16[464,1152]{1,0:T(8,128)(2,1)}, bf16[464,1152]{1,0:T(8,128)(2,1)}, u32[]{:S(2)}, u32[]{:S(2)}) collective-permute-start(bf16[464,1152]{1,0:T(8,128)(2,1)} %fusion.14), channel_id=1, source_target_pairs={{0,4},{4,0},{8,12},{12,8},{16,20},{20,16},{24,28},{28,24},{32,36},... | collective-permute-start | bytes 3207176 | tf_op jit(solution)/shard_map/while/body/eval_jaxpr/ppermute | solution.py:17
  102.7 3.6 %collective-permute-start.2 = (bf16[464,1152]{1,0:T(8,128)(2,1)}, bf16[464,1152]{1,0:T(8,128)(2,1)}, u32[]{:S(2)}, u32[]{:S(2)}) collective-permute-start(bf16[464,1152]{1,0:T(8,128)(2,1)} %fusion.14), channel_id=1, source_target_pairs={{0,8},{4,12},{8,0},{12,4},{16,24},{20,28},{24,16},{28,20},{32,40},... | collective-permute-start | bytes 3207176 | tf_op jit(solution)/shard_map/while/body/eval_jaxpr/ppermute | solution.py:17
  106.3 0.0 copy-done.2
  106.3 0.0 copy-start.3
  106.3 0.1 copy.26.img_in
  106.5 1.4 copy-done.3
  107.9 1.3 copy.27.txt_in
  109.2 0.1 pad_add_fusion.2.bases
  109.3 0.0 collective-permute-done.near1
  109.3 19.8 %collective-permute-done.1.near2 = bf16[464,1152]{1,0:T(8,128)(2,1)} collective-permute-done((bf16[464,1152]{1,0:T(8,128)(2,1)}, bf16[464,1152]{1,0:T(8,128)(2,1)}, u32[]{:S(2)}, u32[]{:S(2)}) %collective-permute-start.1) | collective-permute-done | bytes 1069088 | tf_op jit(solution)/shard_map/while/body/eval_jaxpr/ppermute | solution.py:17
  129.1 22.4 %collective-permute-done.2.near3 = bf16[464,1152]{1,0:T(8,128)(2,1)} collective-permute-done((bf16[464,1152]{1,0:T(8,128)(2,1)}, bf16[464,1152]{1,0:T(8,128)(2,1)}, u32[]{:S(2)}, u32[]{:S(2)}) %collective-permute-start.2) | collective-permute-done | bytes 1069088 | tf_op jit(solution)/shard_map/while/body/eval_jaxpr/ppermute | solution.py:17
  151.6 0.0 copy-start
  151.6 1.6 copy-done
  153.1 9.1 %near_kernel.8 = (f32[448,1152]{1,0:T(8,128)}, f32[448,1152]{1,0:T(8,128)}) custom-call(s32[6]{0:T(128)S(1)} %pad_add_fusion.2.bases, f32[2]{0:T(128)S(1)} %get-tuple-element.387.scalars, bf16[448,1152]{1,0:T(8,128)(2,1)} %get-tuple-element.385.img, bf16[448,1152]{1,0:T(8,128)(2,1)} %get-tuple-element.384.txt, s32[448,1]{1,0:T(8,128)S(1)} %get-tuple-element.388.lab_col, ...), custom_call_target="tpu_custom_call" | custom-call | flops 2774532096 | bytes 9289728 | tf_op jit(solution)/shard_map/while/body/eval_jaxpr/near_kernel/pallas_call | solution.py:107
  162.3 12.6 %collective-permute-start.4 = (s32[1,448]{1,0:T(1,128)S(1)}, s32[1,448]{1,0:T(1,128)S(1)}, u32[]{:S(2)}, u32[]{:S(2)}) collective-permute-start(s32[1,448]{1,0:T(1,128)S(1)} %get-tuple-element.226), channel_id=1, source_target_pairs={{0,256},{4,260},{8,264},{12,268},{16,272},{20,276},{24,280},{28,28... | collective-permute-start | bytes 5384 | tf_op jit(solution)/shard_map/ppermute | solution.py:17
  174.9 0.0 collective-permute-done.5.far_txt
  174.9 0.0 copy-start.4
  174.9 4.8 %far_texts_kernel.1.image_grad = bf16[448,1152]{1,0:T(8,128)(2,1)} custom-call(f32[2]{0:T(128)S(1)} %get-tuple-element.400, s32[5]{0:T(128)S(1)} %xor_multiply_fusion.1.bases, bf16[448,1152]{1,0:T(8,128)(2,1)} %img.3, s32[448,1]{1,0:T(8,128)S(1)} %get-tuple-element.399, bf16[448,1152]{1,0:T(8,128)(2,1)} %collective-permute-done.5.far_txt, ...), custom_call_target="tpu_custom_call" | custom-call | flops 924844032 | bytes 3096576 | tf_op jit(solution)/shard_map/far_texts_kernel/pallas_call | solution.py:107
  179.7 14.4 %collective-permute-done.4.far_lab = s32[1,448]{1,0:T(1,128)S(1)} collective-permute-done((s32[1,448]{1,0:T(1,128)S(1)}, s32[1,448]{1,0:T(1,128)S(1)}, u32[]{:S(2)}, u32[]{:S(2)}) %collective-permute-start.4) | collective-permute-done | bytes 1824 | tf_op jit(solution)/shard_map/ppermute | solution.py:17
  194.1 0.0 collective-permute-done.3.far_img
  194.1 0.0 copy-done.4
  194.1 3.7 %far_images_kernel.1 = (bf16[448,1152]{1,0:T(8,128)(2,1)}, bf16[448,1152]{1,0:T(8,128)(2,1)}) custom-call(f32[2]{0:T(128)S(1)} %get-tuple-element.400, s32[5]{0:T(128)S(1)} %xor_multiply_fusion.1.bases, bf16[448,1152]{1,0:T(8,128)(2,1)} %txt.3, bf16[448,1152]{1,0:T(8,128)(2,1)S(1)} %collective-permute-done.3.far_img, ...), custom_call_target="tpu_custom_call", output_to_operand_aliasing={{1}: (6, {})} | custom-call | flops 924844032 | bytes 3096576 | tf_op jit(solution)/shard_map/far_images_kernel/pallas_call | solution.py:107
  (6 shorter events, 0.0 us)
Async XLA Ops:
  0.6 174.2 %collective-permute-start.5 = (bf16[448,1152]{1,0:T(8,128)(2,1)}, bf16[448,1152]{1,0:T(8,128)(2,1)}, u32[]{:S(2)}, u32[]{:S(2)}) collective-permute-start(bf16[448,1152]{1,0:T(8,128)(2,1)} %txt.3), channel_id=1, source_target_pairs={{0,256},{4,260},{8,264},{12,268},{16,272},{20,276},{24,280},{28,28... | collective-permute-start | bytes 3096584 | tf_op jit(solution)/shard_map/ppermute | solution.py:17
  15.5 178.7 %collective-permute-start.3 = (bf16[448,1152]{1,0:T(8,128)(2,1)}, bf16[448,1152]{1,0:T(8,128)(2,1)S(1)}, u32[]{:S(2)}, u32[]{:S(2)}) collective-permute-start(bf16[448,1152]{1,0:T(8,128)(2,1)} %img.3), channel_id=1, source_target_pairs={{0,256},{4,260},{8,264},{12,268},{16,272},{20,276},{24,280},{28,28... | collective-permute-start | bytes 3096584 | tf_op jit(solution)/shard_map/ppermute | solution.py:17
  21.0 0.7 copy-start.1
  21.7 5.7 %copy-start.5 = (s32[5]{0:T(128)S(1)}, s32[5]{0:T(128)}, u32[]{:S(2)}) copy-start(s32[5]{0:T(128)} %constant.78.clone.5) | copy-start | bytes 64
  27.5 12.5 %copy-start.2 = (f32[448,1152]{1,0:T(8,128)S(1)}, f32[448,1152]{1,0:T(8,128)}, u32[]{:S(2)}) copy-start(f32[448,1152]{1,0:T(8,128)} %get-tuple-element.367) | copy-start | bytes 6193156 | tf_op jit(solution)/shard_map/while
  30.0 13.0 %collective-permute-start = (bf16[464,1152]{1,0:T(8,128)(2,1)}, bf16[464,1152]{1,0:T(8,128)(2,1)}, u32[]{:S(2)}, u32[]{:S(2)}) collective-permute-start(bf16[464,1152]{1,0:T(8,128)(2,1)} %fusion.14), channel_id=1, source_target_pairs={{0,1},{1,0},{2,3},{3,2},{4,5},{5,4},{6,7},{7,6},{8,9},{9,8},{10,11... | collective-permute-start | bytes 3207176 | tf_op jit(solution)/shard_map/while/body/eval_jaxpr/ppermute | solution.py:17
  32.0 28.6 %collective-permute-start.1 = (bf16[464,1152]{1,0:T(8,128)(2,1)}, bf16[464,1152]{1,0:T(8,128)(2,1)}, u32[]{:S(2)}, u32[]{:S(2)}) collective-permute-start(bf16[464,1152]{1,0:T(8,128)(2,1)} %fusion.14), channel_id=1, source_target_pairs={{0,4},{4,0},{8,12},{12,8},{16,20},{20,16},{24,28},{28,24},{32,36},... | collective-permute-start | bytes 3207176 | tf_op jit(solution)/shard_map/while/body/eval_jaxpr/ppermute | solution.py:17
  35.4 49.9 %collective-permute-start.2 = (bf16[464,1152]{1,0:T(8,128)(2,1)}, bf16[464,1152]{1,0:T(8,128)(2,1)}, u32[]{:S(2)}, u32[]{:S(2)}) collective-permute-start(bf16[464,1152]{1,0:T(8,128)(2,1)} %fusion.14), channel_id=1, source_target_pairs={{0,8},{4,12},{8,0},{12,4},{16,24},{20,28},{24,16},{28,20},{32,40},... | collective-permute-start | bytes 3207176 | tf_op jit(solution)/shard_map/while/body/eval_jaxpr/ppermute | solution.py:17
  40.0 1.6 copy-start.3
  85.3 1.6 copy-start
  96.0 10.3 %copy-start.2 = (f32[448,1152]{1,0:T(8,128)S(1)}, f32[448,1152]{1,0:T(8,128)}, u32[]{:S(2)}) copy-start(f32[448,1152]{1,0:T(8,128)} %get-tuple-element.367) | copy-start | bytes 6193156 | tf_op jit(solution)/shard_map/while
  98.6 10.7 %collective-permute-start = (bf16[464,1152]{1,0:T(8,128)(2,1)}, bf16[464,1152]{1,0:T(8,128)(2,1)}, u32[]{:S(2)}, u32[]{:S(2)}) collective-permute-start(bf16[464,1152]{1,0:T(8,128)(2,1)} %fusion.14), channel_id=1, source_target_pairs={{0,1},{1,0},{2,3},{3,2},{4,5},{5,4},{6,7},{7,6},{8,9},{9,8},{10,11... | collective-permute-start | bytes 3207176 | tf_op jit(solution)/shard_map/while/body/eval_jaxpr/ppermute | solution.py:17
  100.5 28.6 %collective-permute-start.1 = (bf16[464,1152]{1,0:T(8,128)(2,1)}, bf16[464,1152]{1,0:T(8,128)(2,1)}, u32[]{:S(2)}, u32[]{:S(2)}) collective-permute-start(bf16[464,1152]{1,0:T(8,128)(2,1)} %fusion.14), channel_id=1, source_target_pairs={{0,4},{4,0},{8,12},{12,8},{16,20},{20,16},{24,28},{28,24},{32,36},... | collective-permute-start | bytes 3207176 | tf_op jit(solution)/shard_map/while/body/eval_jaxpr/ppermute | solution.py:17
  102.7 48.9 %collective-permute-start.2 = (bf16[464,1152]{1,0:T(8,128)(2,1)}, bf16[464,1152]{1,0:T(8,128)(2,1)}, u32[]{:S(2)}, u32[]{:S(2)}) collective-permute-start(bf16[464,1152]{1,0:T(8,128)(2,1)} %fusion.14), channel_id=1, source_target_pairs={{0,8},{4,12},{8,0},{12,4},{16,24},{20,28},{24,16},{28,20},{32,40},... | collective-permute-start | bytes 3207176 | tf_op jit(solution)/shard_map/while/body/eval_jaxpr/ppermute | solution.py:17
  106.3 1.6 copy-start.3
  151.6 1.6 copy-start
  162.3 31.9 %collective-permute-start.4 = (s32[1,448]{1,0:T(1,128)S(1)}, s32[1,448]{1,0:T(1,128)S(1)}, u32[]{:S(2)}, u32[]{:S(2)}) collective-permute-start(s32[1,448]{1,0:T(1,128)S(1)} %get-tuple-element.226), channel_id=1, source_target_pairs={{0,256},{4,260},{8,264},{12,268},{16,272},{20,276},{24,280},{28,28... | collective-permute-start | bytes 5384 | tf_op jit(solution)/shard_map/ppermute | solution.py:17
  174.9 19.2 %copy-start.4 = (f32[448,1152]{1,0:T(8,128)S(1)}, f32[448,1152]{1,0:T(8,128)}, u32[]{:S(2)}) copy-start(f32[448,1152]{1,0:T(8,128)} %get-tuple-element.229.txt_in) | copy-start | bytes 6193156

commit v5 on v4

--- a/solution.py
+++ b/solution.py
@@ -9,12 +9,23 @@
 SMEM = pl.BlockSpec(memory_space=pltpu.SMEM)
 DIGIT_ROWS = 16
 CHUNKS = 2
+RING = 16
+FIRST_STEPS = 1
 VMEM_LIMIT = 28 << 20
 
 
 def from_partner(block, axis, bit):
     count = lax.axis_size(axis)
     return lax.ppermute(block, axis, [(i, i ^ (1 << bit)) for i in range(count)])
+
+
+def along_ring(block, steps):
+    axes = ("dp", "pair")
+    count = lax.axis_size(axes)
+    step = count // RING * steps
+    return lax.ppermute(
+        block, axes, [(i, (i + (step if i % 2 == 0 else -step)) % count) for i in range(count)]
+    )
 
 
 def gradient(rows, cols, hit, scale, shift):
@@ -38,24 +49,25 @@
     return (d[0:1] + 256.0 * d[1:2] + 65536.0 * d[2:3]).astype(jnp.int32)
 
 
-def own_kernel(scalars, bases, img, txt, lab_col, lab_row, img_acc, txt_acc, lab_out):
-    count = img.shape[0]
-    scale, shift = scalars[0], scalars[1]
-    img_acc[...] = gradient(img[...], txt[...], hit_columns(lab_col[...], bases[0], count, count), scale, shift)
-    txt_acc[...] = gradient(txt[...], img[...], hit_rows(lab_row[...], bases[0], count, count), scale, shift)
-    lab_out[...] = lab_row[...]
+def own_kernel(bases, scalars, img, txt, lab_col, part, img_in, txt_in, img_out, txt_out):
+    add_meetings(((0, part),), bases, scalars, img, txt, lab_col, img_in, txt_in, img_out, txt_out)
 
 
 def near_kernel(bases, scalars, img, txt, lab_col, near1, near2, near3, img_in, txt_in, img_out, txt_out):
+    nears = ((1, near1), (2, near2), (3, near3))
+    add_meetings(nears, bases, scalars, img, txt, lab_col, img_in, txt_in, img_out, txt_out)
+
+
+def add_meetings(parts, bases, scalars, img, txt, lab_col, img_in, txt_in, img_out, txt_out):
     count = img.shape[0]
-    chunk = (near1.shape[0] - DIGIT_ROWS) // 2
+    chunk = (parts[0][1].shape[0] - DIGIT_ROWS) // 2
     scale, shift = scalars[0], scalars[1]
     img_total, txt_total = img_in[...], txt_in[...]
-    for which, near in ((1, near1), (2, near2), (3, near3)):
+    for which, part in parts:
         hit = hit_columns(lab_col[...], bases[which] + bases[5], count, chunk)
-        img_total += gradient(img[...], near[:chunk, :], hit, scale, shift)
-        hit = hit_rows(label_row_of(near[2 * chunk :, :], chunk), bases[0], count, chunk)
-        txt_total += gradient(txt[...], near[chunk : 2 * chunk, :], hit, scale, shift)
+        img_total += gradient(img[...], part[:chunk, :], hit, scale, shift)
+        hit = hit_rows(label_row_of(part[2 * chunk :, :], chunk), bases[0], count, chunk)
+        txt_total += gradient(txt[...], part[chunk : 2 * chunk, :], hit, scale, shift)
     img_out[...] = img_total
     txt_out[...] = txt_total
 
@@ -95,15 +107,14 @@
     acc = jax.ShapeDtypeStruct((count, width), jnp.float32)
     out = jax.ShapeDtypeStruct((count, width), jnp.bfloat16)
 
-    def kernel(body, out_shape, *args, passed=None, products=1):
+    def kernel(body, out_shape, *args, passed=0, products=1):
         many = isinstance(out_shape, tuple)
         specs = [SMEM, SMEM] + [VMEM] * (len(args) - 2)
         out_specs = (VMEM,) * len(out_shape) if many else VMEM
-        aliases = {}
-        if passed is not None:
+        aliases = {len(args) - i: len(out_shape) - i for i in range(1, passed + 1)}
+        if products == 0:
             specs[-1] = anywhere
             out_specs = out_specs[:-1] + (anywhere,)
-            aliases = {len(args) - 1: len(out_shape) - 1}
         return pl.pallas_call(
             body,
             out_shape=out_shape,
@@ -117,20 +128,16 @@
 
     digits = jnp.stack([labels & 255, (labels >> 8) & 255, labels >> 16]).astype(jnp.bfloat16)
     digits = jnp.pad(digits, ((0, DIGIT_ROWS - 3), (0, width - count)))
-    far_txt = from_partner(texts, "dp", far)
-    far_img = from_partner(images, "dp", far)
+    second = RING // 2 - FIRST_STEPS
+    far_txt = along_ring(along_ring(texts, FIRST_STEPS), second)
+    far_img = along_ring(along_ring(images, FIRST_STEPS), second)
+    far_lab = from_partner(labels.reshape(1, count), "dp", far)
 
     offsets = jnp.array([0, 1, pair_size, 2 * pair_size, pair_size << far], jnp.int32)
     bases = jnp.bitwise_xor(myself, offsets) * count
     scalars = jnp.concatenate([jnp.exp(log_scale), bias])
     lab_col = labels.reshape(count, 1)
-    lab_row = labels.reshape(1, count)
-
-    lab = jax.ShapeDtypeStruct((1, count), jnp.int32)
-    *sums, lab_sent = kernel(
-        own_kernel, (acc, acc, lab), scalars, bases, images, texts, lab_col, lab_row, products=2
-    )
-    far_lab = from_partner(lab_sent, "dp", far)
+    sums = (jnp.zeros((count, width), jnp.float32),) * 2
     chunk = count // CHUNKS
 
     def near(step, sums):
@@ -147,14 +154,14 @@
         )
         arrived = [from_partner(part, axis, bit) for axis, bit in (("dp", 1), ("dp", 0), ("pair", 0))]
         here = jnp.concatenate([bases, jnp.reshape(at, (1,))])
-        return kernel(
-            near_kernel, (acc, acc), here, scalars, images, texts, lab_col, *arrived[::-1], *sums, products=3
-        )
+        mine = (here, scalars, images, texts, lab_col)
+        sums = kernel(own_kernel, (acc, acc), *mine, part, *sums, passed=2, products=2)
+        return kernel(near_kernel, (acc, acc), *mine, *arrived[::-1], *sums, passed=2, products=3)
 
-    img_acc, txt_acc = lax.fori_loop(0, CHUNKS, near, tuple(sums))
+    img_acc, txt_acc = lax.fori_loop(0, CHUNKS, near, sums)
     image_grad = kernel(far_texts_kernel, out, scalars, bases, images, lab_col, far_txt, img_acc)
     text_grad, image_grad = kernel(
-        far_images_kernel, (out, out), scalars, bases, texts, far_img, far_lab, txt_acc, image_grad, passed=image_grad
+        far_images_kernel, (out, out), scalars, bases, texts, far_img, far_lab, txt_acc, image_grad, passed=1, products=0
     )
     return image_grad, text_grad
 

time: 199 us -> 198 us (level)
  the two profiles are of different devices: /device:TPU:40 before, /device:TPU:33 now
where the time goes in v5:
time: 198 us; the launch traced here: 197 us
  waiting for transfers between devices  83.6 us (42%)
  starting transfers between devices  62.9 us (32%)
  Pallas kernels  41.2 us (21%)
  local copies, waits for them, and re-layouts  6.2 us (3%)
  between operations  2.12 us (1%)
    ppermute x7, waiting for transfers between devices, from_partner(): return lax.ppermute(block, axis, [(i, i ^ 1 << bit) for i in range(count)])  83.3 us
    pallas_call x6, Pallas kernels, kernel(): pl.pallas_call(body, out_shape=out_shape, in_specs=specs, out_specs=out_s...  41.2 us
    ppermute x4, starting transfers between devices, along_ring(): lax.ppermute(block, axes, [(i, (i + (step if i % 2 == 0 else -step)) % co...  37.8 us
    ppermute x7, starting transfers between devices, from_partner(): return lax.ppermute(block, axis, [(i, i ^ 1 << bit) for i in range(count)])  25.1 us
  transfers between devices with their start and end apart: 11, of which 6 were waited for; matrix products, arithmetic and copies ran while one was open for 4% of the time, Pallas kernels for 19%

profile of v5, /device:TPU:33, one launch (start us, length us, event | category | flops | bytes accessed | tf_op | source)
XLA Modules:
  0.0 197.3 jit_solution(15180156377643103482)
XLA Ops:
  0.6 1.9 collective-permute-start.6
  2.6 10.9 %collective-permute-start.3 = (bf16[448,1152]{1,0:T(8,128)(2,1)}, bf16[448,1152]{1,0:T(8,128)(2,1)}, u32[]{:S(2)}, u32[]{:S(2)}) collective-permute-start(bf16[448,1152]{1,0:T(8,128)(2,1)} %img.1), channel_id=1, source_target_pairs={{0,32},{1,481},{2,34},{3,483},{4,36},{5,485},{6,38},{7,487},{8,40}... | collective-permute-start | bytes 3096584 | tf_op jit(solution)/shard_map/ppermute | solution.py:26
  13.5 0.7 and_convert_fusion.1
  15.6 0.8 copy.13.lab_col
  16.4 0.1 pad_maximum_fusion.scalars
  16.5 0.0 copy-start.1
  16.5 0.0 copy-start.7
  16.5 0.3 collective-permute-done.6
  16.8 13.9 %collective-permute-start.7 = (bf16[448,1152]{1,0:T(8,128)(2,1)}, bf16[448,1152]{1,0:T(8,128)(2,1)S(1)}, u32[]{:S(2)}, u32[]{:S(2)}) collective-permute-start(bf16[448,1152]{1,0:T(8,128)(2,1)} %collective-permute-done.6), channel_id=1, source_target_pairs={{0,224},{1,289},{2,226},{3,291},{4,228},{5,293},{6,230},{7,295},{8... | collective-permute-start | bytes 3096584 | tf_op jit(solution)/shard_map/ppermute | solution.py:26
  30.7 0.0 collective-permute-done.3
  30.7 11.0 %collective-permute-start.4 = (bf16[448,1152]{1,0:T(8,128)(2,1)}, bf16[448,1152]{1,0:T(8,128)(2,1)S(1)}, u32[]{:S(2)}, u32[]{:S(2)}) collective-permute-start(bf16[448,1152]{1,0:T(8,128)(2,1)} %collective-permute-done.3), channel_id=1, source_target_pairs={{0,224},{1,289},{2,226},{3,291},{4,228},{5,293},{6,230},{7,295},{8... | collective-permute-start | bytes 3096584 | tf_op jit(solution)/shard_map/ppermute | solution.py:26
  41.8 1.5 broadcast_in_dim.3
  43.2 1.4 broadcast_in_dim.3.clone
  44.7 0.0 copy-done.1
  44.7 0.0 copy-done.7
  44.7 0.0 copy-start.5
  44.7 0.0 copy-start.6
  44.7 134.9 %while.18 = (s32[]{:T(128)}, f32[448,1152]{1,0:T(8,128)}, f32[448,1152]{1,0:T(8,128)}, bf16[448,1152]{1,0:T(8,128)(2,1)}, bf16[448,1152]{1,0:T(8,128)(2,1)S(1)},...) while((s32[]{:T(128)}, f32[448,1152]{1,0:T(8,128)}, ...), condition=%wide.region_1.2_spmd.clone, body=%wide.region_0.1_spmd.clone.sunk | while | flops 4628496384 | bytes 40756720 | solution.py:161
  44.7 0.1 constant_dynamic-slice_fusion.5
  44.8 1.1 constant_dynamic-slice_fusion.6
  45.9 0.1 fusion.14.part
  46.0 7.4 %collective-permute-start = (bf16[464,1152]{1,0:T(8,128)(2,1)S(1)}, bf16[464,1152]{1,0:T(8,128)(2,1)}, u32[]{:S(2)}, u32[]{:S(2)}) collective-permute-start(bf16[464,1152]{1,0:T(8,128)(2,1)S(1)} %fusion.14.part), channel_id=1, source_target_pairs={{0,1},{1,0},{2,3},{3,2},{4,5},{5,4},{6,7},{7,6},{8,9},{9,8},{10,11... | collective-permute-start | bytes 3207176 | tf_op jit(solution)/shard_map/while/body/eval_jaxpr/ppermute | solution.py:19
  53.4 3.1 %collective-permute-start.1 = (bf16[464,1152]{1,0:T(8,128)(2,1)S(1)}, bf16[464,1152]{1,0:T(8,128)(2,1)}, u32[]{:S(2)}, u32[]{:S(2)}) collective-permute-start(bf16[464,1152]{1,0:T(8,128)(2,1)S(1)} %fusion.14.part), channel_id=1, source_target_pairs={{0,4},{4,0},{8,12},{12,8},{16,20},{20,16},{24,28},{28,24},{32,36},... | collective-permute-start | bytes 3207176 | tf_op jit(solution)/shard_map/while/body/eval_jaxpr/ppermute | solution.py:19
  56.5 4.4 %collective-permute-start.2 = (bf16[464,1152]{1,0:T(8,128)(2,1)S(1)}, bf16[464,1152]{1,0:T(8,128)(2,1)}, u32[]{:S(2)}, u32[]{:S(2)}) collective-permute-start(bf16[464,1152]{1,0:T(8,128)(2,1)S(1)} %fusion.14.part), channel_id=1, source_target_pairs={{0,8},{4,12},{8,0},{12,4},{16,24},{20,28},{24,16},{28,20},{32,40},... | collective-permute-start | bytes 3207176 | tf_op jit(solution)/shard_map/while/body/eval_jaxpr/ppermute | solution.py:19
  60.9 0.1 pad_add_fusion.2.bases
  61.0 0.0 copy-start.3
  61.0 7.1 %own_kernel.8 = (f32[448,1152]{1,0:T(8,128)}, f32[448,1152]{1,0:T(8,128)}) custom-call(s32[6]{0:T(128)S(1)} %pad_add_fusion.2.bases, f32[2]{0:T(128)S(1)} %get-tuple-element.389.scalars, bf16[448,1152]{1,0:T(8,128)(2,1)} %get-tuple-element.420, bf16[448,1152]{1,0:T(8,128)(2,1)} %get-tuple-element.386.txt, ...), custom_call_target="tpu_custom_call", output_to_operand_aliasing={{1}: (7, {}), {0}: (6, {})} | custom-call | flops 1849688064 | bytes 6193152 | tf_op jit(solution)/shard_map/while/body/eval_jaxpr/own_kernel/pallas_call | solution.py:118
  68.1 0.0 collective-permute-done.near1
  68.1 12.5 %collective-permute-done.1.near2 = bf16[464,1152]{1,0:T(8,128)(2,1)} collective-permute-done((bf16[464,1152]{1,0:T(8,128)(2,1)S(1)}, bf16[464,1152]{1,0:T(8,128)(2,1)}, u32[]{:S(2)}, u32[]{:S(2)}) %collective-permute-start.1) | collective-permute-done | bytes 1069088 | tf_op jit(solution)/shard_map/while/body/eval_jaxpr/ppermute | solution.py:19
  80.6 25.1 %collective-permute-done.2.near3 = bf16[464,1152]{1,0:T(8,128)(2,1)} collective-permute-done((bf16[464,1152]{1,0:T(8,128)(2,1)S(1)}, bf16[464,1152]{1,0:T(8,128)(2,1)}, u32[]{:S(2)}, u32[]{:S(2)}) %collective-permute-start.2) | collective-permute-done | bytes 1069088 | tf_op jit(solution)/shard_map/while/body/eval_jaxpr/ppermute | solution.py:19
  105.7 0.0 copy-done.3
  105.7 0.0 copy-start.2
  105.7 9.9 %near_kernel.8 = (f32[448,1152]{1,0:T(8,128)}, f32[448,1152]{1,0:T(8,128)}) custom-call(s32[6]{0:T(128)S(1)} %pad_add_fusion.2.bases, f32[2]{0:T(128)S(1)} %get-tuple-element.389.scalars, bf16[448,1152]{1,0:T(8,128)(2,1)} %get-tuple-element.420, bf16[448,1152]{1,0:T(8,128)(2,1)S(1)} %copy-done.3, ...), custom_call_target="tpu_custom_call", output_to_operand_aliasing={{1}: (9, {}), {0}: (8, {})} | custom-call | flops 2774532096 | bytes 9289728 | tf_op jit(solution)/shard_map/while/body/eval_jaxpr/near_kernel/pallas_call | solution.py:118
  115.6 0.0 copy-done.2
  115.6 0.1 constant_dynamic-slice_fusion.5
  115.7 1.1 constant_dynamic-slice_fusion.6
  116.8 0.1 fusion.14.part
  116.9 2.7 %collective-permute-start = (bf16[464,1152]{1,0:T(8,128)(2,1)S(1)}, bf16[464,1152]{1,0:T(8,128)(2,1)}, u32[]{:S(2)}, u32[]{:S(2)}) collective-permute-start(bf16[464,1152]{1,0:T(8,128)(2,1)S(1)} %fusion.14.part), channel_id=1, source_target_pairs={{0,1},{1,0},{2,3},{3,2},{4,5},{5,4},{6,7},{7,6},{8,9},{9,8},{10,11... | collective-permute-start | bytes 3207176 | tf_op jit(solution)/shard_map/while/body/eval_jaxpr/ppermute | solution.py:19
  119.6 1.9 collective-permute-start.1
  121.5 3.3 %collective-permute-start.2 = (bf16[464,1152]{1,0:T(8,128)(2,1)S(1)}, bf16[464,1152]{1,0:T(8,128)(2,1)}, u32[]{:S(2)}, u32[]{:S(2)}) collective-permute-start(bf16[464,1152]{1,0:T(8,128)(2,1)S(1)} %fusion.14.part), channel_id=1, source_target_pairs={{0,8},{4,12},{8,0},{12,4},{16,24},{20,28},{24,16},{28,20},{32,40},... | collective-permute-start | bytes 3207176 | tf_op jit(solution)/shard_map/while/body/eval_jaxpr/ppermute | solution.py:19
  124.8 0.1 pad_add_fusion.2.bases
  124.9 0.0 copy-start.3
  124.9 7.1 %own_kernel.8 = (f32[448,1152]{1,0:T(8,128)}, f32[448,1152]{1,0:T(8,128)}) custom-call(s32[6]{0:T(128)S(1)} %pad_add_fusion.2.bases, f32[2]{0:T(128)S(1)} %get-tuple-element.389.scalars, bf16[448,1152]{1,0:T(8,128)(2,1)} %get-tuple-element.420, bf16[448,1152]{1,0:T(8,128)(2,1)} %get-tuple-element.386.txt, ...), custom_call_target="tpu_custom_call", output_to_operand_aliasing={{1}: (7, {}), {0}: (6, {})} | custom-call | flops 1849688064 | bytes 6193152 | tf_op jit(solution)/shard_map/while/body/eval_jaxpr/own_kernel/pallas_call | solution.py:118
  132.0 0.0 collective-permute-done.near1
  132.0 14.8 %collective-permute-done.1.near2 = bf16[464,1152]{1,0:T(8,128)(2,1)} collective-permute-done((bf16[464,1152]{1,0:T(8,128)(2,1)S(1)}, bf16[464,1152]{1,0:T(8,128)(2,1)}, u32[]{:S(2)}, u32[]{:S(2)}) %collective-permute-start.1) | collective-permute-done | bytes 1069088 | tf_op jit(solution)/shard_map/while/body/eval_jaxpr/ppermute | solution.py:19
  146.8 22.8 %collective-permute-done.2.near3 = bf16[464,1152]{1,0:T(8,128)(2,1)} collective-permute-done((bf16[464,1152]{1,0:T(8,128)(2,1)S(1)}, bf16[464,1152]{1,0:T(8,128)(2,1)}, u32[]{:S(2)}, u32[]{:S(2)}) %collective-permute-start.2) | collective-permute-done | bytes 1069088 | tf_op jit(solution)/shard_map/while/body/eval_jaxpr/ppermute | solution.py:19
  169.7 0.0 copy-done.3
  169.7 0.0 copy-start.2
  169.7 9.9 %near_kernel.8 = (f32[448,1152]{1,0:T(8,128)}, f32[448,1152]{1,0:T(8,128)}) custom-call(s32[6]{0:T(128)S(1)} %pad_add_fusion.2.bases, f32[2]{0:T(128)S(1)} %get-tuple-element.389.scalars, bf16[448,1152]{1,0:T(8,128)(2,1)} %get-tuple-element.420, bf16[448,1152]{1,0:T(8,128)(2,1)S(1)} %copy-done.3, ...), custom_call_target="tpu_custom_call", output_to_operand_aliasing={{1}: (9, {}), {0}: (8, {})} | custom-call | flops 2774532096 | bytes 9289728 | tf_op jit(solution)/shard_map/while/body/eval_jaxpr/near_kernel/pallas_call | solution.py:118
  179.6 0.0 copy-done.2
  179.6 0.0 copy-done.5
  179.6 2.4 %collective-permute-start.5 = (s32[1,448]{1,0:T(1,128)S(1)}, s32[1,448]{1,0:T(1,128)S(1)}, u32[]{:S(2)}, u32[]{:S(2)}) collective-permute-start(s32[1,448]{1,0:T(1,128)S(1)} %bitcast.6), channel_id=1, source_target_pairs={{0,256},{4,260},{8,264},{12,268},{16,272},{20,276},{24,280},{28,28... | collective-permute-start | bytes 5384 | tf_op jit(solution)/shard_map/ppermute | solution.py:19
  181.9 0.0 copy-done.6
  182.0 0.0 collective-permute-done.7.far_txt
  182.0 0.0 copy-start
  182.0 0.0 copy-start.4
  182.0 4.2 %far_texts_kernel.1.image_grad = bf16[448,1152]{1,0:T(8,128)(2,1)} custom-call(f32[2]{0:T(128)S(1)} %get-tuple-element.411, s32[5]{0:T(128)S(1)} %xor_multiply_fusion.1.bases, bf16[448,1152]{1,0:T(8,128)(2,1)S(1)} %get-tuple-element.409, s32[448,1]{1,0:T(8,128)S(1)} %get-tuple-element.412, bf16[448,1152]{1,0:T(8,128)(2,1)S(1)} %collective-permute-done.7.far_txt, ...), custom_call_target="tpu_custom_call" | custom-call | flops 924844032 | bytes 3096576 | tf_op jit(solution)/shard_map/far_texts_kernel/pallas_call | solution.py:118
  186.2 8.1 %collective-permute-done.5.far_lab = s32[1,448]{1,0:T(1,128)S(1)} collective-permute-done((s32[1,448]{1,0:T(1,128)S(1)}, s32[1,448]{1,0:T(1,128)S(1)}, u32[]{:S(2)}, u32[]{:S(2)}) %collective-permute-start.5) | collective-permute-done | bytes 1824 | tf_op jit(solution)/shard_map/ppermute | solution.py:19
  194.2 0.0 collective-permute-done.4.far_img
  194.2 0.0 copy-done
  194.2 0.0 copy-done.4
  194.2 3.0 %far_images_kernel.1 = (bf16[448,1152]{1,0:T(8,128)(2,1)}, bf16[448,1152]{1,0:T(8,128)(2,1)}) custom-call(f32[2]{0:T(128)S(1)} %get-tuple-element.411, s32[5]{0:T(128)S(1)} %xor_multiply_fusion.1.bases, bf16[448,1152]{1,0:T(8,128)(2,1)S(1)} %copy-done.4, bf16[448,1152]{1,0:T(8,128)(2,1)S(1)} %collective-permute-done.4.far_img, ...), custom_call_target="tpu_custom_call", output_to_operand_aliasing={{1}: (6, {})} | custom-call | tf_op jit(solution)/shard_map/far_images_kernel/pallas_call | solution.py:118
  (7 shorter events, 0.0 us)
Async XLA Ops:
  0.6 16.2 %collective-permute-start.6 = (bf16[448,1152]{1,0:T(8,128)(2,1)}, bf16[448,1152]{1,0:T(8,128)(2,1)}, u32[]{:S(2)}, u32[]{:S(2)}) collective-permute-start(bf16[448,1152]{1,0:T(8,128)(2,1)} %txt.1), channel_id=1, source_target_pairs={{0,32},{1,481},{2,34},{3,483},{4,36},{5,485},{6,38},{7,487},{8,40}... | collective-permute-start | bytes 3096584 | tf_op jit(solution)/shard_map/ppermute | solution.py:26
  2.6 28.1 %collective-permute-start.3 = (bf16[448,1152]{1,0:T(8,128)(2,1)}, bf16[448,1152]{1,0:T(8,128)(2,1)}, u32[]{:S(2)}, u32[]{:S(2)}) collective-permute-start(bf16[448,1152]{1,0:T(8,128)(2,1)} %img.1), channel_id=1, source_target_pairs={{0,32},{1,481},{2,34},{3,483},{4,36},{5,485},{6,38},{7,487},{8,40}... | collective-permute-start | bytes 3096584 | tf_op jit(solution)/shard_map/ppermute | solution.py:26
  16.5 28.2 %copy-start.1 = (bf16[448,1152]{1,0:T(8,128)(2,1)S(1)}, bf16[448,1152]{1,0:T(8,128)(2,1)}, u32[]{:S(2)}) copy-start(bf16[448,1152]{1,0:T(8,128)(2,1)} %img.1) | copy-start | bytes 3096580
  16.5 28.2 %copy-start.7 = (s32[5]{0:T(128)S(1)}, s32[5]{0:T(128)}, u32[]{:S(2)}) copy-start(s32[5]{0:T(128)} %constant.80.clone.5) | copy-start | bytes 64
  16.8 165.2 %collective-permute-start.7 = (bf16[448,1152]{1,0:T(8,128)(2,1)}, bf16[448,1152]{1,0:T(8,128)(2,1)S(1)}, u32[]{:S(2)}, u32[]{:S(2)}) collective-permute-start(bf16[448,1152]{1,0:T(8,128)(2,1)} %collective-permute-done.6), channel_id=1, source_target_pairs={{0,224},{1,289},{2,226},{3,291},{4,228},{5,293},{6,230},{7,295},{8... | collective-permute-start | bytes 3096584 | tf_op jit(solution)/shard_map/ppermute | solution.py:26
  30.7 163.5 %collective-permute-start.4 = (bf16[448,1152]{1,0:T(8,128)(2,1)}, bf16[448,1152]{1,0:T(8,128)(2,1)S(1)}, u32[]{:S(2)}, u32[]{:S(2)}) collective-permute-start(bf16[448,1152]{1,0:T(8,128)(2,1)} %collective-permute-done.3), channel_id=1, source_target_pairs={{0,224},{1,289},{2,226},{3,291},{4,228},{5,293},{6,230},{7,295},{8... | collective-permute-start | bytes 3096584 | tf_op jit(solution)/shard_map/ppermute | solution.py:26
  44.7 134.9 %copy-start.5 = (s32[448]{0:T(512)S(1)}, s32[448]{0:T(512)}, u32[]{:S(2)}) copy-start(s32[448]{0:T(512)} %param.10) | copy-start | bytes 5380
  44.7 137.3 %copy-start.6 = (s32[5]{0:T(128)S(1)}, s32[5]{0:T(128)}, u32[]{:S(2)}) copy-start(s32[5]{0:T(128)} %constant.80.clone) | copy-start | bytes 64
  46.0 22.1 %collective-permute-start = (bf16[464,1152]{1,0:T(8,128)(2,1)S(1)}, bf16[464,1152]{1,0:T(8,128)(2,1)}, u32[]{:S(2)}, u32[]{:S(2)}) collective-permute-start(bf16[464,1152]{1,0:T(8,128)(2,1)S(1)} %fusion.14.part), channel_id=1, source_target_pairs={{0,1},{1,0},{2,3},{3,2},{4,5},{5,4},{6,7},{7,6},{8,9},{9,8},{10,11... | collective-permute-start | bytes 3207176 | tf_op jit(solution)/shard_map/while/body/eval_jaxpr/ppermute | solution.py:19
  53.4 27.2 %collective-permute-start.1 = (bf16[464,1152]{1,0:T(8,128)(2,1)S(1)}, bf16[464,1152]{1,0:T(8,128)(2,1)}, u32[]{:S(2)}, u32[]{:S(2)}) collective-permute-start(bf16[464,1152]{1,0:T(8,128)(2,1)S(1)} %fusion.14.part), channel_id=1, source_target_pairs={{0,4},{4,0},{8,12},{12,8},{16,20},{20,16},{24,28},{28,24},{32,36},... | collective-permute-start | bytes 3207176 | tf_op jit(solution)/shard_map/while/body/eval_jaxpr/ppermute | solution.py:19
  56.5 49.2 %collective-permute-start.2 = (bf16[464,1152]{1,0:T(8,128)(2,1)S(1)}, bf16[464,1152]{1,0:T(8,128)(2,1)}, u32[]{:S(2)}, u32[]{:S(2)}) collective-permute-start(bf16[464,1152]{1,0:T(8,128)(2,1)S(1)} %fusion.14.part), channel_id=1, source_target_pairs={{0,8},{4,12},{8,0},{12,4},{16,24},{20,28},{24,16},{28,20},{32,40},... | collective-permute-start | bytes 3207176 | tf_op jit(solution)/shard_map/while/body/eval_jaxpr/ppermute | solution.py:19
  61.0 44.7 %copy-start.3 = (bf16[448,1152]{1,0:T(8,128)(2,1)S(1)}, bf16[448,1152]{1,0:T(8,128)(2,1)}, u32[]{:S(2)}) copy-start(bf16[448,1152]{1,0:T(8,128)(2,1)} %get-tuple-element.386.txt) | copy-start | bytes 3096580 | tf_op jit(solution)/shard_map/while
  105.7 9.9 %copy-start.2 = (bf16[448,1152]{1,0:T(8,128)(2,1)S(1)}, bf16[448,1152]{1,0:T(8,128)(2,1)}, u32[]{:S(2)}) copy-start(bf16[448,1152]{1,0:T(8,128)(2,1)} %get-tuple-element.420) | copy-start | bytes 3096580 | tf_op jit(solution)/shard_map/while
  116.9 15.1 %collective-permute-start = (bf16[464,1152]{1,0:T(8,128)(2,1)S(1)}, bf16[464,1152]{1,0:T(8,128)(2,1)}, u32[]{:S(2)}, u32[]{:S(2)}) collective-permute-start(bf16[464,1152]{1,0:T(8,128)(2,1)S(1)} %fusion.14.part), channel_id=1, source_target_pairs={{0,1},{1,0},{2,3},{3,2},{4,5},{5,4},{6,7},{7,6},{8,9},{9,8},{10,11... | collective-permute-start | bytes 3207176 | tf_op jit(solution)/shard_map/while/body/eval_jaxpr/ppermute | solution.py:19
  119.6 27.2 %collective-permute-start.1 = (bf16[464,1152]{1,0:T(8,128)(2,1)S(1)}, bf16[464,1152]{1,0:T(8,128)(2,1)}, u32[]{:S(2)}, u32[]{:S(2)}) collective-permute-start(bf16[464,1152]{1,0:T(8,128)(2,1)S(1)} %fusion.14.part), channel_id=1, source_target_pairs={{0,4},{4,0},{8,12},{12,8},{16,20},{20,16},{24,28},{28,24},{32,36},... | collective-permute-start | bytes 3207176 | tf_op jit(solution)/shard_map/while/body/eval_jaxpr/ppermute | solution.py:19
  121.5 48.1 %collective-permute-start.2 = (bf16[464,1152]{1,0:T(8,128)(2,1)S(1)}, bf16[464,1152]{1,0:T(8,128)(2,1)}, u32[]{:S(2)}, u32[]{:S(2)}) collective-permute-start(bf16[464,1152]{1,0:T(8,128)(2,1)S(1)} %fusion.14.part), channel_id=1, source_target_pairs={{0,8},{4,12},{8,0},{12,4},{16,24},{20,28},{24,16},{28,20},{32,40},... | collective-permute-start | bytes 3207176 | tf_op jit(solution)/shard_map/while/body/eval_jaxpr/ppermute | solution.py:19
  124.9 44.7 %copy-start.3 = (bf16[448,1152]{1,0:T(8,128)(2,1)S(1)}, bf16[448,1152]{1,0:T(8,128)(2,1)}, u32[]{:S(2)}) copy-start(bf16[448,1152]{1,0:T(8,128)(2,1)} %get-tuple-element.386.txt) | copy-start | bytes 3096580 | tf_op jit(solution)/shard_map/while
  169.7 9.9 %copy-start.2 = (bf16[448,1152]{1,0:T(8,128)(2,1)S(1)}, bf16[448,1152]{1,0:T(8,128)(2,1)}, u32[]{:S(2)}) copy-start(bf16[448,1152]{1,0:T(8,128)(2,1)} %get-tuple-element.420) | copy-start | bytes 3096580 | tf_op jit(solution)/shard_map/while
  179.6 14.7 %collective-permute-start.5 = (s32[1,448]{1,0:T(1,128)S(1)}, s32[1,448]{1,0:T(1,128)S(1)}, u32[]{:S(2)}, u32[]{:S(2)}) collective-permute-start(s32[1,448]{1,0:T(1,128)S(1)} %bitcast.6), channel_id=1, source_target_pairs={{0,256},{4,260},{8,264},{12,268},{16,272},{20,276},{24,280},{28,28... | collective-permute-start | bytes 5384 | tf_op jit(solution)/shard_map/ppermute | solution.py:19
  182.0 12.3 %copy-start = (f32[448,1152]{1,0:T(8,128)S(1)}, f32[448,1152]{1,0:T(8,128)}, u32[]{:S(2)}) copy-start(f32[448,1152]{1,0:T(8,128)} %get-tuple-element.407) | copy-start | bytes 6193156
  182.0 12.3 %copy-start.4 = (bf16[448,1152]{1,0:T(8,128)(2,1)S(1)}, bf16[448,1152]{1,0:T(8,128)(2,1)}, u32[]{:S(2)}) copy-start(bf16[448,1152]{1,0:T(8,128)(2,1)} %get-tuple-element.408) | copy-start | bytes 3096580

commit v6 on v5

--- a/solution.py
+++ b/solution.py
@@ -83,7 +83,8 @@
 def far_images_kernel(scalars, bases, txt, far_img, far_lab, txt_in, image_grad, text_grad, image_grad_out):
     count = txt.shape[0]
     scale, shift = scalars[0], scalars[1]
-    hit = hit_rows(far_lab[...], bases[0], count, count)
+    their_lab = jnp.where(bases[4] < bases[0], far_lab[0:1, :], far_lab[1:2, :])
+    hit = hit_rows(their_lab, bases[0], count, count)
     total = txt_in[...] + gradient(txt[...], far_img[...], hit, scale, shift)
     text_grad[...] = (scale * total).astype(jnp.bfloat16)
 
@@ -131,7 +132,10 @@
     second = RING // 2 - FIRST_STEPS
     far_txt = along_ring(along_ring(texts, FIRST_STEPS), second)
     far_img = along_ring(along_ring(images, FIRST_STEPS), second)
-    far_lab = from_partner(labels.reshape(1, count), "dp", far)
+    half = 1 << far
+    far_lab = lax.all_gather(
+        labels, "dp", axis_index_groups=[[i, i + half] for i in range(half)], axis=0
+    )
 
     offsets = jnp.array([0, 1, pair_size, 2 * pair_size, pair_size << far], jnp.int32)
     bases = jnp.bitwise_xor(myself, offsets) * count

time: 198 us -> 207 us (1.045)
  the two profiles are of different devices: /device:TPU:33 before, /device:TPU:202 now
where the time goes in v6:
time: 207 us; the launch traced here: 206 us
  waiting for transfers between devices  93 us (45%)
  Pallas kernels  41.5 us (20%)
  starting transfers between devices  39.1 us (19%)
  blocking collectives  19.6 us (9%)
  local copies, waits for them, and re-layouts  8.39 us (4%)
  between operations  2.74 us (1%)
    ppermute x6, waiting for transfers between devices, from_partner(): return lax.ppermute(block, axis, [(i, i ^ 1 << bit) for i in range(count)])  75.7 us
    pallas_call x6, Pallas kernels, kernel(): pl.pallas_call(body, out_shape=out_shape, in_specs=specs, out_specs=out_s...  41.5 us
    ppermute x4, starting transfers between devices, along_ring(): lax.ppermute(block, axes, [(i, (i + (step if i % 2 == 0 else -step)) % co...  22.6 us
    unnamed x1, blocking collectives  19.6 us
    ppermute x4, waiting for transfers between devices, along_ring(): lax.ppermute(block, axes, [(i, (i + (step if i % 2 == 0 else -step)) % co...  17.3 us
    ppermute x6, starting transfers between devices, from_partner(): return lax.ppermute(block, axis, [(i, i ^ 1 << bit) for i in range(count)])  16.4 us
  transfers between devices with their start and end apart: 10, of which 5 were waited for; matrix products, arithmetic and copies ran while one was open for 5% of the time, Pallas kernels for 19%

profile of v6, /device:TPU:202, one launch (start us, length us, event | category | flops | bytes accessed | tf_op | source)
XLA Modules:
  0.0 206.2 jit_solution(1104349167236422985)
XLA Ops:
  0.6 3.8 %collective-permute-start.5 = (bf16[448,1152]{1,0:T(8,128)(2,1)}, bf16[448,1152]{1,0:T(8,128)(2,1)}, u32[]{:S(2)}, u32[]{:S(2)}) collective-permute-start(bf16[448,1152]{1,0:T(8,128)(2,1)} %txt.1), channel_id=1, source_target_pairs={{0,32},{1,481},{2,34},{3,483},{4,36},{5,485},{6,38},{7,487},{8,40}... | collective-permute-start | bytes 3096584 | tf_op jit(solution)/shard_map/ppermute | solution.py:26
  4.5 5.0 %collective-permute-start.3 = (bf16[448,1152]{1,0:T(8,128)(2,1)}, bf16[448,1152]{1,0:T(8,128)(2,1)}, u32[]{:S(2)}, u32[]{:S(2)}) collective-permute-start(bf16[448,1152]{1,0:T(8,128)(2,1)} %img.1), channel_id=1, source_target_pairs={{0,32},{1,481},{2,34},{3,483},{4,36},{5,485},{6,38},{7,487},{8,40}... | collective-permute-start | bytes 3096584 | tf_op jit(solution)/shard_map/ppermute | solution.py:26
  9.5 0.7 and_convert_fusion.1
  11.6 0.8 copy.13.lab_col
  12.4 1.3 dynamic-slice
  14.3 0.9 dynamic-update-slice
  15.2 19.6 %all-reduce.2 = s32[896]{0:T(1024)S(1)} all-reduce(s32[896]{0:T(1024)S(1)} %dynamic-update-slice), channel_id=2, replica_groups={{0,256},{4,260},{8,264},{12,268},{16,272},{20,276},{24,280},{28,284},{3..., use_global_device_ids=true, to_apply=%add.2 | all-reduce | flops 896 | bytes 7168
  34.8 0.1 reshape.18.far_lab
  34.9 0.1 pad_maximum_fusion.scalars
  35.0 0.7 xor_multiply_fusion.1.bases
  35.7 0.0 copy-start.1
  35.7 0.0 copy-start.4
  35.7 0.0 collective-permute-done.5
  35.7 2.1 collective-permute-start.6
  37.8 0.0 collective-permute-done.3
  37.8 11.7 %collective-permute-start.4 = (bf16[448,1152]{1,0:T(8,128)(2,1)}, bf16[448,1152]{1,0:T(8,128)(2,1)S(1)}, u32[]{:S(2)}, u32[]{:S(2)}) collective-permute-start(bf16[448,1152]{1,0:T(8,128)(2,1)} %collective-permute-done.3), channel_id=1, source_target_pairs={{0,224},{1,289},{2,226},{3,291},{4,228},{5,293},{6,230},{7,295},{8... | collective-permute-start | bytes 3096584 | tf_op jit(solution)/shard_map/ppermute | solution.py:26
  49.5 1.5 broadcast_in_dim.3
  51.0 1.4 broadcast_in_dim.3.clone
  52.4 0.0 copy-done.1
  52.4 0.0 copy-done.4
  52.4 128.9 %while.18 = (s32[]{:T(128)}, f32[448,1152]{1,0:T(8,128)}, f32[448,1152]{1,0:T(8,128)}, bf16[448,1152]{1,0:T(8,128)(2,1)S(1)}, bf16[448,1152]{1,0:T(8,128)(2,1)},...) while((s32[]{:T(128)}, f32[448,1152]{1,0:T(8,128)}, ...), condition=%wide.region_1.2_spmd.clone, body=%wide.region_0.1_spmd.clone.sunk | while | flops 4628496384 | bytes 40756720 | solution.py:165
  52.4 0.1 constant_dynamic-slice_fusion.5
  52.5 1.1 constant_dynamic-slice_fusion.6
  53.6 0.1 fusion.14.part
  53.7 1.9 collective-permute-start
  55.6 2.4 %collective-permute-start.1 = (bf16[464,1152]{1,0:T(8,128)(2,1)S(1)}, bf16[464,1152]{1,0:T(8,128)(2,1)}, u32[]{:S(2)}, u32[]{:S(2)}) collective-permute-start(bf16[464,1152]{1,0:T(8,128)(2,1)S(1)} %fusion.14.part), channel_id=1, source_target_pairs={{0,4},{4,0},{8,12},{12,8},{16,20},{20,16},{24,28},{28,24},{32,36},... | collective-permute-start | bytes 3207176 | tf_op jit(solution)/shard_map/while/body/eval_jaxpr/ppermute | solution.py:19
  58.1 4.3 %collective-permute-start.2 = (bf16[464,1152]{1,0:T(8,128)(2,1)S(1)}, bf16[464,1152]{1,0:T(8,128)(2,1)}, u32[]{:S(2)}, u32[]{:S(2)}) collective-permute-start(bf16[464,1152]{1,0:T(8,128)(2,1)S(1)} %fusion.14.part), channel_id=1, source_target_pairs={{0,8},{4,12},{8,0},{12,4},{16,24},{20,28},{24,16},{28,20},{32,40},... | collective-permute-start | bytes 3207176 | tf_op jit(solution)/shard_map/while/body/eval_jaxpr/ppermute | solution.py:19
  62.4 0.1 pad_add_fusion.2.bases
  62.5 0.0 copy-start.3
  62.5 7.1 %own_kernel.8 = (f32[448,1152]{1,0:T(8,128)}, f32[448,1152]{1,0:T(8,128)}) custom-call(s32[6]{0:T(128)S(1)} %pad_add_fusion.2.bases, f32[2]{0:T(128)S(1)} %get-tuple-element.389.scalars, bf16[448,1152]{1,0:T(8,128)(2,1)} %get-tuple-element.387.img, bf16[448,1152]{1,0:T(8,128)(2,1)} %get-tuple-element.419, ...), custom_call_target="tpu_custom_call", output_to_operand_aliasing={{1}: (7, {}), {0}: (6, {})} | custom-call | flops 1849688064 | bytes 6193152 | tf_op jit(solution)/shard_map/while/body/eval_jaxpr/own_kernel/pallas_call | solution.py:119
  69.6 0.0 collective-permute-done.near1
  69.6 14.4 %collective-permute-done.1.near2 = bf16[464,1152]{1,0:T(8,128)(2,1)} collective-permute-done((bf16[464,1152]{1,0:T(8,128)(2,1)S(1)}, bf16[464,1152]{1,0:T(8,128)(2,1)}, u32[]{:S(2)}, u32[]{:S(2)}) %collective-permute-start.1) | collective-permute-done | bytes 1069088 | tf_op jit(solution)/shard_map/while/body/eval_jaxpr/ppermute | solution.py:19
  84.0 23.4 %collective-permute-done.2.near3 = bf16[464,1152]{1,0:T(8,128)(2,1)} collective-permute-done((bf16[464,1152]{1,0:T(8,128)(2,1)S(1)}, bf16[464,1152]{1,0:T(8,128)(2,1)}, u32[]{:S(2)}, u32[]{:S(2)}) %collective-permute-start.2) | collective-permute-done | bytes 1069088 | tf_op jit(solution)/shard_map/while/body/eval_jaxpr/ppermute | solution.py:19
  107.5 0.0 copy-done.3
  107.5 0.0 copy-start.2
  107.5 9.9 %near_kernel.8 = (f32[448,1152]{1,0:T(8,128)}, f32[448,1152]{1,0:T(8,128)}) custom-call(s32[6]{0:T(128)S(1)} %pad_add_fusion.2.bases, f32[2]{0:T(128)S(1)} %get-tuple-element.389.scalars, bf16[448,1152]{1,0:T(8,128)(2,1)S(1)} %copy-done.3, bf16[448,1152]{1,0:T(8,128)(2,1)} %get-tuple-element.419, ...), custom_call_target="tpu_custom_call", output_to_operand_aliasing={{1}: (9, {}), {0}: (8, {})} | custom-call | flops 2774532096 | bytes 9289728 | tf_op jit(solution)/shard_map/while/body/eval_jaxpr/near_kernel/pallas_call | solution.py:119
  117.4 0.0 copy-done.2
  117.4 0.1 constant_dynamic-slice_fusion.5
  117.5 1.1 constant_dynamic-slice_fusion.6
  118.6 0.1 fusion.14.part
  118.7 1.9 collective-permute-start
  120.6 3.7 %collective-permute-start.1 = (bf16[464,1152]{1,0:T(8,128)(2,1)S(1)}, bf16[464,1152]{1,0:T(8,128)(2,1)}, u32[]{:S(2)}, u32[]{:S(2)}) collective-permute-start(bf16[464,1152]{1,0:T(8,128)(2,1)S(1)} %fusion.14.part), channel_id=1, source_target_pairs={{0,4},{4,0},{8,12},{12,8},{16,20},{20,16},{24,28},{28,24},{32,36},... | collective-permute-start | bytes 3207176 | tf_op jit(solution)/shard_map/while/body/eval_jaxpr/ppermute | solution.py:19
  124.3 2.1 %collective-permute-start.2 = (bf16[464,1152]{1,0:T(8,128)(2,1)S(1)}, bf16[464,1152]{1,0:T(8,128)(2,1)}, u32[]{:S(2)}, u32[]{:S(2)}) collective-permute-start(bf16[464,1152]{1,0:T(8,128)(2,1)S(1)} %fusion.14.part), channel_id=1, source_target_pairs={{0,8},{4,12},{8,0},{12,4},{16,24},{20,28},{24,16},{28,20},{32,40},... | collective-permute-start | bytes 3207176 | tf_op jit(solution)/shard_map/while/body/eval_jaxpr/ppermute | solution.py:19
  126.4 0.1 pad_add_fusion.2.bases
  126.5 0.0 copy-start.3
  126.5 7.1 %own_kernel.8 = (f32[448,1152]{1,0:T(8,128)}, f32[448,1152]{1,0:T(8,128)}) custom-call(s32[6]{0:T(128)S(1)} %pad_add_fusion.2.bases, f32[2]{0:T(128)S(1)} %get-tuple-element.389.scalars, bf16[448,1152]{1,0:T(8,128)(2,1)} %get-tuple-element.387.img, bf16[448,1152]{1,0:T(8,128)(2,1)} %get-tuple-element.419, ...), custom_call_target="tpu_custom_call", output_to_operand_aliasing={{1}: (7, {}), {0}: (6, {})} | custom-call | flops 1849688064 | bytes 6193152 | tf_op jit(solution)/shard_map/while/body/eval_jaxpr/own_kernel/pallas_call | solution.py:119
  133.6 0.0 collective-permute-done.near1
  133.6 15.4 %collective-permute-done.1.near2 = bf16[464,1152]{1,0:T(8,128)(2,1)} collective-permute-done((bf16[464,1152]{1,0:T(8,128)(2,1)S(1)}, bf16[464,1152]{1,0:T(8,128)(2,1)}, u32[]{:S(2)}, u32[]{:S(2)}) %collective-permute-start.1) | collective-permute-done | bytes 1069088 | tf_op jit(solution)/shard_map/while/body/eval_jaxpr/ppermute | solution.py:19
  149.0 22.5 %collective-permute-done.2.near3 = bf16[464,1152]{1,0:T(8,128)(2,1)} collective-permute-done((bf16[464,1152]{1,0:T(8,128)(2,1)S(1)}, bf16[464,1152]{1,0:T(8,128)(2,1)}, u32[]{:S(2)}, u32[]{:S(2)}) %collective-permute-start.2) | collective-permute-done | bytes 1069088 | tf_op jit(solution)/shard_map/while/body/eval_jaxpr/ppermute | solution.py:19
  171.5 0.0 copy-done.3
  171.5 0.0 copy-start.2
  171.5 9.9 %near_kernel.8 = (f32[448,1152]{1,0:T(8,128)}, f32[448,1152]{1,0:T(8,128)}) custom-call(s32[6]{0:T(128)S(1)} %pad_add_fusion.2.bases, f32[2]{0:T(128)S(1)} %get-tuple-element.389.scalars, bf16[448,1152]{1,0:T(8,128)(2,1)S(1)} %copy-done.3, bf16[448,1152]{1,0:T(8,128)(2,1)} %get-tuple-element.419, ...), custom_call_target="tpu_custom_call", output_to_operand_aliasing={{1}: (9, {}), {0}: (8, {})} | custom-call | flops 2774532096 | bytes 9289728 | tf_op jit(solution)/shard_map/while/body/eval_jaxpr/near_kernel/pallas_call | solution.py:119
  181.4 0.0 copy-done.2
  181.4 0.0 collective-permute-done.6.far_txt
  181.4 0.0 copy-start
  181.4 4.5 %far_texts_kernel.1.image_grad = bf16[448,1152]{1,0:T(8,128)(2,1)} custom-call(f32[2]{0:T(128)S(1)} %get-tuple-element.410, s32[5]{0:T(128)S(1)} %xor_multiply_fusion.1.bases, bf16[448,1152]{1,0:T(8,128)(2,1)} %get-tuple-element.408, s32[448,1]{1,0:T(8,128)S(1)} %get-tuple-element.411, bf16[448,1152]{1,0:T(8,128)(2,1)S(1)} %collective-permute-done.6.far_txt, ...), custom_call_target="tpu_custom_call" | custom-call | flops 924844032 | bytes 3096576 | tf_op jit(solution)/shard_map/far_texts_kernel/pallas_call | solution.py:119
  185.9 17.3 %collective-permute-done.4.far_img = bf16[448,1152]{1,0:T(8,128)(2,1)S(1)} collective-permute-done((bf16[448,1152]{1,0:T(8,128)(2,1)}, bf16[448,1152]{1,0:T(8,128)(2,1)S(1)}, u32[]{:S(2)}, u32[]{:S(2)}) %collective-permute-start.4) | collective-permute-done | bytes 1032224 | tf_op jit(solution)/shard_map/ppermute | solution.py:26
  203.2 0.0 copy-done
  203.2 3.0 %far_images_kernel.1 = (bf16[448,1152]{1,0:T(8,128)(2,1)}, bf16[448,1152]{1,0:T(8,128)(2,1)}) custom-call(f32[2]{0:T(128)S(1)} %get-tuple-element.410, s32[5]{0:T(128)S(1)} %xor_multiply_fusion.1.bases, bf16[448,1152]{1,0:T(8,128)(2,1)S(1)} %get-tuple-element.407, ...), custom_call_target="tpu_custom_call", output_to_operand_aliasing={{1}: (6, {})} | custom-call | tf_op jit(solution)/shard_map/far_images_kernel/pallas_call | solution.py:119
  (7 shorter events, 0.0 us)
Async XLA Ops:
  0.6 35.1 %collective-permute-start.5 = (bf16[448,1152]{1,0:T(8,128)(2,1)}, bf16[448,1152]{1,0:T(8,128)(2,1)}, u32[]{:S(2)}, u32[]{:S(2)}) collective-permute-start(bf16[448,1152]{1,0:T(8,128)(2,1)} %txt.1), channel_id=1, source_target_pairs={{0,32},{1,481},{2,34},{3,483},{4,36},{5,485},{6,38},{7,487},{8,40}... | collective-permute-start | bytes 3096584 | tf_op jit(solution)/shard_map/ppermute | solution.py:26
  4.5 33.3 %collective-permute-start.3 = (bf16[448,1152]{1,0:T(8,128)(2,1)}, bf16[448,1152]{1,0:T(8,128)(2,1)}, u32[]{:S(2)}, u32[]{:S(2)}) collective-permute-start(bf16[448,1152]{1,0:T(8,128)(2,1)} %img.1), channel_id=1, source_target_pairs={{0,32},{1,481},{2,34},{3,483},{4,36},{5,485},{6,38},{7,487},{8,40}... | collective-permute-start | bytes 3096584 | tf_op jit(solution)/shard_map/ppermute | solution.py:26
  35.7 16.7 %copy-start.1 = (bf16[448,1152]{1,0:T(8,128)(2,1)S(1)}, bf16[448,1152]{1,0:T(8,128)(2,1)}, u32[]{:S(2)}) copy-start(bf16[448,1152]{1,0:T(8,128)(2,1)} %txt.1) | copy-start | bytes 3096580
  35.7 16.7 %copy-start.4 = (s32[5]{0:T(128)S(1)}, s32[5]{0:T(128)}, u32[]{:S(2)}) copy-start(s32[5]{0:T(128)} %constant.80.clone.5) | copy-start | bytes 64
  35.7 145.6 %collective-permute-start.6 = (bf16[448,1152]{1,0:T(8,128)(2,1)}, bf16[448,1152]{1,0:T(8,128)(2,1)S(1)}, u32[]{:S(2)}, u32[]{:S(2)}) collective-permute-start(bf16[448,1152]{1,0:T(8,128)(2,1)} %collective-permute-done.5), channel_id=1, source_target_pairs={{0,224},{1,289},{2,226},{3,291},{4,228},{5,293},{6,230},{7,295},{8... | collective-permute-start | bytes 3096584 | tf_op jit(solution)/shard_map/ppermute | solution.py:26
  37.8 165.4 %collective-permute-start.4 = (bf16[448,1152]{1,0:T(8,128)(2,1)}, bf16[448,1152]{1,0:T(8,128)(2,1)S(1)}, u32[]{:S(2)}, u32[]{:S(2)}) collective-permute-start(bf16[448,1152]{1,0:T(8,128)(2,1)} %collective-permute-done.3), channel_id=1, source_target_pairs={{0,224},{1,289},{2,226},{3,291},{4,228},{5,293},{6,230},{7,295},{8... | collective-permute-start | bytes 3096584 | tf_op jit(solution)/shard_map/ppermute | solution.py:26
  53.7 15.9 %collective-permute-start = (bf16[464,1152]{1,0:T(8,128)(2,1)S(1)}, bf16[464,1152]{1,0:T(8,128)(2,1)}, u32[]{:S(2)}, u32[]{:S(2)}) collective-permute-start(bf16[464,1152]{1,0:T(8,128)(2,1)S(1)} %fusion.14.part), channel_id=1, source_target_pairs={{0,1},{1,0},{2,3},{3,2},{4,5},{5,4},{6,7},{7,6},{8,9},{9,8},{10,11... | collective-permute-start | bytes 3207176 | tf_op jit(solution)/shard_map/while/body/eval_jaxpr/ppermute | solution.py:19
  55.6 28.4 %collective-permute-start.1 = (bf16[464,1152]{1,0:T(8,128)(2,1)S(1)}, bf16[464,1152]{1,0:T(8,128)(2,1)}, u32[]{:S(2)}, u32[]{:S(2)}) collective-permute-start(bf16[464,1152]{1,0:T(8,128)(2,1)S(1)} %fusion.14.part), channel_id=1, source_target_pairs={{0,4},{4,0},{8,12},{12,8},{16,20},{20,16},{24,28},{28,24},{32,36},... | collective-permute-start | bytes 3207176 | tf_op jit(solution)/shard_map/while/body/eval_jaxpr/ppermute | solution.py:19
  58.1 49.4 %collective-permute-start.2 = (bf16[464,1152]{1,0:T(8,128)(2,1)S(1)}, bf16[464,1152]{1,0:T(8,128)(2,1)}, u32[]{:S(2)}, u32[]{:S(2)}) collective-permute-start(bf16[464,1152]{1,0:T(8,128)(2,1)S(1)} %fusion.14.part), channel_id=1, source_target_pairs={{0,8},{4,12},{8,0},{12,4},{16,24},{20,28},{24,16},{28,20},{32,40},... | collective-permute-start | bytes 3207176 | tf_op jit(solution)/shard_map/while/body/eval_jaxpr/ppermute | solution.py:19
  62.5 45.0 %copy-start.3 = (bf16[448,1152]{1,0:T(8,128)(2,1)S(1)}, bf16[448,1152]{1,0:T(8,128)(2,1)}, u32[]{:S(2)}) copy-start(bf16[448,1152]{1,0:T(8,128)(2,1)} %get-tuple-element.387.img) | copy-start | bytes 3096580 | tf_op jit(solution)/shard_map/while
  107.5 9.9 %copy-start.2 = (bf16[448,1152]{1,0:T(8,128)(2,1)S(1)}, bf16[448,1152]{1,0:T(8,128)(2,1)}, u32[]{:S(2)}) copy-start(bf16[448,1152]{1,0:T(8,128)(2,1)} %get-tuple-element.419) | copy-start | bytes 3096580 | tf_op jit(solution)/shard_map/while
  118.7 15.0 %collective-permute-start = (bf16[464,1152]{1,0:T(8,128)(2,1)S(1)}, bf16[464,1152]{1,0:T(8,128)(2,1)}, u32[]{:S(2)}, u32[]{:S(2)}) collective-permute-start(bf16[464,1152]{1,0:T(8,128)(2,1)S(1)} %fusion.14.part), channel_id=1, source_target_pairs={{0,1},{1,0},{2,3},{3,2},{4,5},{5,4},{6,7},{7,6},{8,9},{9,8},{10,11... | collective-permute-start | bytes 3207176 | tf_op jit(solution)/shard_map/while/body/eval_jaxpr/ppermute | solution.py:19
  120.6 28.4 %collective-permute-start.1 = (bf16[464,1152]{1,0:T(8,128)(2,1)S(1)}, bf16[464,1152]{1,0:T(8,128)(2,1)}, u32[]{:S(2)}, u32[]{:S(2)}) collective-permute-start(bf16[464,1152]{1,0:T(8,128)(2,1)S(1)} %fusion.14.part), channel_id=1, source_target_pairs={{0,4},{4,0},{8,12},{12,8},{16,20},{20,16},{24,28},{28,24},{32,36},... | collective-permute-start | bytes 3207176 | tf_op jit(solution)/shard_map/while/body/eval_jaxpr/ppermute | solution.py:19
  124.3 47.2 %collective-permute-start.2 = (bf16[464,1152]{1,0:T(8,128)(2,1)S(1)}, bf16[464,1152]{1,0:T(8,128)(2,1)}, u32[]{:S(2)}, u32[]{:S(2)}) collective-permute-start(bf16[464,1152]{1,0:T(8,128)(2,1)S(1)} %fusion.14.part), channel_id=1, source_target_pairs={{0,8},{4,12},{8,0},{12,4},{16,24},{20,28},{24,16},{28,20},{32,40},... | collective-permute-start | bytes 3207176 | tf_op jit(solution)/shard_map/while/body/eval_jaxpr/ppermute | solution.py:19
  126.5 45.0 %copy-start.3 = (bf16[448,1152]{1,0:T(8,128)(2,1)S(1)}, bf16[448,1152]{1,0:T(8,128)(2,1)}, u32[]{:S(2)}) copy-start(bf16[448,1152]{1,0:T(8,128)(2,1)} %get-tuple-element.387.img) | copy-start | bytes 3096580 | tf_op jit(solution)/shard_map/while
  171.5 9.9 %copy-start.2 = (bf16[448,1152]{1,0:T(8,128)(2,1)S(1)}, bf16[448,1152]{1,0:T(8,128)(2,1)}, u32[]{:S(2)}) copy-start(bf16[448,1152]{1,0:T(8,128)(2,1)} %get-tuple-element.419) | copy-start | bytes 3096580 | tf_op jit(solution)/shard_map/while
  181.4 21.8 %copy-start = (f32[448,1152]{1,0:T(8,128)S(1)}, f32[448,1152]{1,0:T(8,128)}, u32[]{:S(2)}) copy-start(f32[448,1152]{1,0:T(8,128)} %get-tuple-element.406) | copy-start | bytes 6193156

commit v7 on v5

--- a/solution.py
+++ b/solution.py
@@ -107,12 +107,12 @@
     acc = jax.ShapeDtypeStruct((count, width), jnp.float32)
     out = jax.ShapeDtypeStruct((count, width), jnp.bfloat16)
 
-    def kernel(body, out_shape, *args, passed=0, products=1):
+    def kernel(body, out_shape, *args, passed=0, products=0, last_stays=False):
         many = isinstance(out_shape, tuple)
         specs = [SMEM, SMEM] + [VMEM] * (len(args) - 2)
         out_specs = (VMEM,) * len(out_shape) if many else VMEM
         aliases = {len(args) - i: len(out_shape) - i for i in range(1, passed + 1)}
-        if products == 0:
+        if last_stays:
             specs[-1] = anywhere
             out_specs = out_specs[:-1] + (anywhere,)
         return pl.pallas_call(
@@ -137,10 +137,17 @@
     bases = jnp.bitwise_xor(myself, offsets) * count
     scalars = jnp.concatenate([jnp.exp(log_scale), bias])
     lab_col = labels.reshape(count, 1)
+    chunk = count // CHUNKS
     sums = (jnp.zeros((count, width), jnp.float32),) * 2
-    chunk = count // CHUNKS
+    nothing = (jnp.zeros((2 * chunk + DIGIT_ROWS, width), jnp.bfloat16),) * 3
 
-    def near(step, sums):
+    def meet(body, at, parts, sums, products):
+        here = jnp.concatenate([bases, jnp.reshape(at, (1,))])
+        args = (here, scalars, images, texts, lab_col, *parts, *sums)
+        return kernel(body, (acc, acc), *args, passed=2, products=products)
+
+    def near(step, state):
+        before, sums = state
         at = step * chunk
         part = jnp.concatenate(
             [
@@ -153,15 +160,16 @@
             axis=0,
         )
         arrived = [from_partner(part, axis, bit) for axis, bit in (("dp", 1), ("dp", 0), ("pair", 0))]
-        here = jnp.concatenate([bases, jnp.reshape(at, (1,))])
-        mine = (here, scalars, images, texts, lab_col)
-        sums = kernel(own_kernel, (acc, acc), *mine, part, *sums, passed=2, products=2)
-        return kernel(near_kernel, (acc, acc), *mine, *arrived[::-1], *sums, passed=2, products=3)
+        sums = meet(own_kernel, at, (part,), sums, 1)
+        sums = meet(near_kernel, at - chunk, before, sums, 3)
+        return tuple(arrived[::-1]), tuple(sums)
 
-    img_acc, txt_acc = lax.fori_loop(0, CHUNKS, near, sums)
+    arrived, sums = lax.fori_loop(0, CHUNKS, near, (nothing, sums))
+    img_acc, txt_acc = meet(near_kernel, jnp.int32((CHUNKS - 1) * chunk), arrived, sums, 0)
     image_grad = kernel(far_texts_kernel, out, scalars, bases, images, lab_col, far_txt, img_acc)
     text_grad, image_grad = kernel(
-        far_images_kernel, (out, out), scalars, bases, texts, far_img, far_lab, txt_acc, image_grad, passed=1, products=0
+        far_images_kernel, (out, out), scalars, bases, texts, far_img, far_lab, txt_acc, image_grad,
+        passed=1, last_stays=True,
     )
     return image_grad, text_grad
 

time: 198 us -> 198 us (level)
  the two profiles are of different devices: /device:TPU:33 before, /device:TPU:37 now
where the time goes in v7:
time: 198 us; the launch traced here: 197 us
  starting transfers between devices  62 us (31%)
  waiting for transfers between devices  58.1 us (29%)
  Pallas kernels  49.8 us (25%)
  local copies, waits for them, and re-layouts  23.9 us (12%)
  between operations  2.09 us (1%)
    ppermute x7, waiting for transfers between devices, from_partner(): return lax.ppermute(block, axis, [(i, i ^ 1 << bit) for i in range(count)])  57.7 us
    pallas_call x7, Pallas kernels, kernel(): pl.pallas_call(body, out_shape=out_shape, in_specs=specs, out_specs=out_s...  49.8 us
    ppermute x4, starting transfers between devices, along_ring(): lax.ppermute(block, axes, [(i, (i + (step if i % 2 == 0 else -step)) % co...  37.8 us
    ppermute x7, starting transfers between devices, from_partner(): return lax.ppermute(block, axis, [(i, i ^ 1 << bit) for i in range(count)])  24.2 us
    while x26, local copies, waits for them, and re-layouts  14.4 us
  transfers between devices with their start and end apart: 11, of which 6 were waited for; matrix products, arithmetic and copies ran while one was open for 13% of the time, Pallas kernels for 24%

profile of v7, /device:TPU:37, one launch (start us, length us, event | category | flops | bytes accessed | tf_op | source)
XLA Modules:
  0.0 197.2 jit_solution(4069126548036420624)
XLA Ops:
  0.6 1.9 collective-permute-start.6
  2.6 10.9 %collective-permute-start.3 = (bf16[448,1152]{1,0:T(8,128)(2,1)}, bf16[448,1152]{1,0:T(8,128)(2,1)}, u32[]{:S(2)}, u32[]{:S(2)}) collective-permute-start(bf16[448,1152]{1,0:T(8,128)(2,1)} %img.3), channel_id=1, source_target_pairs={{0,32},{1,481},{2,34},{3,483},{4,36},{5,485},{6,38},{7,487},{8,40}... | collective-permute-start | bytes 3096584 | tf_op jit(solution)/shard_map/ppermute | solution.py:26
  13.5 0.7 and_convert_fusion.1
  15.6 0.8 copy.16.lab_col
  16.4 0.1 pad_maximum_fusion.scalars
  16.5 0.3 collective-permute-done.6
  16.8 13.9 %collective-permute-start.7 = (bf16[448,1152]{1,0:T(8,128)(2,1)}, bf16[448,1152]{1,0:T(8,128)(2,1)S(1)}, u32[]{:S(2)}, u32[]{:S(2)}) collective-permute-start(bf16[448,1152]{1,0:T(8,128)(2,1)} %collective-permute-done.6), channel_id=1, source_target_pairs={{0,224},{1,289},{2,226},{3,291},{4,228},{5,293},{6,230},{7,295},{8... | collective-permute-start | bytes 3096584 | tf_op jit(solution)/shard_map/ppermute | solution.py:26
  30.7 0.0 collective-permute-done.3
  30.7 11.0 %collective-permute-start.4 = (bf16[448,1152]{1,0:T(8,128)(2,1)}, bf16[448,1152]{1,0:T(8,128)(2,1)S(1)}, u32[]{:S(2)}, u32[]{:S(2)}) collective-permute-start(bf16[448,1152]{1,0:T(8,128)(2,1)} %collective-permute-done.3), channel_id=1, source_target_pairs={{0,224},{1,289},{2,226},{3,291},{4,228},{5,293},{6,230},{7,295},{8... | collective-permute-start | bytes 3096584 | tf_op jit(solution)/shard_map/ppermute | solution.py:26
  41.8 1.5 broadcast_in_dim.7
  43.2 1.4 broadcast_in_dim.7.clone
  44.7 1.2 broadcast_in_dim.6
  45.8 1.1 broadcast_in_dim.6.clone
  46.9 1.1 broadcast_in_dim.6.clone.1
  48.0 0.0 copy-done.1
  48.0 0.0 copy-done.10
  48.1 118.9 %while.24 = (s32[]{:T(128)}, bf16[464,1152]{1,0:T(8,128)(2,1)}, bf16[464,1152]{1,0:T(8,128)(2,1)}, bf16[464,1152]{1,0:T(8,128)(2,1)}, f32[448,1152]{1,0:T(8,128)...) while((s32[]{:T(128)}, bf16[464,1152]{1,0:T(8,128)(2,1)}, ...), condition=%wide.region_1.2_spmd.clone, body=%wide.region_0.1_spmd.clone.sunk | while | flops 3703652352 | bytes 56903308 | solution.py:167
  48.1 0.1 constant_dynamic-slice_fusion.5
  48.2 1.1 constant_dynamic-slice_fusion.6
  49.3 0.1 fusion.14.part
  49.4 7.4 %collective-permute-start = (bf16[464,1152]{1,0:T(8,128)(2,1)S(1)}, bf16[464,1152]{1,0:T(8,128)(2,1)}, u32[]{:S(2)}, u32[]{:S(2)}) collective-permute-start(bf16[464,1152]{1,0:T(8,128)(2,1)S(1)} %fusion.14.part), channel_id=1, source_target_pairs={{0,1},{1,0},{2,3},{3,2},{4,5},{5,4},{6,7},{7,6},{8,9},{9,8},{10,11... | collective-permute-start | bytes 3207176 | tf_op jit(solution)/shard_map/while/body/eval_jaxpr/ppermute | solution.py:19
  56.8 2.8 %collective-permute-start.1 = (bf16[464,1152]{1,0:T(8,128)(2,1)S(1)}, bf16[464,1152]{1,0:T(8,128)(2,1)}, u32[]{:S(2)}, u32[]{:S(2)}) collective-permute-start(bf16[464,1152]{1,0:T(8,128)(2,1)S(1)} %fusion.14.part), channel_id=1, source_target_pairs={{0,4},{4,0},{8,12},{12,8},{16,20},{20,16},{24,28},{28,24},{32,36},... | collective-permute-start | bytes 3207176 | tf_op jit(solution)/shard_map/while/body/eval_jaxpr/ppermute | solution.py:19
  59.6 2.4 %collective-permute-start.2 = (bf16[464,1152]{1,0:T(8,128)(2,1)S(1)}, bf16[464,1152]{1,0:T(8,128)(2,1)}, u32[]{:S(2)}, u32[]{:S(2)}) collective-permute-start(bf16[464,1152]{1,0:T(8,128)(2,1)S(1)} %fusion.14.part), channel_id=1, source_target_pairs={{0,8},{4,12},{8,0},{12,4},{16,24},{20,28},{24,16},{28,20},{32,40},... | collective-permute-start | bytes 3207176 | tf_op jit(solution)/shard_map/while/body/eval_jaxpr/ppermute | solution.py:19
  62.0 0.1 pad_add_fusion.4
  62.1 7.1 %own_kernel.8 = (f32[448,1152]{1,0:T(8,128)}, f32[448,1152]{1,0:T(8,128)}) custom-call(s32[6]{0:T(128)S(1)} %get-tuple-element.455.bases, f32[2]{0:T(128)S(1)} %get-tuple-element.507.scalars, bf16[448,1152]{1,0:T(8,128)(2,1)} %get-tuple-element.543, bf16[448,1152]{1,0:T(8,128)(2,1)} %get-tuple-element.504.txt, ...), custom_call_target="tpu_custom_call", output_to_operand_aliasing={{1}: (7, {}), {0}: (6, {})} | custom-call | flops 924844032 | bytes 3096576 | tf_op jit(solution)/shard_map/while/body/eval_jaxpr/own_kernel/pallas_call | solution.py:118
  69.3 0.0 copy-done.3
  69.3 0.0 copy-done.5
  69.3 0.0 copy-done.6
  69.3 0.0 copy-done.7
  69.3 9.2 %near_kernel.10 = (f32[448,1152]{1,0:T(8,128)}, f32[448,1152]{1,0:T(8,128)}) custom-call(s32[6]{0:T(128)S(1)} %get-tuple-element.454.bases, f32[2]{0:T(128)S(1)} %get-tuple-element.507.scalars, bf16[448,1152]{1,0:T(8,128)(2,1)} %get-tuple-element.543, bf16[448,1152]{1,0:T(8,128)(2,1)S(1)} %copy-done.3, ...), custom_call_target="tpu_custom_call", output_to_operand_aliasing={{1}: (9, {}), {0}: (8, {})} | custom-call | flops 2774532096 | bytes 9289728 | tf_op jit(solution)/shard_map/while/body/eval_jaxpr/near_kernel/pallas_call | solution.py:118
  78.5 0.0 collective-permute-done
  78.5 2.4 %copy.35 = bf16[464,1152]{1,0:T(8,128)(2,1)} copy(bf16[464,1152]{1,0:T(8,128)(2,1)} %collective-permute-done) | data formatting | bytes 2138112 | tf_op jit(solution)/shard_map/while
  80.9 3.0 %collective-permute-done.1 = bf16[464,1152]{1,0:T(8,128)(2,1)} collective-permute-done((bf16[464,1152]{1,0:T(8,128)(2,1)S(1)}, bf16[464,1152]{1,0:T(8,128)(2,1)}, u32[]{:S(2)}, u32[]{:S(2)}) %collective-permute-start.1) | collective-permute-done | bytes 1069088 | tf_op jit(solution)/shard_map/while/body/eval_jaxpr/ppermute | solution.py:19
  84.0 2.4 %copy.36 = bf16[464,1152]{1,0:T(8,128)(2,1)} copy(bf16[464,1152]{1,0:T(8,128)(2,1)} %collective-permute-done.1) | data formatting | bytes 2138112 | tf_op jit(solution)/shard_map/while
  86.3 20.5 %collective-permute-done.2 = bf16[464,1152]{1,0:T(8,128)(2,1)} collective-permute-done((bf16[464,1152]{1,0:T(8,128)(2,1)S(1)}, bf16[464,1152]{1,0:T(8,128)(2,1)}, u32[]{:S(2)}, u32[]{:S(2)}) %collective-permute-start.2) | collective-permute-done | bytes 1069088 | tf_op jit(solution)/shard_map/while/body/eval_jaxpr/ppermute | solution.py:19
  106.9 2.4 %copy.37 = bf16[464,1152]{1,0:T(8,128)(2,1)} copy(bf16[464,1152]{1,0:T(8,128)(2,1)} %collective-permute-done.2) | data formatting | bytes 2138112 | tf_op jit(solution)/shard_map/while
  109.3 0.0 copy-done.2
  109.3 0.1 constant_dynamic-slice_fusion.5
  109.4 1.1 constant_dynamic-slice_fusion.6
  110.5 0.1 fusion.14.part
  110.6 2.7 %collective-permute-start = (bf16[464,1152]{1,0:T(8,128)(2,1)S(1)}, bf16[464,1152]{1,0:T(8,128)(2,1)}, u32[]{:S(2)}, u32[]{:S(2)}) collective-permute-start(bf16[464,1152]{1,0:T(8,128)(2,1)S(1)} %fusion.14.part), channel_id=1, source_target_pairs={{0,1},{1,0},{2,3},{3,2},{4,5},{5,4},{6,7},{7,6},{8,9},{9,8},{10,11... | collective-permute-start | bytes 3207176 | tf_op jit(solution)/shard_map/while/body/eval_jaxpr/ppermute | solution.py:19
  113.3 2.8 %collective-permute-start.1 = (bf16[464,1152]{1,0:T(8,128)(2,1)S(1)}, bf16[464,1152]{1,0:T(8,128)(2,1)}, u32[]{:S(2)}, u32[]{:S(2)}) collective-permute-start(bf16[464,1152]{1,0:T(8,128)(2,1)S(1)} %fusion.14.part), channel_id=1, source_target_pairs={{0,4},{4,0},{8,12},{12,8},{16,20},{20,16},{24,28},{28,24},{32,36},... | collective-permute-start | bytes 3207176 | tf_op jit(solution)/shard_map/while/body/eval_jaxpr/ppermute | solution.py:19
  116.1 3.5 %collective-permute-start.2 = (bf16[464,1152]{1,0:T(8,128)(2,1)S(1)}, bf16[464,1152]{1,0:T(8,128)(2,1)}, u32[]{:S(2)}, u32[]{:S(2)}) collective-permute-start(bf16[464,1152]{1,0:T(8,128)(2,1)S(1)} %fusion.14.part), channel_id=1, source_target_pairs={{0,8},{4,12},{8,0},{12,4},{16,24},{20,28},{24,16},{28,20},{32,40},... | collective-permute-start | bytes 3207176 | tf_op jit(solution)/shard_map/while/body/eval_jaxpr/ppermute | solution.py:19
  119.6 0.1 pad_add_fusion.4
  119.7 7.1 %own_kernel.8 = (f32[448,1152]{1,0:T(8,128)}, f32[448,1152]{1,0:T(8,128)}) custom-call(s32[6]{0:T(128)S(1)} %get-tuple-element.455.bases, f32[2]{0:T(128)S(1)} %get-tuple-element.507.scalars, bf16[448,1152]{1,0:T(8,128)(2,1)} %get-tuple-element.543, bf16[448,1152]{1,0:T(8,128)(2,1)} %get-tuple-element.504.txt, ...), custom_call_target="tpu_custom_call", output_to_operand_aliasing={{1}: (7, {}), {0}: (6, {})} | custom-call | flops 924844032 | bytes 3096576 | tf_op jit(solution)/shard_map/while/body/eval_jaxpr/own_kernel/pallas_call | solution.py:118
  126.9 9.2 %near_kernel.10 = (f32[448,1152]{1,0:T(8,128)}, f32[448,1152]{1,0:T(8,128)}) custom-call(s32[6]{0:T(128)S(1)} %get-tuple-element.454.bases, f32[2]{0:T(128)S(1)} %get-tuple-element.507.scalars, bf16[448,1152]{1,0:T(8,128)(2,1)} %get-tuple-element.543, bf16[448,1152]{1,0:T(8,128)(2,1)S(1)} %copy-done.3, ...), custom_call_target="tpu_custom_call", output_to_operand_aliasing={{1}: (9, {}), {0}: (8, {})} | custom-call | flops 2774532096 | bytes 9289728 | tf_op jit(solution)/shard_map/while/body/eval_jaxpr/near_kernel/pallas_call | solution.py:118
  136.1 0.0 collective-permute-done
  136.1 2.4 %copy.35 = bf16[464,1152]{1,0:T(8,128)(2,1)} copy(bf16[464,1152]{1,0:T(8,128)(2,1)} %collective-permute-done) | data formatting | bytes 2138112 | tf_op jit(solution)/shard_map/while
  138.5 2.0 %collective-permute-done.1 = bf16[464,1152]{1,0:T(8,128)(2,1)} collective-permute-done((bf16[464,1152]{1,0:T(8,128)(2,1)S(1)}, bf16[464,1152]{1,0:T(8,128)(2,1)}, u32[]{:S(2)}, u32[]{:S(2)}) %collective-permute-start.1) | collective-permute-done | bytes 1069088 | tf_op jit(solution)/shard_map/while/body/eval_jaxpr/ppermute | solution.py:19
  140.5 2.4 %copy.36 = bf16[464,1152]{1,0:T(8,128)(2,1)} copy(bf16[464,1152]{1,0:T(8,128)(2,1)} %collective-permute-done.1) | data formatting | bytes 2138112 | tf_op jit(solution)/shard_map/while
  142.9 21.6 %collective-permute-done.2 = bf16[464,1152]{1,0:T(8,128)(2,1)} collective-permute-done((bf16[464,1152]{1,0:T(8,128)(2,1)S(1)}, bf16[464,1152]{1,0:T(8,128)(2,1)}, u32[]{:S(2)}, u32[]{:S(2)}) %collective-permute-start.2) | collective-permute-done | bytes 1069088 | tf_op jit(solution)/shard_map/while/body/eval_jaxpr/ppermute | solution.py:19
  164.5 2.4 %copy.37 = bf16[464,1152]{1,0:T(8,128)(2,1)} copy(bf16[464,1152]{1,0:T(8,128)(2,1)} %collective-permute-done.2) | data formatting | bytes 2138112 | tf_op jit(solution)/shard_map/while
  166.9 0.0 copy-done.2
  166.9 2.5 %collective-permute-start.5 = (s32[1,448]{1,0:T(1,128)S(1)}, s32[1,448]{1,0:T(1,128)S(1)}, u32[]{:S(2)}, u32[]{:S(2)}) collective-permute-start(s32[1,448]{1,0:T(1,128)S(1)} %bitcast.9), channel_id=1, source_target_pairs={{0,256},{4,260},{8,264},{12,268},{16,272},{20,276},{24,280},{28,28... | collective-permute-start | bytes 5384 | tf_op jit(solution)/shard_map/ppermute | solution.py:19
  169.5 0.0 copy-done.9
  169.5 0.1 pad_add_fusion.2.bases
  169.6 9.8 %near_kernel.9 = (f32[448,1152]{1,0:T(8,128)}, f32[448,1152]{1,0:T(8,128)}) custom-call(s32[6]{0:T(128)S(1)} %pad_add_fusion.2.bases, f32[2]{0:T(128)S(1)} %get-tuple-element.533, bf16[448,1152]{1,0:T(8,128)(2,1)S(1)} %get-tuple-element.531, bf16[448,1152]{1,0:T(8,128)(2,1)} %get-tuple-element.530, ...), custom_call_target="tpu_custom_call", output_to_operand_aliasing={{1}: (9, {}), {0}: (8, {})} | custom-call | tf_op jit(solution)/shard_map/near_kernel/pallas_call | solution.py:118
  179.4 0.0 collective-permute-done.7.far_txt
  179.4 0.0 copy-start.4
  179.4 4.2 %far_texts_kernel.1.image_grad = bf16[448,1152]{1,0:T(8,128)(2,1)} custom-call(f32[2]{0:T(128)S(1)} %get-tuple-element.533, s32[5]{0:T(128)S(1)} %xor_multiply_fusion.1.bases, bf16[448,1152]{1,0:T(8,128)(2,1)S(1)} %get-tuple-element.531, s32[448,1]{1,0:T(8,128)S(1)} %get-tuple-element.534, bf16[448,1152]{1,0:T(8,128)(2,1)S(1)} %collective-permute-done.7.far_txt, ...), custom_call_target="tpu_custom_call" | custom-call | tf_op jit(solution)/shard_map/far_texts_kernel/pallas_call | solution.py:118
  183.6 10.5 %collective-permute-done.5.far_lab = s32[1,448]{1,0:T(1,128)S(1)} collective-permute-done((s32[1,448]{1,0:T(1,128)S(1)}, s32[1,448]{1,0:T(1,128)S(1)}, u32[]{:S(2)}, u32[]{:S(2)}) %collective-permute-start.5) | collective-permute-done | bytes 1824 | tf_op jit(solution)/shard_map/ppermute | solution.py:19
  194.1 0.0 collective-permute-done.4.far_img
  194.1 0.0 copy-done.4
  194.1 3.0 %far_images_kernel.1 = (bf16[448,1152]{1,0:T(8,128)(2,1)}, bf16[448,1152]{1,0:T(8,128)(2,1)}) custom-call(f32[2]{0:T(128)S(1)} %get-tuple-element.533, s32[5]{0:T(128)S(1)} %xor_multiply_fusion.1.bases, bf16[448,1152]{1,0:T(8,128)(2,1)S(1)} %copy-done.4, bf16[448,1152]{1,0:T(8,128)(2,1)S(1)} %collective-permute-done.4.far_img, ...), custom_call_target="tpu_custom_call", output_to_operand_aliasing={{1}: (6, {})} | custom-call | tf_op jit(solution)/shard_map/far_images_kernel/pallas_call | solution.py:118
  (28 shorter events, 0.1 us)
Async XLA Ops:
  0.6 16.2 %collective-permute-start.6 = (bf16[448,1152]{1,0:T(8,128)(2,1)}, bf16[448,1152]{1,0:T(8,128)(2,1)}, u32[]{:S(2)}, u32[]{:S(2)}) collective-permute-start(bf16[448,1152]{1,0:T(8,128)(2,1)} %txt.3), channel_id=1, source_target_pairs={{0,32},{1,481},{2,34},{3,483},{4,36},{5,485},{6,38},{7,487},{8,40}... | collective-permute-start | bytes 3096584 | tf_op jit(solution)/shard_map/ppermute | solution.py:26
  2.6 28.1 %collective-permute-start.3 = (bf16[448,1152]{1,0:T(8,128)(2,1)}, bf16[448,1152]{1,0:T(8,128)(2,1)}, u32[]{:S(2)}, u32[]{:S(2)}) collective-permute-start(bf16[448,1152]{1,0:T(8,128)(2,1)} %img.3), channel_id=1, source_target_pairs={{0,32},{1,481},{2,34},{3,483},{4,36},{5,485},{6,38},{7,487},{8,40}... | collective-permute-start | bytes 3096584 | tf_op jit(solution)/shard_map/ppermute | solution.py:26
  16.8 162.6 %collective-permute-start.7 = (bf16[448,1152]{1,0:T(8,128)(2,1)}, bf16[448,1152]{1,0:T(8,128)(2,1)S(1)}, u32[]{:S(2)}, u32[]{:S(2)}) collective-permute-start(bf16[448,1152]{1,0:T(8,128)(2,1)} %collective-permute-done.6), channel_id=1, source_target_pairs={{0,224},{1,289},{2,226},{3,291},{4,228},{5,293},{6,230},{7,295},{8... | collective-permute-start | bytes 3096584 | tf_op jit(solution)/shard_map/ppermute | solution.py:26
  30.7 163.4 %collective-permute-start.4 = (bf16[448,1152]{1,0:T(8,128)(2,1)}, bf16[448,1152]{1,0:T(8,128)(2,1)S(1)}, u32[]{:S(2)}, u32[]{:S(2)}) collective-permute-start(bf16[448,1152]{1,0:T(8,128)(2,1)} %collective-permute-done.3), channel_id=1, source_target_pairs={{0,224},{1,289},{2,226},{3,291},{4,228},{5,293},{6,230},{7,295},{8... | collective-permute-start | bytes 3096584 | tf_op jit(solution)/shard_map/ppermute | solution.py:26
  45.8 2.2 %copy-start.1 = (bf16[448,1152]{1,0:T(8,128)(2,1)S(1)}, bf16[448,1152]{1,0:T(8,128)(2,1)}, u32[]{:S(2)}) copy-start(bf16[448,1152]{1,0:T(8,128)(2,1)} %img.3) | copy-start | bytes 3096580
  45.8 2.2 %copy-start.10 = (s32[5]{0:T(128)S(1)}, s32[5]{0:T(128)}, u32[]{:S(2)}) copy-start(s32[5]{0:T(128)} %constant.86.clone.5) | copy-start | bytes 64
  48.1 118.9 %copy-start.8 = (s32[448]{0:T(512)S(1)}, s32[448]{0:T(512)}, u32[]{:S(2)}) copy-start(s32[448]{0:T(512)} %param.10) | copy-start | bytes 5380
  48.1 121.4 %copy-start.9 = (s32[5]{0:T(128)S(1)}, s32[5]{0:T(128)}, u32[]{:S(2)}) copy-start(s32[5]{0:T(128)} %constant.86.clone) | copy-start | bytes 64
  49.4 29.1 %collective-permute-start = (bf16[464,1152]{1,0:T(8,128)(2,1)S(1)}, bf16[464,1152]{1,0:T(8,128)(2,1)}, u32[]{:S(2)}, u32[]{:S(2)}) collective-permute-start(bf16[464,1152]{1,0:T(8,128)(2,1)S(1)} %fusion.14.part), channel_id=1, source_target_pairs={{0,1},{1,0},{2,3},{3,2},{4,5},{5,4},{6,7},{7,6},{8,9},{9,8},{10,11... | collective-permute-start | bytes 3207176 | tf_op jit(solution)/shard_map/while/body/eval_jaxpr/ppermute | solution.py:19
  56.8 27.2 %collective-permute-start.1 = (bf16[464,1152]{1,0:T(8,128)(2,1)S(1)}, bf16[464,1152]{1,0:T(8,128)(2,1)}, u32[]{:S(2)}, u32[]{:S(2)}) collective-permute-start(bf16[464,1152]{1,0:T(8,128)(2,1)S(1)} %fusion.14.part), channel_id=1, source_target_pairs={{0,4},{4,0},{8,12},{12,8},{16,20},{20,16},{24,28},{28,24},{32,36},... | collective-permute-start | bytes 3207176 | tf_op jit(solution)/shard_map/while/body/eval_jaxpr/ppermute | solution.py:19
  59.6 47.3 %collective-permute-start.2 = (bf16[464,1152]{1,0:T(8,128)(2,1)S(1)}, bf16[464,1152]{1,0:T(8,128)(2,1)}, u32[]{:S(2)}, u32[]{:S(2)}) collective-permute-start(bf16[464,1152]{1,0:T(8,128)(2,1)S(1)} %fusion.14.part), channel_id=1, source_target_pairs={{0,8},{4,12},{8,0},{12,4},{16,24},{20,28},{24,16},{28,20},{32,40},... | collective-permute-start | bytes 3207176 | tf_op jit(solution)/shard_map/while/body/eval_jaxpr/ppermute | solution.py:19
  62.1 7.1 %copy-start.3 = (bf16[448,1152]{1,0:T(8,128)(2,1)S(1)}, bf16[448,1152]{1,0:T(8,128)(2,1)}, u32[]{:S(2)}) copy-start(bf16[448,1152]{1,0:T(8,128)(2,1)} %get-tuple-element.504.txt) | copy-start | bytes 3096580 | tf_op jit(solution)/shard_map/while
  62.1 7.1 %copy-start.5 = (bf16[464,1152]{1,0:T(8,128)(2,1)S(1)}, bf16[464,1152]{1,0:T(8,128)(2,1)}, u32[]{:S(2)}) copy-start(bf16[464,1152]{1,0:T(8,128)(2,1)} %get-tuple-element.480.near1) | copy-start | bytes 3207172 | tf_op jit(solution)/shard_map/while
  62.1 7.2 %copy-start.6 = (bf16[464,1152]{1,0:T(8,128)(2,1)S(1)}, bf16[464,1152]{1,0:T(8,128)(2,1)}, u32[]{:S(2)}) copy-start(bf16[464,1152]{1,0:T(8,128)(2,1)} %get-tuple-element.481.near2) | copy-start | bytes 3207172 | tf_op jit(solution)/shard_map/while
  62.1 7.2 %copy-start.7 = (bf16[464,1152]{1,0:T(8,128)(2,1)S(1)}, bf16[464,1152]{1,0:T(8,128)(2,1)}, u32[]{:S(2)}) copy-start(bf16[464,1152]{1,0:T(8,128)(2,1)} %get-tuple-element.482.near3) | copy-start | bytes 3207172 | tf_op jit(solution)/shard_map/while
  106.9 2.4 %copy-start.2 = (bf16[448,1152]{1,0:T(8,128)(2,1)S(1)}, bf16[448,1152]{1,0:T(8,128)(2,1)}, u32[]{:S(2)}) copy-start(bf16[448,1152]{1,0:T(8,128)(2,1)} %get-tuple-element.543) | copy-start | bytes 3096580 | tf_op jit(solution)/shard_map/while
  110.6 25.5 %collective-permute-start = (bf16[464,1152]{1,0:T(8,128)(2,1)S(1)}, bf16[464,1152]{1,0:T(8,128)(2,1)}, u32[]{:S(2)}, u32[]{:S(2)}) collective-permute-start(bf16[464,1152]{1,0:T(8,128)(2,1)S(1)} %fusion.14.part), channel_id=1, source_target_pairs={{0,1},{1,0},{2,3},{3,2},{4,5},{5,4},{6,7},{7,6},{8,9},{9,8},{10,11... | collective-permute-start | bytes 3207176 | tf_op jit(solution)/shard_map/while/body/eval_jaxpr/ppermute | solution.py:19
  113.3 27.2 %collective-permute-start.1 = (bf16[464,1152]{1,0:T(8,128)(2,1)S(1)}, bf16[464,1152]{1,0:T(8,128)(2,1)}, u32[]{:S(2)}, u32[]{:S(2)}) collective-permute-start(bf16[464,1152]{1,0:T(8,128)(2,1)S(1)} %fusion.14.part), channel_id=1, source_target_pairs={{0,4},{4,0},{8,12},{12,8},{16,20},{20,16},{24,28},{28,24},{32,36},... | collective-permute-start | bytes 3207176 | tf_op jit(solution)/shard_map/while/body/eval_jaxpr/ppermute | solution.py:19
  116.1 48.4 %collective-permute-start.2 = (bf16[464,1152]{1,0:T(8,128)(2,1)S(1)}, bf16[464,1152]{1,0:T(8,128)(2,1)}, u32[]{:S(2)}, u32[]{:S(2)}) collective-permute-start(bf16[464,1152]{1,0:T(8,128)(2,1)S(1)} %fusion.14.part), channel_id=1, source_target_pairs={{0,8},{4,12},{8,0},{12,4},{16,24},{20,28},{24,16},{28,20},{32,40},... | collective-permute-start | bytes 3207176 | tf_op jit(solution)/shard_map/while/body/eval_jaxpr/ppermute | solution.py:19
  119.7 7.1 %copy-start.3 = (bf16[448,1152]{1,0:T(8,128)(2,1)S(1)}, bf16[448,1152]{1,0:T(8,128)(2,1)}, u32[]{:S(2)}) copy-start(bf16[448,1152]{1,0:T(8,128)(2,1)} %get-tuple-element.504.txt) | copy-start | bytes 3096580 | tf_op jit(solution)/shard_map/while
  119.7 7.1 %copy-start.5 = (bf16[464,1152]{1,0:T(8,128)(2,1)S(1)}, bf16[464,1152]{1,0:T(8,128)(2,1)}, u32[]{:S(2)}) copy-start(bf16[464,1152]{1,0:T(8,128)(2,1)} %get-tuple-element.480.near1) | copy-start | bytes 3207172 | tf_op jit(solution)/shard_map/while
  119.7 7.2 %copy-start.6 = (bf16[464,1152]{1,0:T(8,128)(2,1)S(1)}, bf16[464,1152]{1,0:T(8,128)(2,1)}, u32[]{:S(2)}) copy-start(bf16[464,1152]{1,0:T(8,128)(2,1)} %get-tuple-element.481.near2) | copy-start | bytes 3207172 | tf_op jit(solution)/shard_map/while
  119.7 7.2 %copy-start.7 = (bf16[464,1152]{1,0:T(8,128)(2,1)S(1)}, bf16[464,1152]{1,0:T(8,128)(2,1)}, u32[]{:S(2)}) copy-start(bf16[464,1152]{1,0:T(8,128)(2,1)} %get-tuple-element.482.near3) | copy-start | bytes 3207172 | tf_op jit(solution)/shard_map/while
  164.5 2.4 %copy-start.2 = (bf16[448,1152]{1,0:T(8,128)(2,1)S(1)}, bf16[448,1152]{1,0:T(8,128)(2,1)}, u32[]{:S(2)}) copy-start(bf16[448,1152]{1,0:T(8,128)(2,1)} %get-tuple-element.543) | copy-start | bytes 3096580 | tf_op jit(solution)/shard_map/while
  166.9 27.2 %collective-permute-start.5 = (s32[1,448]{1,0:T(1,128)S(1)}, s32[1,448]{1,0:T(1,128)S(1)}, u32[]{:S(2)}, u32[]{:S(2)}) collective-permute-start(s32[1,448]{1,0:T(1,128)S(1)} %bitcast.9), channel_id=1, source_target_pairs={{0,256},{4,260},{8,264},{12,268},{16,272},{20,276},{24,280},{28,28... | collective-permute-start | bytes 5384 | tf_op jit(solution)/shard_map/ppermute | solution.py:19
  179.4 14.7 %copy-start = (f32[448,1152]{1,0:T(8,128)S(1)}, f32[448,1152]{1,0:T(8,128)}, u32[]{:S(2)}) copy-start(f32[448,1152]{1,0:T(8,128)} %get-tuple-element.293.txt_in) | copy-start | bytes 6193156
  179.4 14.7 %copy-start.4 = (bf16[448,1152]{1,0:T(8,128)(2,1)S(1)}, bf16[448,1152]{1,0:T(8,128)(2,1)}, u32[]{:S(2)}) copy-start(bf16[448,1152]{1,0:T(8,128)(2,1)} %get-tuple-element.530) | copy-start | bytes 3096580

commit v8 on v7

--- a/solution.py
+++ b/solution.py
@@ -70,6 +70,10 @@
         txt_total += gradient(txt[...], part[chunk : 2 * chunk, :], hit, scale, shift)
     img_out[...] = img_total
     txt_out[...] = txt_total
+
+
+def pass_kernel(scalars, bases, txt_in, nearly_img, out):
+    pass
 
 
 def far_texts_kernel(scalars, bases, img, lab_col, far_txt, img_in, image_grad):
@@ -130,7 +134,7 @@
     digits = jnp.pad(digits, ((0, DIGIT_ROWS - 3), (0, width - count)))
     second = RING // 2 - FIRST_STEPS
     far_txt = along_ring(along_ring(texts, FIRST_STEPS), second)
-    far_img = along_ring(along_ring(images, FIRST_STEPS), second)
+    nearly_img = along_ring(images, second)
     far_lab = from_partner(labels.reshape(1, count), "dp", far)
 
     offsets = jnp.array([0, 1, pair_size, 2 * pair_size, pair_size << far], jnp.int32)
@@ -165,6 +169,18 @@
         return tuple(arrived[::-1]), tuple(sums)
 
     arrived, sums = lax.fori_loop(0, CHUNKS, near, (nothing, sums))
+    anywhere_in = [SMEM, SMEM, anywhere, anywhere]
+    nearly_img = pl.pallas_call(
+        pass_kernel,
+        out_shape=out,
+        in_specs=anywhere_in,
+        out_specs=anywhere,
+        input_output_aliases={3: 0},
+        compiler_params=params,
+        cost_estimate=cost(0, count, width),
+        name="pass_kernel",
+    )(scalars, bases, sums[1], nearly_img)
+    far_img = along_ring(nearly_img, FIRST_STEPS)
     img_acc, txt_acc = meet(near_kernel, jnp.int32((CHUNKS - 1) * chunk), arrived, sums, 0)
     image_grad = kernel(far_texts_kernel, out, scalars, bases, images, lab_col, far_txt, img_acc)
     text_grad, image_grad = kernel(

time: 198 us -> 200 us (1.010)
  the two profiles are of different devices: /device:TPU:37 before, /device:TPU:8 now
where the time goes in v8:
time: 200 us; the launch traced here: 199 us
  waiting for transfers between devices  70.9 us (35%)
  starting transfers between devices  53.7 us (27%)
  Pallas kernels  46.6 us (23%)
  local copies, waits for them, and re-layouts  24 us (12%)
  between operations  2.09 us (1%)
    ppermute x7, waiting for transfers between devices, from_partner(): return lax.ppermute(block, axis, [(i, i ^ 1 << bit) for i in range(count)])  62.5 us
    pallas_call x7, Pallas kernels, kernel(): pl.pallas_call(body, out_shape=out_shape, in_specs=specs, out_specs=out_s...  46.1 us
    ppermute x4, starting transfers between devices, along_ring(): lax.ppermute(block, axes, [(i, (i + (step if i % 2 == 0 else -step)) % co...  31.4 us
    ppermute x7, starting transfers between devices, from_partner(): return lax.ppermute(block, axis, [(i, i ^ 1 << bit) for i in range(count)])  22.3 us
    while x26, local copies, waits for them, and re-layouts  14.4 us
    ppermute x4, waiting for transfers between devices, along_ring(): lax.ppermute(block, axes, [(i, (i + (step if i % 2 == 0 else -step)) % co...  8.37 us
  transfers between devices with their start and end apart: 11, of which 7 were waited for; matrix products, arithmetic and copies ran while one was open for 13% of the time, Pallas kernels for 22%

profile of v8, /device:TPU:8, one launch (start us, length us, event | category | flops | bytes accessed | tf_op | source)
XLA Modules:
  0.0 199.4 jit_solution(13739606167036261932)
XLA Ops:
  0.6 3.8 %collective-permute-start.6 = (bf16[448,1152]{1,0:T(8,128)(2,1)}, bf16[448,1152]{1,0:T(8,128)(2,1)}, u32[]{:S(2)}, u32[]{:S(2)}) collective-permute-start(bf16[448,1152]{1,0:T(8,128)(2,1)} %txt.3), channel_id=1, source_target_pairs={{0,32},{1,481},{2,34},{3,483},{4,36},{5,485},{6,38},{7,487},{8,40}... | collective-permute-start | bytes 3096584 | tf_op jit(solution)/shard_map/ppermute | solution.py:26
  4.5 14.4 %collective-permute-start.3 = (bf16[448,1152]{1,0:T(8,128)(2,1)}, bf16[448,1152]{1,0:T(8,128)(2,1)S(1)}, u32[]{:S(2)}, u32[]{:S(2)}) collective-permute-start(bf16[448,1152]{1,0:T(8,128)(2,1)} %img.3), channel_id=1, source_target_pairs={{0,224},{1,289},{2,226},{3,291},{4,228},{5,293},{6,230},{7,295},{8... | collective-permute-start | bytes 3096584 | tf_op jit(solution)/shard_map/ppermute | solution.py:26
  18.8 0.7 and_convert_fusion.1
  20.9 0.8 copy.16.lab_col
  21.7 0.1 pad_maximum_fusion.scalars
  21.8 0.7 xor_multiply_fusion.1.bases
  22.5 2.5 %collective-permute-done.6 = bf16[448,1152]{1,0:T(8,128)(2,1)} collective-permute-done((bf16[448,1152]{1,0:T(8,128)(2,1)}, bf16[448,1152]{1,0:T(8,128)(2,1)}, u32[]{:S(2)}, u32[]{:S(2)}) %collective-permute-start.6) | collective-permute-done | bytes 1032224 | tf_op jit(solution)/shard_map/ppermute | solution.py:26
  24.9 11.1 %collective-permute-start.7 = (bf16[448,1152]{1,0:T(8,128)(2,1)}, bf16[448,1152]{1,0:T(8,128)(2,1)S(1)}, u32[]{:S(2)}, u32[]{:S(2)}) collective-permute-start(bf16[448,1152]{1,0:T(8,128)(2,1)} %collective-permute-done.6), channel_id=1, source_target_pairs={{0,224},{1,289},{2,226},{3,291},{4,228},{5,293},{6,230},{7,295},{8... | collective-permute-start | bytes 3096584 | tf_op jit(solution)/shard_map/ppermute | solution.py:26
  36.1 1.5 broadcast_in_dim.7
  37.6 1.4 broadcast_in_dim.7.clone
  39.0 1.2 broadcast_in_dim.6
  40.2 1.1 broadcast_in_dim.6.clone
  41.3 1.1 broadcast_in_dim.6.clone.1
  42.4 0.0 copy-done.2
  42.4 0.0 copy-done.10
  42.4 117.4 %while.24 = (s32[]{:T(128)}, bf16[464,1152]{1,0:T(8,128)(2,1)}, bf16[464,1152]{1,0:T(8,128)(2,1)}, bf16[464,1152]{1,0:T(8,128)(2,1)}, f32[448,1152]{1,0:T(8,128)...) while((s32[]{:T(128)}, bf16[464,1152]{1,0:T(8,128)(2,1)}, ...), condition=%wide.region_1.2_spmd.clone, body=%wide.region_0.1_spmd.clone.sunk | while | flops 3703652352 | bytes 56903308 | solution.py:171
  42.4 0.1 constant_dynamic-slice_fusion.5
  42.5 1.2 constant_dynamic-slice_fusion.6
  43.6 0.1 fusion.14.part
  43.7 4.5 %collective-permute-start = (bf16[464,1152]{1,0:T(8,128)(2,1)S(1)}, bf16[464,1152]{1,0:T(8,128)(2,1)}, u32[]{:S(2)}, u32[]{:S(2)}) collective-permute-start(bf16[464,1152]{1,0:T(8,128)(2,1)S(1)} %fusion.14.part), channel_id=1, source_target_pairs={{0,1},{1,0},{2,3},{3,2},{4,5},{5,4},{6,7},{7,6},{8,9},{9,8},{10,11... | collective-permute-start | bytes 3207176 | tf_op jit(solution)/shard_map/while/body/eval_jaxpr/ppermute | solution.py:19
  48.3 3.4 %collective-permute-start.1 = (bf16[464,1152]{1,0:T(8,128)(2,1)S(1)}, bf16[464,1152]{1,0:T(8,128)(2,1)}, u32[]{:S(2)}, u32[]{:S(2)}) collective-permute-start(bf16[464,1152]{1,0:T(8,128)(2,1)S(1)} %fusion.14.part), channel_id=1, source_target_pairs={{0,4},{4,0},{8,12},{12,8},{16,20},{20,16},{24,28},{28,24},{32,36},... | collective-permute-start | bytes 3207176 | tf_op jit(solution)/shard_map/while/body/eval_jaxpr/ppermute | solution.py:19
  51.7 4.6 %collective-permute-start.2 = (bf16[464,1152]{1,0:T(8,128)(2,1)S(1)}, bf16[464,1152]{1,0:T(8,128)(2,1)}, u32[]{:S(2)}, u32[]{:S(2)}) collective-permute-start(bf16[464,1152]{1,0:T(8,128)(2,1)S(1)} %fusion.14.part), channel_id=1, source_target_pairs={{0,8},{4,12},{8,0},{12,4},{16,24},{20,28},{24,16},{28,20},{32,40},... | collective-permute-start | bytes 3207176 | tf_op jit(solution)/shard_map/while/body/eval_jaxpr/ppermute | solution.py:19
  56.3 0.1 pad_add_fusion.4
  56.4 7.1 %own_kernel.8 = (f32[448,1152]{1,0:T(8,128)}, f32[448,1152]{1,0:T(8,128)}) custom-call(s32[6]{0:T(128)S(1)} %get-tuple-element.455.bases, f32[2]{0:T(128)S(1)} %get-tuple-element.507.scalars, bf16[448,1152]{1,0:T(8,128)(2,1)} %get-tuple-element.545, bf16[448,1152]{1,0:T(8,128)(2,1)} %get-tuple-element.504.txt, ...), custom_call_target="tpu_custom_call", output_to_operand_aliasing={{1}: (7, {}), {0}: (6, {})} | custom-call | flops 924844032 | bytes 3096576 | tf_op jit(solution)/shard_map/while/body/eval_jaxpr/own_kernel/pallas_call | solution.py:122
  63.6 0.0 copy-done.4
  63.6 0.0 copy-done.6
  63.6 0.0 copy-done.7
  63.6 9.2 %near_kernel.10 = (f32[448,1152]{1,0:T(8,128)}, f32[448,1152]{1,0:T(8,128)}) custom-call(s32[6]{0:T(128)S(1)} %get-tuple-element.454.bases, f32[2]{0:T(128)S(1)} %get-tuple-element.507.scalars, bf16[448,1152]{1,0:T(8,128)(2,1)} %get-tuple-element.545, bf16[448,1152]{1,0:T(8,128)(2,1)S(1)} %copy-done.4, ...), custom_call_target="tpu_custom_call", output_to_operand_aliasing={{1}: (9, {}), {0}: (8, {})} | custom-call | flops 2774532096 | bytes 9289728 | tf_op jit(solution)/shard_map/while/body/eval_jaxpr/near_kernel/pallas_call | solution.py:122
  72.8 0.0 collective-permute-done
  72.8 2.4 %copy.36 = bf16[464,1152]{1,0:T(8,128)(2,1)} copy(bf16[464,1152]{1,0:T(8,128)(2,1)} %collective-permute-done) | data formatting | bytes 2138112 | tf_op jit(solution)/shard_map/while
  75.2 1.5 collective-permute-done.1
  76.7 2.4 %copy.37 = bf16[464,1152]{1,0:T(8,128)(2,1)} copy(bf16[464,1152]{1,0:T(8,128)(2,1)} %collective-permute-done.1) | data formatting | bytes 2138112 | tf_op jit(solution)/shard_map/while
  79.1 21.8 %collective-permute-done.2 = bf16[464,1152]{1,0:T(8,128)(2,1)} collective-permute-done((bf16[464,1152]{1,0:T(8,128)(2,1)S(1)}, bf16[464,1152]{1,0:T(8,128)(2,1)}, u32[]{:S(2)}, u32[]{:S(2)}) %collective-permute-start.2) | collective-permute-done | bytes 1069088 | tf_op jit(solution)/shard_map/while/body/eval_jaxpr/ppermute | solution.py:19
  100.9 2.4 %copy.38 = bf16[464,1152]{1,0:T(8,128)(2,1)} copy(bf16[464,1152]{1,0:T(8,128)(2,1)} %collective-permute-done.2) | data formatting | bytes 2138112 | tf_op jit(solution)/shard_map/while
  103.3 0.1 constant_dynamic-slice_fusion.5
  103.4 1.1 constant_dynamic-slice_fusion.6
  104.5 0.1 fusion.14.part
  104.6 1.9 collective-permute-start
  106.5 2.1 %collective-permute-start.1 = (bf16[464,1152]{1,0:T(8,128)(2,1)S(1)}, bf16[464,1152]{1,0:T(8,128)(2,1)}, u32[]{:S(2)}, u32[]{:S(2)}) collective-permute-start(bf16[464,1152]{1,0:T(8,128)(2,1)S(1)} %fusion.14.part), channel_id=1, source_target_pairs={{0,4},{4,0},{8,12},{12,8},{16,20},{20,16},{24,28},{28,24},{32,36},... | collective-permute-start | bytes 3207176 | tf_op jit(solution)/shard_map/while/body/eval_jaxpr/ppermute | solution.py:19
  108.7 3.6 %collective-permute-start.2 = (bf16[464,1152]{1,0:T(8,128)(2,1)S(1)}, bf16[464,1152]{1,0:T(8,128)(2,1)}, u32[]{:S(2)}, u32[]{:S(2)}) collective-permute-start(bf16[464,1152]{1,0:T(8,128)(2,1)S(1)} %fusion.14.part), channel_id=1, source_target_pairs={{0,8},{4,12},{8,0},{12,4},{16,24},{20,28},{24,16},{28,20},{32,40},... | collective-permute-start | bytes 3207176 | tf_op jit(solution)/shard_map/while/body/eval_jaxpr/ppermute | solution.py:19
  112.3 0.1 pad_add_fusion.4
  112.4 7.1 %own_kernel.8 = (f32[448,1152]{1,0:T(8,128)}, f32[448,1152]{1,0:T(8,128)}) custom-call(s32[6]{0:T(128)S(1)} %get-tuple-element.455.bases, f32[2]{0:T(128)S(1)} %get-tuple-element.507.scalars, bf16[448,1152]{1,0:T(8,128)(2,1)} %get-tuple-element.545, bf16[448,1152]{1,0:T(8,128)(2,1)} %get-tuple-element.504.txt, ...), custom_call_target="tpu_custom_call", output_to_operand_aliasing={{1}: (7, {}), {0}: (6, {})} | custom-call | flops 924844032 | bytes 3096576 | tf_op jit(solution)/shard_map/while/body/eval_jaxpr/own_kernel/pallas_call | solution.py:122
  119.6 0.0 copy-done.7
  119.6 0.0 copy-done.8
  119.6 9.2 %near_kernel.10 = (f32[448,1152]{1,0:T(8,128)}, f32[448,1152]{1,0:T(8,128)}) custom-call(s32[6]{0:T(128)S(1)} %get-tuple-element.454.bases, f32[2]{0:T(128)S(1)} %get-tuple-element.507.scalars, bf16[448,1152]{1,0:T(8,128)(2,1)} %get-tuple-element.545, bf16[448,1152]{1,0:T(8,128)(2,1)S(1)} %copy-done.4, ...), custom_call_target="tpu_custom_call", output_to_operand_aliasing={{1}: (9, {}), {0}: (8, {})} | custom-call | flops 2774532096 | bytes 9289728 | tf_op jit(solution)/shard_map/while/body/eval_jaxpr/near_kernel/pallas_call | solution.py:122
  128.8 0.0 collective-permute-done
  128.8 2.4 %copy.36 = bf16[464,1152]{1,0:T(8,128)(2,1)} copy(bf16[464,1152]{1,0:T(8,128)(2,1)} %collective-permute-done) | data formatting | bytes 2138112 | tf_op jit(solution)/shard_map/while
  131.2 3.7 %collective-permute-done.1 = bf16[464,1152]{1,0:T(8,128)(2,1)} collective-permute-done((bf16[464,1152]{1,0:T(8,128)(2,1)S(1)}, bf16[464,1152]{1,0:T(8,128)(2,1)}, u32[]{:S(2)}, u32[]{:S(2)}) %collective-permute-start.1) | collective-permute-done | bytes 1069088 | tf_op jit(solution)/shard_map/while/body/eval_jaxpr/ppermute | solution.py:19
  134.9 2.4 %copy.37 = bf16[464,1152]{1,0:T(8,128)(2,1)} copy(bf16[464,1152]{1,0:T(8,128)(2,1)} %collective-permute-done.1) | data formatting | bytes 2138112 | tf_op jit(solution)/shard_map/while
  137.3 20.1 %collective-permute-done.2 = bf16[464,1152]{1,0:T(8,128)(2,1)} collective-permute-done((bf16[464,1152]{1,0:T(8,128)(2,1)S(1)}, bf16[464,1152]{1,0:T(8,128)(2,1)}, u32[]{:S(2)}, u32[]{:S(2)}) %collective-permute-start.2) | collective-permute-done | bytes 1069088 | tf_op jit(solution)/shard_map/while/body/eval_jaxpr/ppermute | solution.py:19
  157.3 2.4 %copy.38 = bf16[464,1152]{1,0:T(8,128)(2,1)} copy(bf16[464,1152]{1,0:T(8,128)(2,1)} %collective-permute-done.2) | data formatting | bytes 2138112 | tf_op jit(solution)/shard_map/while
  159.8 0.0 collective-permute-done.3.nearly_img
  159.8 0.5 pass_kernel.1
  160.3 2.1 %collective-permute-start.4 = (bf16[448,1152]{1,0:T(8,128)(2,1)S(1)}, bf16[448,1152]{1,0:T(8,128)(2,1)S(1)}, u32[]{:S(2)}, u32[]{:S(2)}) collective-permute-start(bf16[448,1152]{1,0:T(8,128)(2,1)S(1)} %pass_kernel.1), channel_id=1, source_target_pairs={{0,32},{1,481},{2,34},{3,483},{4,36},{5,485},{6,38},{7,487},{8,40}... | collective-permute-start | bytes 3096584 | tf_op jit(solution)/shard_map/ppermute | solution.py:26
  162.4 2.1 %collective-permute-start.5 = (s32[1,448]{1,0:T(1,128)S(1)}, s32[1,448]{1,0:T(1,128)S(1)}, u32[]{:S(2)}, u32[]{:S(2)}) collective-permute-start(s32[1,448]{1,0:T(1,128)S(1)} %bitcast.9), channel_id=1, source_target_pairs={{0,256},{4,260},{8,264},{12,268},{16,272},{20,276},{24,280},{28,28... | collective-permute-start | bytes 5384 | tf_op jit(solution)/shard_map/ppermute | solution.py:19
  164.5 0.1 pad_add_fusion.2.bases
  164.6 0.0 copy-done
  164.6 7.4 %near_kernel.9 = (f32[448,1152]{1,0:T(8,128)S(1)}, f32[448,1152]{1,0:T(8,128)S(1)}) custom-call(s32[6]{0:T(128)S(1)} %pad_add_fusion.2.bases, f32[2]{0:T(128)S(1)} %get-tuple-element.535, bf16[448,1152]{1,0:T(8,128)(2,1)S(1)} %get-tuple-element.533, bf16[448,1152]{1,0:T(8,128)(2,1)} %get-tuple-element.532, ...), custom_call_target="tpu_custom_call", output_to_operand_aliasing={{1}: (9, {}), {0}: (8, {})} | custom-call | tf_op jit(solution)/shard_map/near_kernel/pallas_call | solution.py:122
  172.0 5.9 %collective-permute-done.7.far_txt = bf16[448,1152]{1,0:T(8,128)(2,1)S(1)} collective-permute-done((bf16[448,1152]{1,0:T(8,128)(2,1)}, bf16[448,1152]{1,0:T(8,128)(2,1)S(1)}, u32[]{:S(2)}, u32[]{:S(2)}) %collective-permute-start.7) | collective-permute-done | bytes 1032224 | tf_op jit(solution)/shard_map/ppermute | solution.py:26
  177.9 3.0 %far_texts_kernel.1.image_grad = bf16[448,1152]{1,0:T(8,128)(2,1)} custom-call(f32[2]{0:T(128)S(1)} %get-tuple-element.535, s32[5]{0:T(128)S(1)} %xor_multiply_fusion.1.bases, bf16[448,1152]{1,0:T(8,128)(2,1)S(1)} %get-tuple-element.533, s32[448,1]{1,0:T(8,128)S(1)} %get-tuple-element.536, bf16[448,1152]{1,0:T(8,128)(2,1)S(1)} %collective-permute-done.7.far_txt, ...), custom_call_target="tpu_custom_call" | custom-call | tf_op jit(solution)/shard_map/far_texts_kernel/pallas_call | solution.py:122
  180.9 15.4 %collective-permute-done.5.far_lab = s32[1,448]{1,0:T(1,128)S(1)} collective-permute-done((s32[1,448]{1,0:T(1,128)S(1)}, s32[1,448]{1,0:T(1,128)S(1)}, u32[]{:S(2)}, u32[]{:S(2)}) %collective-permute-start.5) | collective-permute-done | bytes 1824 | tf_op jit(solution)/shard_map/ppermute | solution.py:19
  196.3 0.0 collective-permute-done.4.far_img
  196.3 0.0 copy-done.5
  196.3 3.0 %far_images_kernel.1 = (bf16[448,1152]{1,0:T(8,128)(2,1)}, bf16[448,1152]{1,0:T(8,128)(2,1)}) custom-call(f32[2]{0:T(128)S(1)} %get-tuple-element.535, s32[5]{0:T(128)S(1)} %xor_multiply_fusion.1.bases, bf16[448,1152]{1,0:T(8,128)(2,1)S(1)} %copy-done.5, bf16[448,1152]{1,0:T(8,128)(2,1)S(1)} %collective-permute-done.4.far_img, ...), custom_call_target="tpu_custom_call", output_to_operand_aliasing={{1}: (6, {})} | custom-call | tf_op jit(solution)/shard_map/far_images_kernel/pallas_call | solution.py:122
  (29 shorter events, 0.1 us)
Async XLA Ops:
  0.6 24.3 %collective-permute-start.6 = (bf16[448,1152]{1,0:T(8,128)(2,1)}, bf16[448,1152]{1,0:T(8,128)(2,1)}, u32[]{:S(2)}, u32[]{:S(2)}) collective-permute-start(bf16[448,1152]{1,0:T(8,128)(2,1)} %txt.3), channel_id=1, source_target_pairs={{0,32},{1,481},{2,34},{3,483},{4,36},{5,485},{6,38},{7,487},{8,40}... | collective-permute-start | bytes 3096584 | tf_op jit(solution)/shard_map/ppermute | solution.py:26
  4.5 155.3 %collective-permute-start.3 = (bf16[448,1152]{1,0:T(8,128)(2,1)}, bf16[448,1152]{1,0:T(8,128)(2,1)S(1)}, u32[]{:S(2)}, u32[]{:S(2)}) collective-permute-start(bf16[448,1152]{1,0:T(8,128)(2,1)} %img.3), channel_id=1, source_target_pairs={{0,224},{1,289},{2,226},{3,291},{4,228},{5,293},{6,230},{7,295},{8... | collective-permute-start | bytes 3096584 | tf_op jit(solution)/shard_map/ppermute | solution.py:26
  24.9 152.9 %collective-permute-start.7 = (bf16[448,1152]{1,0:T(8,128)(2,1)}, bf16[448,1152]{1,0:T(8,128)(2,1)S(1)}, u32[]{:S(2)}, u32[]{:S(2)}) collective-permute-start(bf16[448,1152]{1,0:T(8,128)(2,1)} %collective-permute-done.6), channel_id=1, source_target_pairs={{0,224},{1,289},{2,226},{3,291},{4,228},{5,293},{6,230},{7,295},{8... | collective-permute-start | bytes 3096584 | tf_op jit(solution)/shard_map/ppermute | solution.py:26
  40.1 2.2 %copy-start.2 = (bf16[448,1152]{1,0:T(8,128)(2,1)S(1)}, bf16[448,1152]{1,0:T(8,128)(2,1)}, u32[]{:S(2)}) copy-start(bf16[448,1152]{1,0:T(8,128)(2,1)} %img.3) | copy-start | bytes 3096580
  40.2 2.2 %copy-start.10 = (s32[5]{0:T(128)S(1)}, s32[5]{0:T(128)}, u32[]{:S(2)}) copy-start(s32[5]{0:T(128)} %constant.86.clone.5) | copy-start | bytes 64
  43.7 29.1 %collective-permute-start = (bf16[464,1152]{1,0:T(8,128)(2,1)S(1)}, bf16[464,1152]{1,0:T(8,128)(2,1)}, u32[]{:S(2)}, u32[]{:S(2)}) collective-permute-start(bf16[464,1152]{1,0:T(8,128)(2,1)S(1)} %fusion.14.part), channel_id=1, source_target_pairs={{0,1},{1,0},{2,3},{3,2},{4,5},{5,4},{6,7},{7,6},{8,9},{9,8},{10,11... | collective-permute-start | bytes 3207176 | tf_op jit(solution)/shard_map/while/body/eval_jaxpr/ppermute | solution.py:19
  48.3 28.5 %collective-permute-start.1 = (bf16[464,1152]{1,0:T(8,128)(2,1)S(1)}, bf16[464,1152]{1,0:T(8,128)(2,1)}, u32[]{:S(2)}, u32[]{:S(2)}) collective-permute-start(bf16[464,1152]{1,0:T(8,128)(2,1)S(1)} %fusion.14.part), channel_id=1, source_target_pairs={{0,4},{4,0},{8,12},{12,8},{16,20},{20,16},{24,28},{28,24},{32,36},... | collective-permute-start | bytes 3207176 | tf_op jit(solution)/shard_map/while/body/eval_jaxpr/ppermute | solution.py:19
  51.7 49.2 %collective-permute-start.2 = (bf16[464,1152]{1,0:T(8,128)(2,1)S(1)}, bf16[464,1152]{1,0:T(8,128)(2,1)}, u32[]{:S(2)}, u32[]{:S(2)}) collective-permute-start(bf16[464,1152]{1,0:T(8,128)(2,1)S(1)} %fusion.14.part), channel_id=1, source_target_pairs={{0,8},{4,12},{8,0},{12,4},{16,24},{20,28},{24,16},{28,20},{32,40},... | collective-permute-start | bytes 3207176 | tf_op jit(solution)/shard_map/while/body/eval_jaxpr/ppermute | solution.py:19
  56.4 7.2 %copy-start.4 = (bf16[448,1152]{1,0:T(8,128)(2,1)S(1)}, bf16[448,1152]{1,0:T(8,128)(2,1)}, u32[]{:S(2)}) copy-start(bf16[448,1152]{1,0:T(8,128)(2,1)} %get-tuple-element.504.txt) | copy-start | bytes 3096580 | tf_op jit(solution)/shard_map/while
  56.4 7.2 %copy-start.6 = (bf16[464,1152]{1,0:T(8,128)(2,1)S(1)}, bf16[464,1152]{1,0:T(8,128)(2,1)}, u32[]{:S(2)}) copy-start(bf16[464,1152]{1,0:T(8,128)(2,1)} %get-tuple-element.480.near1) | copy-start | bytes 3207172 | tf_op jit(solution)/shard_map/while
  56.4 7.2 %copy-start.7 = (bf16[464,1152]{1,0:T(8,128)(2,1)S(1)}, bf16[464,1152]{1,0:T(8,128)(2,1)}, u32[]{:S(2)}) copy-start(bf16[464,1152]{1,0:T(8,128)(2,1)} %get-tuple-element.481.near2) | copy-start | bytes 3207172 | tf_op jit(solution)/shard_map/while
  56.4 7.2 %copy-start.8 = (bf16[464,1152]{1,0:T(8,128)(2,1)S(1)}, bf16[464,1152]{1,0:T(8,128)(2,1)}, u32[]{:S(2)}) copy-start(bf16[464,1152]{1,0:T(8,128)(2,1)} %get-tuple-element.482.near3) | copy-start | bytes 3207172 | tf_op jit(solution)/shard_map/while
  100.9 2.4 %copy-start.3 = (bf16[448,1152]{1,0:T(8,128)(2,1)S(1)}, bf16[448,1152]{1,0:T(8,128)(2,1)}, u32[]{:S(2)}) copy-start(bf16[448,1152]{1,0:T(8,128)(2,1)} %get-tuple-element.545) | copy-start | bytes 3096580 | tf_op jit(solution)/shard_map/while
  104.6 24.2 %collective-permute-start = (bf16[464,1152]{1,0:T(8,128)(2,1)S(1)}, bf16[464,1152]{1,0:T(8,128)(2,1)}, u32[]{:S(2)}, u32[]{:S(2)}) collective-permute-start(bf16[464,1152]{1,0:T(8,128)(2,1)S(1)} %fusion.14.part), channel_id=1, source_target_pairs={{0,1},{1,0},{2,3},{3,2},{4,5},{5,4},{6,7},{7,6},{8,9},{9,8},{10,11... | collective-permute-start | bytes 3207176 | tf_op jit(solution)/shard_map/while/body/eval_jaxpr/ppermute | solution.py:19
  106.5 28.4 %collective-permute-start.1 = (bf16[464,1152]{1,0:T(8,128)(2,1)S(1)}, bf16[464,1152]{1,0:T(8,128)(2,1)}, u32[]{:S(2)}, u32[]{:S(2)}) collective-permute-start(bf16[464,1152]{1,0:T(8,128)(2,1)S(1)} %fusion.14.part), channel_id=1, source_target_pairs={{0,4},{4,0},{8,12},{12,8},{16,20},{20,16},{24,28},{28,24},{32,36},... | collective-permute-start | bytes 3207176 | tf_op jit(solution)/shard_map/while/body/eval_jaxpr/ppermute | solution.py:19
  108.7 48.7 %collective-permute-start.2 = (bf16[464,1152]{1,0:T(8,128)(2,1)S(1)}, bf16[464,1152]{1,0:T(8,128)(2,1)}, u32[]{:S(2)}, u32[]{:S(2)}) collective-permute-start(bf16[464,1152]{1,0:T(8,128)(2,1)S(1)} %fusion.14.part), channel_id=1, source_target_pairs={{0,8},{4,12},{8,0},{12,4},{16,24},{20,28},{24,16},{28,20},{32,40},... | collective-permute-start | bytes 3207176 | tf_op jit(solution)/shard_map/while/body/eval_jaxpr/ppermute | solution.py:19
  112.4 7.2 %copy-start.4 = (bf16[448,1152]{1,0:T(8,128)(2,1)S(1)}, bf16[448,1152]{1,0:T(8,128)(2,1)}, u32[]{:S(2)}) copy-start(bf16[448,1152]{1,0:T(8,128)(2,1)} %get-tuple-element.504.txt) | copy-start | bytes 3096580 | tf_op jit(solution)/shard_map/while
  112.4 7.2 %copy-start.6 = (bf16[464,1152]{1,0:T(8,128)(2,1)S(1)}, bf16[464,1152]{1,0:T(8,128)(2,1)}, u32[]{:S(2)}) copy-start(bf16[464,1152]{1,0:T(8,128)(2,1)} %get-tuple-element.480.near1) | copy-start | bytes 3207172 | tf_op jit(solution)/shard_map/while
  112.4 7.2 %copy-start.7 = (bf16[464,1152]{1,0:T(8,128)(2,1)S(1)}, bf16[464,1152]{1,0:T(8,128)(2,1)}, u32[]{:S(2)}) copy-start(bf16[464,1152]{1,0:T(8,128)(2,1)} %get-tuple-element.481.near2) | copy-start | bytes 3207172 | tf_op jit(solution)/shard_map/while
  112.4 7.2 %copy-start.8 = (bf16[464,1152]{1,0:T(8,128)(2,1)S(1)}, bf16[464,1152]{1,0:T(8,128)(2,1)}, u32[]{:S(2)}) copy-start(bf16[464,1152]{1,0:T(8,128)(2,1)} %get-tuple-element.482.near3) | copy-start | bytes 3207172 | tf_op jit(solution)/shard_map/while
  157.3 2.4 %copy-start.3 = (bf16[448,1152]{1,0:T(8,128)(2,1)S(1)}, bf16[448,1152]{1,0:T(8,128)(2,1)}, u32[]{:S(2)}) copy-start(bf16[448,1152]{1,0:T(8,128)(2,1)} %get-tuple-element.545) | copy-start | bytes 3096580 | tf_op jit(solution)/shard_map/while
  159.8 2.6 %copy-start.9 = (s32[448]{0:T(512)S(1)}, s32[448]{0:T(512)}, u32[]{:S(2)}) copy-start(s32[448]{0:T(512)} %param.10) | copy-start | bytes 5380
  159.8 4.8 %copy-start = (f32[448,1152]{1,0:T(8,128)S(1)}, f32[448,1152]{1,0:T(8,128)}, u32[]{:S(2)}) copy-start(f32[448,1152]{1,0:T(8,128)} %get-tuple-element.531) | copy-start | bytes 6193156
  159.8 4.8 %copy-start.1 = (f32[448,1152]{1,0:T(8,128)S(1)}, f32[448,1152]{1,0:T(8,128)}, u32[]{:S(2)}) copy-start(f32[448,1152]{1,0:T(8,128)} %get-tuple-element.530) | copy-start | bytes 6193156
  160.3 36.0 %collective-permute-start.4 = (bf16[448,1152]{1,0:T(8,128)(2,1)S(1)}, bf16[448,1152]{1,0:T(8,128)(2,1)S(1)}, u32[]{:S(2)}, u32[]{:S(2)}) collective-permute-start(bf16[448,1152]{1,0:T(8,128)(2,1)S(1)} %pass_kernel.1), channel_id=1, source_target_pairs={{0,32},{1,481},{2,34},{3,483},{4,36},{5,485},{6,38},{7,487},{8,40}... | collective-permute-start | bytes 3096584 | tf_op jit(solution)/shard_map/ppermute | solution.py:26
  162.4 33.9 %collective-permute-start.5 = (s32[1,448]{1,0:T(1,128)S(1)}, s32[1,448]{1,0:T(1,128)S(1)}, u32[]{:S(2)}, u32[]{:S(2)}) collective-permute-start(s32[1,448]{1,0:T(1,128)S(1)} %bitcast.9), channel_id=1, source_target_pairs={{0,256},{4,260},{8,264},{12,268},{16,272},{20,276},{24,280},{28,28... | collective-permute-start | bytes 5384 | tf_op jit(solution)/shard_map/ppermute | solution.py:19
  177.9 18.4 %copy-start.5 = (bf16[448,1152]{1,0:T(8,128)(2,1)S(1)}, bf16[448,1152]{1,0:T(8,128)(2,1)}, u32[]{:S(2)}) copy-start(bf16[448,1152]{1,0:T(8,128)(2,1)} %get-tuple-element.532) | copy-start | bytes 3096580

commit v9 on v7

--- a/solution.py
+++ b/solution.py
@@ -11,7 +11,7 @@
 CHUNKS = 2
 RING = 16
 FIRST_STEPS = 1
-VMEM_LIMIT = 28 << 20
+VMEM_LIMIT = 22 << 20
 
 
 def from_partner(block, axis, bit):

time: 198 us -> 198 us (level)
  no operation moved by 1% of the time
where the time goes in v9:
time: 198 us; the launch traced here: 197 us
  starting transfers between devices  62 us (31%)
  waiting for transfers between devices  58.1 us (29%)
  Pallas kernels  49.8 us (25%)
  local copies, waits for them, and re-layouts  23.9 us (12%)
  between operations  2.09 us (1%)
    ppermute x7, waiting for transfers between devices, from_partner(): return lax.ppermute(block, axis, [(i, i ^ 1 << bit) for i in range(count)])  57.7 us
    pallas_call x7, Pallas kernels, kernel(): pl.pallas_call(body, out_shape=out_shape, in_specs=specs, out_specs=out_s...  49.8 us
    ppermute x4, starting transfers between devices, along_ring(): lax.ppermute(block, axes, [(i, (i + (step if i % 2 == 0 else -step)) % co...  37.8 us
    ppermute x7, starting transfers between devices, from_partner(): return lax.ppermute(block, axis, [(i, i ^ 1 << bit) for i in range(count)])  24.2 us
    while x26, local copies, waits for them, and re-layouts  14.4 us
  transfers between devices with their start and end apart: 11, of which 6 were waited for; matrix products, arithmetic and copies ran while one was open for 13% of the time, Pallas kernels for 24%

profile of v9, /device:TPU:37, one launch (start us, length us, event | category | flops | bytes accessed | tf_op | source)
XLA Modules:
  0.0 197.2 jit_solution(2023192312912953974)
XLA Ops:
  0.6 1.9 collective-permute-start.6
  2.6 10.9 %collective-permute-start.3 = (bf16[448,1152]{1,0:T(8,128)(2,1)}, bf16[448,1152]{1,0:T(8,128)(2,1)}, u32[]{:S(2)}, u32[]{:S(2)}) collective-permute-start(bf16[448,1152]{1,0:T(8,128)(2,1)} %img.3), channel_id=1, source_target_pairs={{0,32},{1,481},{2,34},{3,483},{4,36},{5,485},{6,38},{7,487},{8,40}... | collective-permute-start | bytes 3096584 | tf_op jit(solution)/shard_map/ppermute | solution.py:26
  13.5 0.7 and_convert_fusion.1
  15.6 0.8 copy.16.lab_col
  16.4 0.1 pad_maximum_fusion.scalars
  16.5 0.3 collective-permute-done.6
  16.8 13.9 %collective-permute-start.7 = (bf16[448,1152]{1,0:T(8,128)(2,1)}, bf16[448,1152]{1,0:T(8,128)(2,1)S(1)}, u32[]{:S(2)}, u32[]{:S(2)}) collective-permute-start(bf16[448,1152]{1,0:T(8,128)(2,1)} %collective-permute-done.6), channel_id=1, source_target_pairs={{0,224},{1,289},{2,226},{3,291},{4,228},{5,293},{6,230},{7,295},{8... | collective-permute-start | bytes 3096584 | tf_op jit(solution)/shard_map/ppermute | solution.py:26
  30.7 0.0 collective-permute-done.3
  30.7 11.0 %collective-permute-start.4 = (bf16[448,1152]{1,0:T(8,128)(2,1)}, bf16[448,1152]{1,0:T(8,128)(2,1)S(1)}, u32[]{:S(2)}, u32[]{:S(2)}) collective-permute-start(bf16[448,1152]{1,0:T(8,128)(2,1)} %collective-permute-done.3), channel_id=1, source_target_pairs={{0,224},{1,289},{2,226},{3,291},{4,228},{5,293},{6,230},{7,295},{8... | collective-permute-start | bytes 3096584 | tf_op jit(solution)/shard_map/ppermute | solution.py:26
  41.8 1.5 broadcast_in_dim.7
  43.2 1.4 broadcast_in_dim.7.clone
  44.7 1.2 broadcast_in_dim.6
  45.8 1.1 broadcast_in_dim.6.clone
  46.9 1.1 broadcast_in_dim.6.clone.1
  48.0 0.0 copy-done.1
  48.0 0.0 copy-done.10
  48.1 118.9 %while.24 = (s32[]{:T(128)}, bf16[464,1152]{1,0:T(8,128)(2,1)}, bf16[464,1152]{1,0:T(8,128)(2,1)}, bf16[464,1152]{1,0:T(8,128)(2,1)}, f32[448,1152]{1,0:T(8,128)...) while((s32[]{:T(128)}, bf16[464,1152]{1,0:T(8,128)(2,1)}, ...), condition=%wide.region_1.2_spmd.clone, body=%wide.region_0.1_spmd.clone.sunk | while | flops 3703652352 | bytes 56903308 | solution.py:167
  48.1 0.1 constant_dynamic-slice_fusion.5
  48.2 1.1 constant_dynamic-slice_fusion.6
  49.3 0.1 fusion.14.part
  49.4 7.4 %collective-permute-start = (bf16[464,1152]{1,0:T(8,128)(2,1)S(1)}, bf16[464,1152]{1,0:T(8,128)(2,1)}, u32[]{:S(2)}, u32[]{:S(2)}) collective-permute-start(bf16[464,1152]{1,0:T(8,128)(2,1)S(1)} %fusion.14.part), channel_id=1, source_target_pairs={{0,1},{1,0},{2,3},{3,2},{4,5},{5,4},{6,7},{7,6},{8,9},{9,8},{10,11... | collective-permute-start | bytes 3207176 | tf_op jit(solution)/shard_map/while/body/eval_jaxpr/ppermute | solution.py:19
  56.8 2.8 %collective-permute-start.1 = (bf16[464,1152]{1,0:T(8,128)(2,1)S(1)}, bf16[464,1152]{1,0:T(8,128)(2,1)}, u32[]{:S(2)}, u32[]{:S(2)}) collective-permute-start(bf16[464,1152]{1,0:T(8,128)(2,1)S(1)} %fusion.14.part), channel_id=1, source_target_pairs={{0,4},{4,0},{8,12},{12,8},{16,20},{20,16},{24,28},{28,24},{32,36},... | collective-permute-start | bytes 3207176 | tf_op jit(solution)/shard_map/while/body/eval_jaxpr/ppermute | solution.py:19
  59.6 2.4 %collective-permute-start.2 = (bf16[464,1152]{1,0:T(8,128)(2,1)S(1)}, bf16[464,1152]{1,0:T(8,128)(2,1)}, u32[]{:S(2)}, u32[]{:S(2)}) collective-permute-start(bf16[464,1152]{1,0:T(8,128)(2,1)S(1)} %fusion.14.part), channel_id=1, source_target_pairs={{0,8},{4,12},{8,0},{12,4},{16,24},{20,28},{24,16},{28,20},{32,40},... | collective-permute-start | bytes 3207176 | tf_op jit(solution)/shard_map/while/body/eval_jaxpr/ppermute | solution.py:19
  62.0 0.1 pad_add_fusion.4
  62.1 7.1 %own_kernel.8 = (f32[448,1152]{1,0:T(8,128)}, f32[448,1152]{1,0:T(8,128)}) custom-call(s32[6]{0:T(128)S(1)} %get-tuple-element.455.bases, f32[2]{0:T(128)S(1)} %get-tuple-element.507.scalars, bf16[448,1152]{1,0:T(8,128)(2,1)} %get-tuple-element.543, bf16[448,1152]{1,0:T(8,128)(2,1)} %get-tuple-element.504.txt, ...), custom_call_target="tpu_custom_call", output_to_operand_aliasing={{1}: (7, {}), {0}: (6, {})} | custom-call | flops 924844032 | bytes 3096576 | tf_op jit(solution)/shard_map/while/body/eval_jaxpr/own_kernel/pallas_call | solution.py:118
  69.3 0.0 copy-done.3
  69.3 0.0 copy-done.5
  69.3 0.0 copy-done.6
  69.3 0.0 copy-done.7
  69.3 9.2 %near_kernel.10 = (f32[448,1152]{1,0:T(8,128)}, f32[448,1152]{1,0:T(8,128)}) custom-call(s32[6]{0:T(128)S(1)} %get-tuple-element.454.bases, f32[2]{0:T(128)S(1)} %get-tuple-element.507.scalars, bf16[448,1152]{1,0:T(8,128)(2,1)} %get-tuple-element.543, bf16[448,1152]{1,0:T(8,128)(2,1)S(1)} %copy-done.3, ...), custom_call_target="tpu_custom_call", output_to_operand_aliasing={{1}: (9, {}), {0}: (8, {})} | custom-call | flops 2774532096 | bytes 9289728 | tf_op jit(solution)/shard_map/while/body/eval_jaxpr/near_kernel/pallas_call | solution.py:118
  78.5 0.0 collective-permute-done
  78.5 2.4 %copy.35 = bf16[464,1152]{1,0:T(8,128)(2,1)} copy(bf16[464,1152]{1,0:T(8,128)(2,1)} %collective-permute-done) | data formatting | bytes 2138112 | tf_op jit(solution)/shard_map/while
  80.9 3.0 %collective-permute-done.1 = bf16[464,1152]{1,0:T(8,128)(2,1)} collective-permute-done((bf16[464,1152]{1,0:T(8,128)(2,1)S(1)}, bf16[464,1152]{1,0:T(8,128)(2,1)}, u32[]{:S(2)}, u32[]{:S(2)}) %collective-permute-start.1) | collective-permute-done | bytes 1069088 | tf_op jit(solution)/shard_map/while/body/eval_jaxpr/ppermute | solution.py:19
  84.0 2.4 %copy.36 = bf16[464,1152]{1,0:T(8,128)(2,1)} copy(bf16[464,1152]{1,0:T(8,128)(2,1)} %collective-permute-done.1) | data formatting | bytes 2138112 | tf_op jit(solution)/shard_map/while
  86.3 20.5 %collective-permute-done.2 = bf16[464,1152]{1,0:T(8,128)(2,1)} collective-permute-done((bf16[464,1152]{1,0:T(8,128)(2,1)S(1)}, bf16[464,1152]{1,0:T(8,128)(2,1)}, u32[]{:S(2)}, u32[]{:S(2)}) %collective-permute-start.2) | collective-permute-done | bytes 1069088 | tf_op jit(solution)/shard_map/while/body/eval_jaxpr/ppermute | solution.py:19
  106.9 2.4 %copy.37 = bf16[464,1152]{1,0:T(8,128)(2,1)} copy(bf16[464,1152]{1,0:T(8,128)(2,1)} %collective-permute-done.2) | data formatting | bytes 2138112 | tf_op jit(solution)/shard_map/while
  109.3 0.0 copy-done.2
  109.3 0.1 constant_dynamic-slice_fusion.5
  109.4 1.1 constant_dynamic-slice_fusion.6
  110.5 0.1 fusion.14.part
  110.6 2.7 %collective-permute-start = (bf16[464,1152]{1,0:T(8,128)(2,1)S(1)}, bf16[464,1152]{1,0:T(8,128)(2,1)}, u32[]{:S(2)}, u32[]{:S(2)}) collective-permute-start(bf16[464,1152]{1,0:T(8,128)(2,1)S(1)} %fusion.14.part), channel_id=1, source_target_pairs={{0,1},{1,0},{2,3},{3,2},{4,5},{5,4},{6,7},{7,6},{8,9},{9,8},{10,11... | collective-permute-start | bytes 3207176 | tf_op jit(solution)/shard_map/while/body/eval_jaxpr/ppermute | solution.py:19
  113.3 2.8 %collective-permute-start.1 = (bf16[464,1152]{1,0:T(8,128)(2,1)S(1)}, bf16[464,1152]{1,0:T(8,128)(2,1)}, u32[]{:S(2)}, u32[]{:S(2)}) collective-permute-start(bf16[464,1152]{1,0:T(8,128)(2,1)S(1)} %fusion.14.part), channel_id=1, source_target_pairs={{0,4},{4,0},{8,12},{12,8},{16,20},{20,16},{24,28},{28,24},{32,36},... | collective-permute-start | bytes 3207176 | tf_op jit(solution)/shard_map/while/body/eval_jaxpr/ppermute | solution.py:19
  116.1 3.5 %collective-permute-start.2 = (bf16[464,1152]{1,0:T(8,128)(2,1)S(1)}, bf16[464,1152]{1,0:T(8,128)(2,1)}, u32[]{:S(2)}, u32[]{:S(2)}) collective-permute-start(bf16[464,1152]{1,0:T(8,128)(2,1)S(1)} %fusion.14.part), channel_id=1, source_target_pairs={{0,8},{4,12},{8,0},{12,4},{16,24},{20,28},{24,16},{28,20},{32,40},... | collective-permute-start | bytes 3207176 | tf_op jit(solution)/shard_map/while/body/eval_jaxpr/ppermute | solution.py:19
  119.6 0.1 pad_add_fusion.4
  119.7 7.1 %own_kernel.8 = (f32[448,1152]{1,0:T(8,128)}, f32[448,1152]{1,0:T(8,128)}) custom-call(s32[6]{0:T(128)S(1)} %get-tuple-element.455.bases, f32[2]{0:T(128)S(1)} %get-tuple-element.507.scalars, bf16[448,1152]{1,0:T(8,128)(2,1)} %get-tuple-element.543, bf16[448,1152]{1,0:T(8,128)(2,1)} %get-tuple-element.504.txt, ...), custom_call_target="tpu_custom_call", output_to_operand_aliasing={{1}: (7, {}), {0}: (6, {})} | custom-call | flops 924844032 | bytes 3096576 | tf_op jit(solution)/shard_map/while/body/eval_jaxpr/own_kernel/pallas_call | solution.py:118
  126.8 0.0 copy-done.3
  126.8 0.0 copy-done.5
  126.8 0.0 copy-done.6
  126.9 9.2 %near_kernel.10 = (f32[448,1152]{1,0:T(8,128)}, f32[448,1152]{1,0:T(8,128)}) custom-call(s32[6]{0:T(128)S(1)} %get-tuple-element.454.bases, f32[2]{0:T(128)S(1)} %get-tuple-element.507.scalars, bf16[448,1152]{1,0:T(8,128)(2,1)} %get-tuple-element.543, bf16[448,1152]{1,0:T(8,128)(2,1)S(1)} %copy-done.3, ...), custom_call_target="tpu_custom_call", output_to_operand_aliasing={{1}: (9, {}), {0}: (8, {})} | custom-call | flops 2774532096 | bytes 9289728 | tf_op jit(solution)/shard_map/while/body/eval_jaxpr/near_kernel/pallas_call | solution.py:118
  136.1 0.0 collective-permute-done
  136.1 2.4 %copy.35 = bf16[464,1152]{1,0:T(8,128)(2,1)} copy(bf16[464,1152]{1,0:T(8,128)(2,1)} %collective-permute-done) | data formatting | bytes 2138112 | tf_op jit(solution)/shard_map/while
  138.5 2.0 %collective-permute-done.1 = bf16[464,1152]{1,0:T(8,128)(2,1)} collective-permute-done((bf16[464,1152]{1,0:T(8,128)(2,1)S(1)}, bf16[464,1152]{1,0:T(8,128)(2,1)}, u32[]{:S(2)}, u32[]{:S(2)}) %collective-permute-start.1) | collective-permute-done | bytes 1069088 | tf_op jit(solution)/shard_map/while/body/eval_jaxpr/ppermute | solution.py:19
  140.5 2.4 %copy.36 = bf16[464,1152]{1,0:T(8,128)(2,1)} copy(bf16[464,1152]{1,0:T(8,128)(2,1)} %collective-permute-done.1) | data formatting | bytes 2138112 | tf_op jit(solution)/shard_map/while
  142.9 21.6 %collective-permute-done.2 = bf16[464,1152]{1,0:T(8,128)(2,1)} collective-permute-done((bf16[464,1152]{1,0:T(8,128)(2,1)S(1)}, bf16[464,1152]{1,0:T(8,128)(2,1)}, u32[]{:S(2)}, u32[]{:S(2)}) %collective-permute-start.2) | collective-permute-done | bytes 1069088 | tf_op jit(solution)/shard_map/while/body/eval_jaxpr/ppermute | solution.py:19
  164.5 2.4 %copy.37 = bf16[464,1152]{1,0:T(8,128)(2,1)} copy(bf16[464,1152]{1,0:T(8,128)(2,1)} %collective-permute-done.2) | data formatting | bytes 2138112 | tf_op jit(solution)/shard_map/while
  166.9 2.5 %collective-permute-start.5 = (s32[1,448]{1,0:T(1,128)S(1)}, s32[1,448]{1,0:T(1,128)S(1)}, u32[]{:S(2)}, u32[]{:S(2)}) collective-permute-start(s32[1,448]{1,0:T(1,128)S(1)} %bitcast.9), channel_id=1, source_target_pairs={{0,256},{4,260},{8,264},{12,268},{16,272},{20,276},{24,280},{28,28... | collective-permute-start | bytes 5384 | tf_op jit(solution)/shard_map/ppermute | solution.py:19
  169.5 0.1 pad_add_fusion.2.bases
  169.6 9.8 %near_kernel.9 = (f32[448,1152]{1,0:T(8,128)}, f32[448,1152]{1,0:T(8,128)}) custom-call(s32[6]{0:T(128)S(1)} %pad_add_fusion.2.bases, f32[2]{0:T(128)S(1)} %get-tuple-element.533, bf16[448,1152]{1,0:T(8,128)(2,1)S(1)} %get-tuple-element.531, bf16[448,1152]{1,0:T(8,128)(2,1)} %get-tuple-element.530, ...), custom_call_target="tpu_custom_call", output_to_operand_aliasing={{1}: (9, {}), {0}: (8, {})} | custom-call | tf_op jit(solution)/shard_map/near_kernel/pallas_call | solution.py:118
  179.4 0.0 collective-permute-done.7.far_txt
  179.4 0.0 copy-start.4
  179.4 4.2 %far_texts_kernel.1.image_grad = bf16[448,1152]{1,0:T(8,128)(2,1)} custom-call(f32[2]{0:T(128)S(1)} %get-tuple-element.533, s32[5]{0:T(128)S(1)} %xor_multiply_fusion.1.bases, bf16[448,1152]{1,0:T(8,128)(2,1)S(1)} %get-tuple-element.531, s32[448,1]{1,0:T(8,128)S(1)} %get-tuple-element.534, bf16[448,1152]{1,0:T(8,128)(2,1)S(1)} %collective-permute-done.7.far_txt, ...), custom_call_target="tpu_custom_call" | custom-call | tf_op jit(solution)/shard_map/far_texts_kernel/pallas_call | solution.py:118
  183.6 10.5 %collective-permute-done.5.far_lab = s32[1,448]{1,0:T(1,128)S(1)} collective-permute-done((s32[1,448]{1,0:T(1,128)S(1)}, s32[1,448]{1,0:T(1,128)S(1)}, u32[]{:S(2)}, u32[]{:S(2)}) %collective-permute-start.5) | collective-permute-done | bytes 1824 | tf_op jit(solution)/shard_map/ppermute | solution.py:19
  194.1 0.0 collective-permute-done.4.far_img
  194.1 3.0 %far_images_kernel.1 = (bf16[448,1152]{1,0:T(8,128)(2,1)}, bf16[448,1152]{1,0:T(8,128)(2,1)}) custom-call(f32[2]{0:T(128)S(1)} %get-tuple-element.533, s32[5]{0:T(128)S(1)} %xor_multiply_fusion.1.bases, bf16[448,1152]{1,0:T(8,128)(2,1)S(1)} %copy-done.4, bf16[448,1152]{1,0:T(8,128)(2,1)S(1)} %collective-permute-done.4.far_img, ...), custom_call_target="tpu_custom_call", output_to_operand_aliasing={{1}: (6, {})} | custom-call | tf_op jit(solution)/shard_map/far_images_kernel/pallas_call | solution.py:118
  (28 shorter events, 0.1 us)
Async XLA Ops:
  0.6 16.2 %collective-permute-start.6 = (bf16[448,1152]{1,0:T(8,128)(2,1)}, bf16[448,1152]{1,0:T(8,128)(2,1)}, u32[]{:S(2)}, u32[]{:S(2)}) collective-permute-start(bf16[448,1152]{1,0:T(8,128)(2,1)} %txt.3), channel_id=1, source_target_pairs={{0,32},{1,481},{2,34},{3,483},{4,36},{5,485},{6,38},{7,487},{8,40}... | collective-permute-start | bytes 3096584 | tf_op jit(solution)/shard_map/ppermute | solution.py:26
  2.6 28.1 %collective-permute-start.3 = (bf16[448,1152]{1,0:T(8,128)(2,1)}, bf16[448,1152]{1,0:T(8,128)(2,1)}, u32[]{:S(2)}, u32[]{:S(2)}) collective-permute-start(bf16[448,1152]{1,0:T(8,128)(2,1)} %img.3), channel_id=1, source_target_pairs={{0,32},{1,481},{2,34},{3,483},{4,36},{5,485},{6,38},{7,487},{8,40}... | collective-permute-start | bytes 3096584 | tf_op jit(solution)/shard_map/ppermute | solution.py:26
  16.8 162.6 %collective-permute-start.7 = (bf16[448,1152]{1,0:T(8,128)(2,1)}, bf16[448,1152]{1,0:T(8,128)(2,1)S(1)}, u32[]{:S(2)}, u32[]{:S(2)}) collective-permute-start(bf16[448,1152]{1,0:T(8,128)(2,1)} %collective-permute-done.6), channel_id=1, source_target_pairs={{0,224},{1,289},{2,226},{3,291},{4,228},{5,293},{6,230},{7,295},{8... | collective-permute-start | bytes 3096584 | tf_op jit(solution)/shard_map/ppermute | solution.py:26
  30.7 163.4 %collective-permute-start.4 = (bf16[448,1152]{1,0:T(8,128)(2,1)}, bf16[448,1152]{1,0:T(8,128)(2,1)S(1)}, u32[]{:S(2)}, u32[]{:S(2)}) collective-permute-start(bf16[448,1152]{1,0:T(8,128)(2,1)} %collective-permute-done.3), channel_id=1, source_target_pairs={{0,224},{1,289},{2,226},{3,291},{4,228},{5,293},{6,230},{7,295},{8... | collective-permute-start | bytes 3096584 | tf_op jit(solution)/shard_map/ppermute | solution.py:26
  45.8 2.2 %copy-start.1 = (bf16[448,1152]{1,0:T(8,128)(2,1)S(1)}, bf16[448,1152]{1,0:T(8,128)(2,1)}, u32[]{:S(2)}) copy-start(bf16[448,1152]{1,0:T(8,128)(2,1)} %img.3) | copy-start | bytes 3096580
  45.8 2.2 %copy-start.10 = (s32[5]{0:T(128)S(1)}, s32[5]{0:T(128)}, u32[]{:S(2)}) copy-start(s32[5]{0:T(128)} %constant.86.clone.5) | copy-start | bytes 64
  48.1 118.9 %copy-start.8 = (s32[448]{0:T(512)S(1)}, s32[448]{0:T(512)}, u32[]{:S(2)}) copy-start(s32[448]{0:T(512)} %param.10) | copy-start | bytes 5380
  48.1 121.4 %copy-start.9 = (s32[5]{0:T(128)S(1)}, s32[5]{0:T(128)}, u32[]{:S(2)}) copy-start(s32[5]{0:T(128)} %constant.86.clone) | copy-start | bytes 64
  49.4 29.1 %collective-permute-start = (bf16[464,1152]{1,0:T(8,128)(2,1)S(1)}, bf16[464,1152]{1,0:T(8,128)(2,1)}, u32[]{:S(2)}, u32[]{:S(2)}) collective-permute-start(bf16[464,1152]{1,0:T(8,128)(2,1)S(1)} %fusion.14.part), channel_id=1, source_target_pairs={{0,1},{1,0},{2,3},{3,2},{4,5},{5,4},{6,7},{7,6},{8,9},{9,8},{10,11... | collective-permute-start | bytes 3207176 | tf_op jit(solution)/shard_map/while/body/eval_jaxpr/ppermute | solution.py:19
  56.8 27.2 %collective-permute-start.1 = (bf16[464,1152]{1,0:T(8,128)(2,1)S(1)}, bf16[464,1152]{1,0:T(8,128)(2,1)}, u32[]{:S(2)}, u32[]{:S(2)}) collective-permute-start(bf16[464,1152]{1,0:T(8,128)(2,1)S(1)} %fusion.14.part), channel_id=1, source_target_pairs={{0,4},{4,0},{8,12},{12,8},{16,20},{20,16},{24,28},{28,24},{32,36},... | collective-permute-start | bytes 3207176 | tf_op jit(solution)/shard_map/while/body/eval_jaxpr/ppermute | solution.py:19
  59.6 47.3 %collective-permute-start.2 = (bf16[464,1152]{1,0:T(8,128)(2,1)S(1)}, bf16[464,1152]{1,0:T(8,128)(2,1)}, u32[]{:S(2)}, u32[]{:S(2)}) collective-permute-start(bf16[464,1152]{1,0:T(8,128)(2,1)S(1)} %fusion.14.part), channel_id=1, source_target_pairs={{0,8},{4,12},{8,0},{12,4},{16,24},{20,28},{24,16},{28,20},{32,40},... | collective-permute-start | bytes 3207176 | tf_op jit(solution)/shard_map/while/body/eval_jaxpr/ppermute | solution.py:19
  62.1 7.1 %copy-start.3 = (bf16[448,1152]{1,0:T(8,128)(2,1)S(1)}, bf16[448,1152]{1,0:T(8,128)(2,1)}, u32[]{:S(2)}) copy-start(bf16[448,1152]{1,0:T(8,128)(2,1)} %get-tuple-element.504.txt) | copy-start | bytes 3096580 | tf_op jit(solution)/shard_map/while
  62.1 7.1 %copy-start.5 = (bf16[464,1152]{1,0:T(8,128)(2,1)S(1)}, bf16[464,1152]{1,0:T(8,128)(2,1)}, u32[]{:S(2)}) copy-start(bf16[464,1152]{1,0:T(8,128)(2,1)} %get-tuple-element.480.near1) | copy-start | bytes 3207172 | tf_op jit(solution)/shard_map/while
  62.1 7.2 %copy-start.6 = (bf16[464,1152]{1,0:T(8,128)(2,1)S(1)}, bf16[464,1152]{1,0:T(8,128)(2,1)}, u32[]{:S(2)}) copy-start(bf16[464,1152]{1,0:T(8,128)(2,1)} %get-tuple-element.481.near2) | copy-start | bytes 3207172 | tf_op jit(solution)/shard_map/while
  62.1 7.2 %copy-start.7 = (bf16[464,1152]{1,0:T(8,128)(2,1)S(1)}, bf16[464,1152]{1,0:T(8,128)(2,1)}, u32[]{:S(2)}) copy-start(bf16[464,1152]{1,0:T(8,128)(2,1)} %get-tuple-element.482.near3) | copy-start | bytes 3207172 | tf_op jit(solution)/shard_map/while
  106.9 2.4 %copy-start.2 = (bf16[448,1152]{1,0:T(8,128)(2,1)S(1)}, bf16[448,1152]{1,0:T(8,128)(2,1)}, u32[]{:S(2)}) copy-start(bf16[448,1152]{1,0:T(8,128)(2,1)} %get-tuple-element.543) | copy-start | bytes 3096580 | tf_op jit(solution)/shard_map/while
  110.6 25.5 %collective-permute-start = (bf16[464,1152]{1,0:T(8,128)(2,1)S(1)}, bf16[464,1152]{1,0:T(8,128)(2,1)}, u32[]{:S(2)}, u32[]{:S(2)}) collective-permute-start(bf16[464,1152]{1,0:T(8,128)(2,1)S(1)} %fusion.14.part), channel_id=1, source_target_pairs={{0,1},{1,0},{2,3},{3,2},{4,5},{5,4},{6,7},{7,6},{8,9},{9,8},{10,11... | collective-permute-start | bytes 3207176 | tf_op jit(solution)/shard_map/while/body/eval_jaxpr/ppermute | solution.py:19
  113.3 27.2 %collective-permute-start.1 = (bf16[464,1152]{1,0:T(8,128)(2,1)S(1)}, bf16[464,1152]{1,0:T(8,128)(2,1)}, u32[]{:S(2)}, u32[]{:S(2)}) collective-permute-start(bf16[464,1152]{1,0:T(8,128)(2,1)S(1)} %fusion.14.part), channel_id=1, source_target_pairs={{0,4},{4,0},{8,12},{12,8},{16,20},{20,16},{24,28},{28,24},{32,36},... | collective-permute-start | bytes 3207176 | tf_op jit(solution)/shard_map/while/body/eval_jaxpr/ppermute | solution.py:19
  116.1 48.4 %collective-permute-start.2 = (bf16[464,1152]{1,0:T(8,128)(2,1)S(1)}, bf16[464,1152]{1,0:T(8,128)(2,1)}, u32[]{:S(2)}, u32[]{:S(2)}) collective-permute-start(bf16[464,1152]{1,0:T(8,128)(2,1)S(1)} %fusion.14.part), channel_id=1, source_target_pairs={{0,8},{4,12},{8,0},{12,4},{16,24},{20,28},{24,16},{28,20},{32,40},... | collective-permute-start | bytes 3207176 | tf_op jit(solution)/shard_map/while/body/eval_jaxpr/ppermute | solution.py:19
  119.7 7.1 %copy-start.3 = (bf16[448,1152]{1,0:T(8,128)(2,1)S(1)}, bf16[448,1152]{1,0:T(8,128)(2,1)}, u32[]{:S(2)}) copy-start(bf16[448,1152]{1,0:T(8,128)(2,1)} %get-tuple-element.504.txt) | copy-start | bytes 3096580 | tf_op jit(solution)/shard_map/while
  119.7 7.1 %copy-start.5 = (bf16[464,1152]{1,0:T(8,128)(2,1)S(1)}, bf16[464,1152]{1,0:T(8,128)(2,1)}, u32[]{:S(2)}) copy-start(bf16[464,1152]{1,0:T(8,128)(2,1)} %get-tuple-element.480.near1) | copy-start | bytes 3207172 | tf_op jit(solution)/shard_map/while
  119.7 7.2 %copy-start.6 = (bf16[464,1152]{1,0:T(8,128)(2,1)S(1)}, bf16[464,1152]{1,0:T(8,128)(2,1)}, u32[]{:S(2)}) copy-start(bf16[464,1152]{1,0:T(8,128)(2,1)} %get-tuple-element.481.near2) | copy-start | bytes 3207172 | tf_op jit(solution)/shard_map/while
  119.7 7.2 %copy-start.7 = (bf16[464,1152]{1,0:T(8,128)(2,1)S(1)}, bf16[464,1152]{1,0:T(8,128)(2,1)}, u32[]{:S(2)}) copy-start(bf16[464,1152]{1,0:T(8,128)(2,1)} %get-tuple-element.482.near3) | copy-start | bytes 3207172 | tf_op jit(solution)/shard_map/while
  164.5 2.4 %copy-start.2 = (bf16[448,1152]{1,0:T(8,128)(2,1)S(1)}, bf16[448,1152]{1,0:T(8,128)(2,1)}, u32[]{:S(2)}) copy-start(bf16[448,1152]{1,0:T(8,128)(2,1)} %get-tuple-element.543) | copy-start | bytes 3096580 | tf_op jit(solution)/shard_map/while
  166.9 27.2 %collective-permute-start.5 = (s32[1,448]{1,0:T(1,128)S(1)}, s32[1,448]{1,0:T(1,128)S(1)}, u32[]{:S(2)}, u32[]{:S(2)}) collective-permute-start(s32[1,448]{1,0:T(1,128)S(1)} %bitcast.9), channel_id=1, source_target_pairs={{0,256},{4,260},{8,264},{12,268},{16,272},{20,276},{24,280},{28,28... | collective-permute-start | bytes 5384 | tf_op jit(solution)/shard_map/ppermute | solution.py:19
  179.4 14.7 %copy-start = (f32[448,1152]{1,0:T(8,128)S(1)}, f32[448,1152]{1,0:T(8,128)}, u32[]{:S(2)}) copy-start(f32[448,1152]{1,0:T(8,128)} %get-tuple-element.293.txt_in) | copy-start | bytes 6193156
  179.4 14.7 %copy-start.4 = (bf16[448,1152]{1,0:T(8,128)(2,1)S(1)}, bf16[448,1152]{1,0:T(8,128)(2,1)}, u32[]{:S(2)}) copy-start(bf16[448,1152]{1,0:T(8,128)(2,1)} %get-tuple-element.530) | copy-start | bytes 3096580
